TPU v7x, 256 devices: a whole 4x4x8 slice. The times are simulated.
256 devices in a mesh: dp: 32 (over z_hi, y, core), block: 8 (over x, z_lo).
Axes of the slice: x: 4, y: 4, z: 8 (z_hi: 4, z_lo: 2; z = z_hi * 2 + z_lo), core: 2. Of those that a mesh axis runs over, the one named last changes fastest.
Arguments:
- inputs: bfloat16 [8192, 8192], P('block', 'dp'), may hold values from -6 to 6
- grad_out: bfloat16 [8192, 8192], P('block', 'dp'), may hold values from -6 to 6
- up_left: bfloat16 [64, 128, 512], P('block'), may hold values from -0.5 to 0.5
- up_right: bfloat16 [64, 512, 512], P('block'), may hold values from -0.25 to 0.25
- down_left: bfloat16 [64, 512, 512], P('block'), may hold values from -0.25 to 0.25
- down_right: bfloat16 [64, 512, 128], P('block'), may hold values from -0.25 to 0.25
Outputs:
- grad_in: bfloat16 [8192, 8192], P('block', 'dp')
- grad_up_left: float32 [64, 128, 512], P('block', 'dp')
- grad_up_right: float32 [64, 512, 512], P('block', 'dp')
- grad_down_left: float32 [64, 512, 512], P('block', 'dp')
- grad_down_right: float32 [64, 512, 128], P('block', 'dp')
All inputs are finite; a program needn't handle non-finite values.
Results may differ from a plain program's by a relative error of at most 0.0068.
Values may be sent and summed in bfloat16 or wider, within the bound.
No kernel may reach another device: no remote copies, remote signals or barrier semaphores. Data moves between devices by JAX's collectives and lax.ppermute only.
A program may use at most 128 MiB of HBM per device.

v0:
```python
import jax
import jax.numpy as jnp
from jax import lax
from jax.sharding import PartitionSpec as P

BLOCKS = 64
BLK_IN = 128
BLK_HID = 512
SPREAD = 8


root_two_pi = 0.7978845608028654


def gelu_parts(pre):
    inner = root_two_pi * (pre + 0.044715 * pre * pre * pre)
    curve = jnp.tanh(inner)
    value = 0.5 * pre * (1.0 + curve)
    slope = 0.5 * (1.0 + curve) + 0.5 * pre * (1.0 - curve * curve) * root_two_pi * (
        1.0 + 3.0 * 0.044715 * pre * pre
    )
    return (value, slope)


def product(form, left, right):
    return jnp.einsum(form, left, right, preferred_element_type=jnp.float32)


def shards(inputs, grad_out, up_left, up_right, down_left, down_right):
    single = jnp.float32
    half = jnp.bfloat16
    local = up_left.shape[0]
    tokens = inputs.shape[1]
    factor = float(tokens * lax.axis_size("dp")) ** (-0.5)
    feats = inputs.reshape(local, BLK_IN, tokens)
    upstream = grad_out.reshape(local, BLK_IN, tokens)
    mixed = product("bij,bit->bjt", up_left, feats).astype(half)
    spread_in = lax.all_to_all(mixed, "block", split_axis=1, concat_axis=0, tiled=True).reshape(
        BLOCKS, local, SPREAD, tokens
    )
    pre = product("bckt,cbkm->cmt", spread_in, up_right.reshape(local, BLOCKS, SPREAD, BLK_HID))
    value, slope = gelu_parts(pre)
    hidden = value.astype(half)
    lowered = product("cmj,cmt->cjt", down_left, hidden).astype(half)
    spread_down = lax.all_to_all(lowered, "block", split_axis=1, concat_axis=0, tiled=True).reshape(
        BLOCKS, local, SPREAD, tokens
    )
    grad_right_down = factor * product("cdkt,dot->dcko", spread_down, upstream).reshape(
        local, BLK_HID, BLK_IN
    )
    back_down = product("djo,dot->djt", down_right, upstream).astype(half)
    returned = lax.all_to_all(back_down, "block", split_axis=1, concat_axis=0, tiled=True).reshape(
        BLOCKS, local, SPREAD, tokens
    )
    grad_left_down = factor * product("cmt,dckt->cmdk", hidden, returned).reshape(
        local, BLK_HID, BLK_HID
    )
    back_hidden = product(
        "cmdk,dckt->cmt", down_left.reshape(local, BLK_HID, BLOCKS, SPREAD), returned
    )
    back_pre = (back_hidden * slope).astype(half)
    grad_right_up = factor * product("bckt,cmt->cbkm", spread_in, back_pre).reshape(
        local, BLK_HID, BLK_HID
    )
    back_mid = product("cjm,cmt->cjt", up_right, back_pre).astype(half)
    arrived = lax.all_to_all(back_mid, "block", split_axis=1, concat_axis=0, tiled=True).reshape(
        BLOCKS, local, SPREAD, tokens
    )
    grad_left_up = factor * product("bit,cbkt->bick", feats, arrived).reshape(
        local, BLK_IN, BLK_HID
    )
    grad_block = product("bick,cbkt->bit", up_left.reshape(local, BLK_IN, BLOCKS, SPREAD), arrived)
    grad_in = grad_block.astype(half).reshape(local * BLK_IN, tokens)
    grad_left_up, grad_right_up, grad_left_down, grad_right_down = (
        lax.psum_scatter(grad_left_up, "dp", scatter_dimension=1, tiled=True),
        lax.psum_scatter(grad_right_up, "dp", scatter_dimension=1, tiled=True),
        lax.psum_scatter(grad_left_down, "dp", scatter_dimension=1, tiled=True),
        lax.psum_scatter(grad_right_down, "dp", scatter_dimension=1, tiled=True),
    )
    return (grad_in, grad_left_up, grad_right_up, grad_left_down, grad_right_down)


def solution(mesh):
    in_specs = (
        P("block", "dp"),
        P("block", "dp"),
        P("block", None, None),
        P("block", None, None),
        P("block", None, None),
        P("block", None, None),
    )
    out_specs = (
        P("block", "dp"),
        P("block", "dp", None),
        P("block", "dp", None),
        P("block", "dp", None),
        P("block", "dp", None),
    )
    return jax.shard_map(shards, mesh=mesh, in_specs=in_specs, out_specs=out_specs, check_vma=False)
```

profile of v0, /device:TPU:2, one launch (start us, length us, event | category | flops | bytes accessed | tf_op | source)
XLA Modules:
  0.0 571.8 jit_solution(13542776211281947337)
XLA Ops:
  7.2 0.0 copy-start
  7.2 2.2 convolution_convert_fusion
  9.4 2.5 copy.48
  11.9 6.2 %all-to-all-start.1 = ((bf16[8,512,256]{2,0,1:T(8,128)(2,1)}), bf16[8,512,256]{2,0,1:T(8,128)(2,1)S(1)}, u32[]{:S(2)}, u32[]{:S(2)}) async-start(bf16[8,512,256]{2,0,1:T(8,128)(2,1)} %copy.48), calls=%async_computation.1 | async-start | bytes 4194304 | tf_op jit(solution)/shard_map/all_to_all | solution.py:38
  18.1 1.7 convolution_convert_fusion.1
  19.8 2.5 copy.43
  22.4 20.9 %all-to-all-done.1 = bf16[8,512,256]{2,0,1:T(8,128)(2,1)S(1)} async-done(((bf16[8,512,256]{2,0,1:T(8,128)(2,1)}), bf16[8,512,256]{2,0,1:T(8,128)(2,1)S(1)}, u32[]{:S(2)}, u32[]{:S(2)}) %all-to-all-start.1) | async-done | bytes 2097184 | tf_op jit(solution)/shard_map/all_to_all | solution.py:38
  43.3 6.0 %all-to-all-start = ((bf16[8,512,256]{2,0,1:T(8,128)(2,1)}), bf16[8,512,256]{2,0,1:T(8,128)(2,1)}, u32[]{:S(2)}, u32[]{:S(2)}) async-start(bf16[8,512,256]{2,0,1:T(8,128)(2,1)} %copy.43), calls=%async_computation | async-start | bytes 4194304 | tf_op jit(solution)/shard_map/all_to_all | solution.py:52
  49.3 6.5 %copy.45 = bf16[8,512,512]{1,2,0:T(8,128)(2,1)} copy(bf16[8,512,512]{2,1,0:T(8,128)(2,1)} %param.10) | data formatting | bytes 8388608 | tf_op args[4]
  55.8 1.6 copy.49
  57.4 16.0 %all-to-all-done = bf16[8,512,256]{2,0,1:T(8,128)(2,1)} async-done(((bf16[8,512,256]{2,0,1:T(8,128)(2,1)}), bf16[8,512,256]{2,0,1:T(8,128)(2,1)}, u32[]{:S(2)}, u32[]{:S(2)}) %all-to-all-start) | async-done | bytes 2097184 | tf_op jit(solution)/shard_map/all_to_all | solution.py:52
  73.4 1.9 copy.44
  75.3 4.8 fusion.7
  80.1 0.0 copy-start.4
  80.1 4.7 fusion.6
  84.8 1.3 copy-done.3
  86.1 2.7 convert_bitcast_fusion.1
  88.8 3.3 copy.51
  92.1 0.0 copy-start.6
  92.1 30.3 %all_to_all.60 = bf16[8,512,256]{2,0,1:T(8,128)(2,1)S(1)} all-to-all(bf16[8,512,256]{2,0,1:T(8,128)(2,1)S(1)} %copy.51), channel_id=1, replica_groups=mesh['dp'=32,'block'=8] {'block'}, dimensions={1} | all-to-all | bytes 4194304 | tf_op jit(solution)/shard_map/all_to_all | solution.py:66
  122.4 0.3 copy.53
  122.7 2.7 multiply_bitcast_fusion.2
  125.4 3.1 copy.57
  128.5 0.0 reduce-scatter.5.cloned.1.call-update
  128.6 0.0 reduce-scatter.9.cloned.1.call-start
  128.6 4.9 broadcast_multiply_fusion
  133.5 8.0 %copy.102 = f32[8,512,64,8]{1,3,2,0:T(8,128)} copy(f32[8,512,64,8]{1,2,3,0:T(8,128)S(1)} %broadcast_multiply_fusion) | data formatting | bytes 16777216 | tf_op jit(solution)/shard_map/mul | solution.py:55
  141.5 10.5 %copy.62 = f32[8,512,512]{2,0,1:T(8,128)} copy(f32[8,512,512]{1,2,0:T(8,128)} %bitcast.99) | data formatting | bytes 16777216 | tf_op jit(solution)/shard_map/mul | solution.py:55
  152.0 0.0 reduce-scatter.9.cloned.1.call-update
  152.0 0.0 reduce-scatter.11.cloned.1.call-start
  152.1 6.5 %convert_bitcast_fusion = bf16[8,512,256]{1,2,0:T(8,128)(2,1)} fusion(bf16[8,512,512]{2,1,0:T(8,128)(2,1)} %param.10, f32[8,256,512,1]{2,1,3,0:T(8,128)} %copy-done.9), kind=kOutput, calls=%fused_computation.26 | convolution fusion | flops 1084227584 | bytes 10485760 | tf_op jit(solution)/shard_map/cmj,cmt->cjt/dot_general | solution.py:26
  158.6 4.5 copy.63
  163.1 38.1 %all_to_all.61 = bf16[8,512,256]{2,0,1:T(8,128)(2,1)S(1)} all-to-all(bf16[8,512,256]{2,0,1:T(8,128)(2,1)} %copy.63), channel_id=1, replica_groups=mesh['dp'=32,'block'=8] {'block'}, dimensions={1} | all-to-all | bytes 4194304 | tf_op jit(solution)/shard_map/all_to_all | solution.py:45
  201.2 0.5 copy.65
  201.8 2.1 multiply_bitcast_fusion.1
  203.8 0.0 reduce-scatter.11.cloned.1.call-update
  203.8 0.0 reduce-scatter.7.cloned.1.call-start
  203.9 7.4 %multiply_bitcast_fusion = f32[8,512,512]{2,1,0:T(8,128)} fusion(bf16[8,512,256]{1,2,0:T(8,128)(2,1)} %copy-done.3, bf16[64,8,8,256]{3,0,2,1:T(8,128)(2,1)} %bitcast.106), kind=kOutput, calls=%fused_computation.1 | convolution fusion | flops 1075838976 | bytes 12582912 | tf_op jit(solution)/shard_map/bckt,cmt->cbkm/dot_general | solution.py:26
  211.3 0.0 reduce-scatter.7.cloned.1.call-update
  211.3 0.0 copy-start.1
  211.3 2.4 copy.54
  213.7 2.5 fusion.24
  216.2 8.1 %reduce-scatter.5.cloned.1.call-done = f32[8,4,512]{2,0,1:T(8,128)} async-done(((f32[8,128,512]{2,0,1:T(8,128)}), f32[8,4,512]{2,0,1:T(8,128)}) %reduce-scatter.5.cloned.1.call-update) | async-done | bytes 65552 | tf_op jit(solution)/shard_map/reduce_scatter | solution.py:75
  224.3 1.5 copy.67
  225.8 121.3 %reduce-scatter.9.cloned.1.call-done = f32[8,16,512]{2,0,1:T(8,128)} async-done(((f32[8,512,512]{2,0,1:T(8,128)}), f32[8,16,512]{2,0,1:T(8,128)}) %reduce-scatter.9.cloned.1.call-update) | async-done | bytes 262160 | tf_op jit(solution)/shard_map/reduce_scatter | solution.py:77
  347.1 1.8 copy.68
  348.9 92.1 %reduce-scatter.11.cloned.1.call-done = f32[8,16,128]{2,1,0:T(8,128)} async-done(((f32[8,512,128]{2,1,0:T(8,128)}), f32[8,16,128]{2,1,0:T(8,128)}) %reduce-scatter.11.cloned.1.call-update) | async-done | bytes 65552 | tf_op jit(solution)/shard_map/reduce_scatter | solution.py:78
  441.0 124.2 %reduce-scatter.7.cloned.1.call-done = f32[8,16,512]{2,1,0:T(8,128)} async-done(((f32[8,512,512]{2,1,0:T(8,128)}), f32[8,16,512]{2,1,0:T(8,128)}) %reduce-scatter.7.cloned.1.call-update) | async-done | bytes 262160 | tf_op jit(solution)/shard_map/reduce_scatter | solution.py:76
  (16 shorter events, 0.0 us)
Async XLA Ops:
  7.2 10.9 %copy-start = (bf16[8,512,128]{2,1,0:T(8,128)(2,1)S(1)}, bf16[8,512,128]{2,1,0:T(8,128)(2,1)}, u32[]{:S(2)}) copy-start(bf16[8,512,128]{2,1,0:T(8,128)(2,1)} %param.11) | copy-start | bytes 3145732
  11.9 31.4 %all-to-all-start.1 = ((bf16[8,512,256]{2,0,1:T(8,128)(2,1)}), bf16[8,512,256]{2,0,1:T(8,128)(2,1)S(1)}, u32[]{:S(2)}, u32[]{:S(2)}) async-start(bf16[8,512,256]{2,0,1:T(8,128)(2,1)} %copy.48), calls=%async_computation.1 | async-start | bytes 4194304 | tf_op jit(solution)/shard_map/all_to_all | solution.py:38
  43.3 30.1 %all-to-all-start = ((bf16[8,512,256]{2,0,1:T(8,128)(2,1)}), bf16[8,512,256]{2,0,1:T(8,128)(2,1)}, u32[]{:S(2)}, u32[]{:S(2)}) async-start(bf16[8,512,256]{2,0,1:T(8,128)(2,1)} %copy.43), calls=%async_computation | async-start | bytes 4194304 | tf_op jit(solution)/shard_map/all_to_all | solution.py:52
  49.3 175.0 %reduce-scatter.5.cloned.1.call-start = ((), (), s32[]{:S(2)}) async-start(), calls=%async_computation.8 | async-start | bytes 2162688 | tf_op jit(solution)/shard_map/reduce_scatter | solution.py:75
  57.4 17.9 %copy-start.2 = (bf16[8,8,64,256]{3,0,1,2:T(8,128)(2,1)S(1)}, bf16[8,8,64,256]{3,0,1,2:T(8,128)(2,1)}, u32[]{:S(2)}) copy-start(bf16[8,8,64,256]{3,0,1,2:T(8,128)(2,1)} %copy.49) | copy-start | bytes 6291460
  75.2 4.8 copy-start.8
  75.3 4.8 copy-start.5
  80.0 4.7 copy-start.9
  80.1 6.0 %copy-start.4 = (bf16[8,512,512]{2,1,0:T(8,128)(2,1)S(1)}, bf16[8,512,512]{2,1,0:T(8,128)(2,1)}, u32[]{:S(2)}) copy-start(bf16[8,512,512]{2,1,0:T(8,128)(2,1)} %param.9) | copy-start | bytes 12582916
  84.8 1.3 copy-start.3
  92.1 30.6 %copy-start.6 = (bf16[1024,256]{1,0:T(8,128)(2,1)S(1)}, bf16[1024,256]{1,0:T(8,128)(2,1)}, u32[]{:S(2)}) copy-start(bf16[1024,256]{1,0:T(8,128)(2,1)} %param.6) | copy-start | bytes 1572868
  128.6 218.6 %reduce-scatter.9.cloned.1.call-start = ((), (), s32[]{:S(2)}) async-start(), calls=%async_computation.10 | async-start | bytes 8650752 | tf_op jit(solution)/shard_map/reduce_scatter | solution.py:77
  152.0 289.0 %reduce-scatter.11.cloned.1.call-start = ((), (), s32[]{:S(2)}) async-start(), calls=%async_computation.11 | async-start | bytes 2162688 | tf_op jit(solution)/shard_map/reduce_scatter | solution.py:78
  163.1 38.6 %copy-start.7 = (bf16[1024,256]{1,0:T(8,128)(2,1)S(1)}, bf16[1024,256]{1,0:T(8,128)(2,1)}, u32[]{:S(2)}) copy-start(bf16[1024,256]{1,0:T(8,128)(2,1)} %param.7) | copy-start | bytes 1572868
  203.8 361.4 %reduce-scatter.7.cloned.1.call-start = ((), (), s32[]{:S(2)}) async-start(), calls=%async_computation.9 | async-start | bytes 8650752 | tf_op jit(solution)/shard_map/reduce_scatter | solution.py:76
  211.3 353.9 %copy-start.1 = (bf16[8,512,128]{2,1,0:T(8,128)(2,1)S(1)}, bf16[8,512,128]{2,1,0:T(8,128)(2,1)}, u32[]{:S(2)}) copy-start(bf16[8,512,128]{2,1,0:T(8,128)(2,1)} %param.11) | copy-start | bytes 3145732
Sparse Core Ops, SparseCore 0:
  128.7 95.5 reduce-scatter.4
  228.3 118.7 reduce-scatter.8
  352.0 88.9 reduce-scatter.10
  446.0 119.1 reduce-scatter.6
where the time goes:
time: 573 us; the launch traced here: 572 us
  waiting for transfers between devices  383 us (67%)
  blocking collectives  68.4 us (12%)
  local copies, waits for them, and re-layouts  52.3 us (9%)
  matrix products  42.1 us (7%)
  between operations  13.9 us (2%)
  starting transfers between devices  12.3 us (2%)
    reduce_scatter x1, waiting for transfers between devices, shards(): lax.psum_scatter(grad_right_up, 'dp', scatter_dimension=1, tiled=True)  124 us
    reduce_scatter x1, waiting for transfers between devices, shards(): lax.psum_scatter(grad_left_down, 'dp', scatter_dimension=1, tiled=True)  121 us
    reduce_scatter x1, waiting for transfers between devices, shards(): lax.psum_scatter(grad_right_down, 'dp', scatter_dimension=1, tiled=True)  92.1 us
    dot_general x11, matrix products, product(): return jnp.einsum(form, left, right, preferred_element_type=jnp.float32)  42.1 us
    all_to_all x1, blocking collectives, shards(): lax.all_to_all(lowered, 'block', split_axis=1, concat_axis=0, tiled=True)  38.1 us
    all_to_all x1, blocking collectives, shards(): lax.all_to_all(back_mid, 'block', split_axis=1, concat_axis=0, tiled=True)  30.3 us
    all_to_all x1, waiting for transfers between devices, shards(): lax.all_to_all(mixed, 'block', split_axis=1, concat_axis=0, tiled=True)  20.9 us
    mul x2, local copies, waits for them, and re-layouts, shards(): factor * product('cmt,dckt->cmdk', hidden, returned).reshape(local, BLK_H...  18.5 us
  transfers between devices with their start and end apart: 6, of which 6 were waited for; matrix products, arithmetic and copies ran while one was open for 11% of the time, Pallas kernels for 0%

commit v1 on v0

v1 whole, which is shorter than its diff:
```python
import jax
import jax.numpy as jnp
from jax import lax
from jax.experimental import pallas as pl
from jax.experimental.pallas import tpu as pltpu
from jax.sharding import PartitionSpec as P

BLK_IN = 128
BLK_HID = 512
SPREAD = 8
LOCAL = 8
PEERS = 8
PAIR = 2 * SPREAD
ROWS = 16
HALF = LOCAL // 2

half = jnp.bfloat16
single = jnp.float32
root_two_pi = 0.7978845608028654

Z, Y, CORES = 4, 4, 2


def dp_perm(dz, dy, dc):
    pairs = []
    for z in range(Z):
        for y in range(Y):
            for c in range(CORES):
                source = (z * Y + y) * CORES + c
                target = ((z + dz) % Z * Y + (y + dy) % Y) * CORES + (c + dc) % CORES
                pairs.append((source, target))
    return pairs


def gelu_parts(pre):
    inner = root_two_pi * (pre + 0.044715 * pre * pre * pre)
    curve = jnp.tanh(inner)
    value = 0.5 * pre * (1.0 + curve)
    slope = 0.5 * (1.0 + curve) + 0.5 * pre * (1.0 - curve * curve) * root_two_pi * (
        1.0 + 3.0 * 0.044715 * pre * pre
    )
    return value, slope


def dot(left, right, over_left, over_right):
    return lax.dot_general(
        left, right, (((over_left,), (over_right,)), ((), ())), preferred_element_type=single
    )


def spread_pair(first, second):
    tokens = first.shape[-1]
    parts = [r.reshape(BLK_HID // SPREAD, SPREAD, tokens) for r in (first, second)]
    return jnp.concatenate(parts, axis=1).astype(half)


def call(kernel, grid, in_specs, out_specs, out_shape, scratch=(), flops=0, moved=0):
    return pl.pallas_call(
        kernel,
        grid_spec=pltpu.PrefetchScalarGridSpec(
            num_scalar_prefetch=1,
            grid=grid,
            in_specs=in_specs,
            out_specs=out_specs,
            scratch_shapes=list(scratch),
        ),
        out_shape=out_shape,
        compiler_params=pltpu.CompilerParams(vmem_limit_bytes=48 * 1024 * 1024),
        cost_estimate=pl.CostEstimate(flops=flops, bytes_accessed=moved, transcendentals=0),
    )


def first_kernel(me, x_ref, g_ref, up_ref, down_ref, one_ref, two_ref):
    ups, downs = [], []
    for i in range(2):
        rows = slice(i * BLK_IN, (i + 1) * BLK_IN)
        ups.append(dot(up_ref[i], x_ref[rows], 0, 0))
        downs.append(dot(down_ref[i], g_ref[rows], 1, 0))
    for slot, pair in enumerate((ups, downs)):
        spread = spread_pair(*pair).reshape(PEERS, 2, HALF, PAIR, -1)
        one_ref[:, slot] = spread[:, 0]
        two_ref[:, slot] = spread[:, 1]


def first_stage(me, inputs, grad_out, up_left, down_right):
    tokens = inputs.shape[1]
    shape = jax.ShapeDtypeStruct((PEERS, 2, HALF, LOCAL * SPREAD, tokens), half)
    out = pl.BlockSpec((PEERS, 2, HALF, PAIR, tokens), lambda p, me: (0, 0, 0, p, 0))
    return call(
        first_kernel,
        (LOCAL // 2,),
        [
            pl.BlockSpec((2 * BLK_IN, tokens), lambda p, me: (p, 0)),
            pl.BlockSpec((2 * BLK_IN, tokens), lambda p, me: (p, 0)),
            pl.BlockSpec((2, BLK_IN, BLK_HID), lambda p, me: (p, 0, 0)),
            pl.BlockSpec((2, BLK_HID, BLK_IN), lambda p, me: (p, 0, 0)),
        ],
        [out, out],
        [shape, shape],
        flops=4 * LOCAL * BLK_IN * BLK_HID * tokens,
        moved=7 << 20,
    )(me, inputs, grad_out, up_left, down_right)


def place(me, held, own_ref, other_ref, index):
    for ry in range(Y):
        for rz in range(Z):
            group = ((me[2] + rz) % Z * Y + (me[1] + ry) % Y) * CORES
            own_ref[(ry, rz) + index] = held[group + me[0]]
            other_ref[(ry, rz) + index] = held[group + 1 - me[0]]


def middle_kernel(me, got_ref, up_ref, down_ref, back_ref, own_ref, other_ref, held):
    lows, mids = [], []
    for i in range(2):
        v = got_ref[:, 0, i].reshape(BLK_HID, -1)
        f = got_ref[:, 1, i].reshape(BLK_HID, -1)
        up, down = up_ref[i], down_ref[i]
        value, slope = gelu_parts(dot(up, v, 0, 0))
        hidden = value.astype(half)
        lows.append(dot(down, hidden, 0, 0))
        held[0] = dot(hidden, f, 1, 1).astype(half).reshape(-1, ROWS, BLK_HID)
        place(me, held.at[0], own_ref, other_ref, (0, i))
        back = (dot(down, f, 1, 0) * slope).astype(half)
        mids.append(dot(up, back, 1, 0))
        held[1] = dot(v, back, 1, 1).astype(half).reshape(-1, ROWS, BLK_HID)
        place(me, held.at[1], own_ref, other_ref, (1, i))
    back_ref[:, 0] = spread_pair(*lows).reshape(PEERS, LOCAL, PAIR, -1)
    back_ref[:, 1] = spread_pair(*mids).reshape(PEERS, LOCAL, PAIR, -1)


def middle_stage(me, chunk, got, up_right, down_left):
    tokens = got.shape[-1]
    pairs = HALF // 2
    grads = jax.ShapeDtypeStruct((Y, Z, 2, HALF, ROWS, BLK_HID), half)
    grads_spec = pl.BlockSpec(
        (Y, Z, 2, 2, ROWS, BLK_HID), lambda p, me: (0, 0, 0, p, 0, 0)
    )
    weight = pl.BlockSpec((2, BLK_HID, BLK_HID), lambda p, me: (chunk * pairs + p, 0, 0))
    return call(
        middle_kernel,
        (pairs,),
        [
            pl.BlockSpec((PEERS, 2, 2, LOCAL * SPREAD, tokens), lambda p, me: (0, 0, p, 0, 0)),
            weight,
            weight,
        ],
        [
            pl.BlockSpec((PEERS, 2, LOCAL, PAIR, tokens), lambda p, me: (0, 0, 0, p, 0)),
            grads_spec,
            grads_spec,
        ],
        [
            jax.ShapeDtypeStruct((PEERS, 2, LOCAL, HALF * SPREAD, tokens), half),
            grads,
            grads,
        ],
        scratch=[pltpu.VMEM((2, BLK_HID // ROWS, ROWS, BLK_HID), half)],
        flops=12 * HALF * BLK_HID * BLK_HID * tokens,
        moved=16 << 20,
    )(me, got, up_right, down_left)


def last_kernel(me, one_ref, two_ref, x_ref, g_ref, up_ref, in_ref, own_ref, other_ref, held, held_down):
    tokens = x_ref.shape[-1]
    rows4 = BLK_IN // (Z * Y * CORES)
    evens, odds = [], []
    for i in range(4):
        rows = slice(i * BLK_IN, (i + 1) * BLK_IN)
        a2, du = [
            jnp.concatenate([one_ref[:, slot, i], two_ref[:, slot, i]], axis=1).reshape(
                BLK_HID, tokens
            )
            for slot in range(2)
        ]
        in_ref[rows] = dot(up_ref[i], du, 1, 0).astype(half)
        left = dot(x_ref[rows], du, 1, 1).reshape(-1, 2 * rows4, BLK_HID)
        evens.append(left[:, :rows4])
        odds.append(left[:, rows4:])
        right = dot(a2, g_ref[rows], 1, 1).astype(half)
        held_down[:, :, i * BLK_IN : (i + 1) * BLK_IN] = right.reshape(-1, ROWS, BLK_IN)
    for core, parts in enumerate((evens, odds)):
        held[core] = jnp.concatenate(parts, axis=1).astype(half)
    for ry in range(Y):
        for rz in range(Z):
            chip = (me[2] + rz) % Z * Y + (me[1] + ry) % Y
            own_ref[ry, rz, 0, 0] = held[me[0], chip]
            other_ref[ry, rz, 0, 0] = held[1 - me[0], chip]
            own_ref[ry, rz, 1, 0] = held_down[chip * CORES + me[0]]
            other_ref[ry, rz, 1, 0] = held_down[chip * CORES + 1 - me[0]]


def last_stage(me, one, two, inputs, grad_out, up_left):
    tokens = inputs.shape[1]
    groups = LOCAL // 4
    grads = jax.ShapeDtypeStruct((Y, Z, 2, groups, ROWS, BLK_HID), half)
    grads_spec = pl.BlockSpec((Y, Z, 2, 1, ROWS, BLK_HID), lambda p, me: (0, 0, 0, p, 0, 0))
    got = pl.BlockSpec((PEERS, 2, 4, HALF * SPREAD, tokens), lambda p, me: (0, 0, p, 0, 0))
    feats = pl.BlockSpec((4 * BLK_IN, tokens), lambda p, me: (p, 0))
    return call(
        last_kernel,
        (groups,),
        [got, got, feats, feats, pl.BlockSpec((4, BLK_IN, BLK_HID), lambda p, me: (p, 0, 0))],
        [feats, grads_spec, grads_spec],
        [jax.ShapeDtypeStruct(inputs.shape, half), grads, grads],
        scratch=[
            pltpu.VMEM((CORES, Z * Y, ROWS, BLK_HID), half),
            pltpu.VMEM((Z * Y * CORES, ROWS, BLK_HID), half),
        ],
        flops=6 * LOCAL * BLK_IN * BLK_HID * tokens,
        moved=12 << 20,
    )(me, one, two, inputs, grad_out, up_left)


def core_kernel(me, own_ref, got_ref, keep_ref, *send_refs):
    keep_ref[...] = own_ref[0].astype(single) + got_ref[0].astype(single)
    for r, send in enumerate(send_refs):
        send[...] = (own_ref[r + 1].astype(single) + got_ref[r + 1].astype(single)).astype(half)


def core_sum(me, own, got):
    n = own.shape[2]
    whole = pl.BlockSpec((Y, 1, n, ROWS, BLK_HID), lambda p, me: (0, p, 0, 0, 0))
    part = pl.BlockSpec((1, n, ROWS, BLK_HID), lambda p, me: (p, 0, 0, 0))
    shape = (Z, n, ROWS, BLK_HID)
    return call(
        core_kernel,
        (Z,),
        [whole, whole],
        [part] * Y,
        [jax.ShapeDtypeStruct(shape, single)] + [jax.ShapeDtypeStruct(shape, half)] * (Y - 1),
        flops=own.size,
        moved=own.size * 6,
    )(me, own, got)


def line_kernel(me, keep_ref, a_ref, b_ref, c_ref, rest_ref, *send_refs):
    for r in range(Z):
        total = keep_ref[r] + a_ref[r].astype(single)
        total = total + (b_ref[r].astype(single) + c_ref[r].astype(single))
        if r == 0:
            rest_ref[...] = total
        else:
            send_refs[r - 1][...] = total.astype(half)


def line_sum(me, keep, got):
    n = keep.shape[1]
    steps = 2
    whole = pl.BlockSpec((Z, n // steps, ROWS, BLK_HID), lambda p, me: (0, p, 0, 0))
    part = pl.BlockSpec((n // steps, ROWS, BLK_HID), lambda p, me: (p, 0, 0))
    shape = (n, ROWS, BLK_HID)
    return call(
        line_kernel,
        (steps,),
        [whole] * Y,
        [part] * Z,
        [jax.ShapeDtypeStruct(shape, single)] + [jax.ShapeDtypeStruct(shape, half)] * (Z - 1),
        flops=keep.size * 3,
        moved=keep.size * 12,
    )(me, keep, *got)


def end_kernel(factor, me, keep_ref, a_ref, b_ref, c_ref, out_ref):
    total = keep_ref[...] + a_ref[...].astype(single)
    out_ref[...] = factor * (total + (b_ref[...].astype(single) + c_ref[...].astype(single)))


def end_sum(me, factor, keep, got):
    def kernel(*refs):
        end_kernel(factor, *refs)

    whole = pl.BlockSpec(keep.shape, lambda p, me: (0, 0, 0))
    return call(
        kernel,
        (1,),
        [whole] * Z,
        whole,
        jax.ShapeDtypeStruct(keep.shape, single),
        flops=keep.size * 3,
        moved=keep.size * 14,
    )(me, keep, *got)


def reduce_rows(me, factor, own, other):
    shape = own.shape[2:]
    flat = (Y, Z, -1, ROWS, BLK_HID)
    got = lax.ppermute(other.reshape(flat), "dp", dp_perm(0, 0, 1))
    keep, *sends = core_sum(me, own.reshape(flat), got)
    got = [lax.ppermute(s, "dp", dp_perm(0, r + 1, 0)) for r, s in enumerate(sends)]
    keep, *sends = line_sum(me, keep, got)
    got = [lax.ppermute(s, "dp", dp_perm(r + 1, 0, 0)) for r, s in enumerate(sends)]
    return end_sum(me, factor, keep, got).reshape(shape)


def exchange(array):
    return lax.all_to_all(array, "block", split_axis=0, concat_axis=0, tiled=True)


def shards(inputs, grad_out, up_left, up_right, down_left, down_right):
    tokens = inputs.shape[1]
    factor = float(tokens * lax.axis_size("dp")) ** (-0.5)
    dp = lax.axis_index("dp")
    me = jnp.stack([dp % CORES, dp // CORES % Y, dp // (CORES * Y)]).astype(jnp.int32)

    one, two = first_stage(me, inputs, grad_out, up_left, down_right)
    backs, grads = [], []
    for chunk, sent in enumerate((one, two)):
        back, own, other = middle_stage(me, chunk, exchange(sent), up_right, down_left)
        backs.append(exchange(back))
        grads.append(reduce_rows(me, factor, own, other))
    grad_in, own, other = last_stage(me, *backs, inputs, grad_out, up_left)
    outer = reduce_rows(me, factor, own, other)

    grad_left_down, grad_right_up = [
        jnp.concatenate([g[k] for g in grads], axis=0) for k in range(2)
    ]
    rows4 = BLK_IN // (Z * Y * CORES)
    grad_left_up = outer[0].reshape(LOCAL, rows4, BLK_HID)
    grad_right_down = (
        outer[1].reshape(LOCAL // 4, ROWS, 4, BLK_IN).transpose(0, 2, 1, 3).reshape(LOCAL, ROWS, BLK_IN)
    )
    return grad_in, grad_left_up, grad_right_up, grad_left_down, grad_right_down


def solution(mesh):
    in_specs = (
        P("block", "dp"),
        P("block", "dp"),
        P("block", None, None),
        P("block", None, None),
        P("block", None, None),
        P("block", None, None),
    )
    out_specs = (
        P("block", "dp"),
        P("block", "dp", None),
        P("block", "dp", None),
        P("block", "dp", None),
        P("block", "dp", None),
    )
    return jax.shard_map(shards, mesh=mesh, in_specs=in_specs, out_specs=out_specs, check_vma=False)
```

time: 573 us -> 223 us (0.39)
  waiting for transfers between devices: 383 us -> 59.8 us
  starting transfers between devices: 12.3 us -> 70.4 us
  matrix products: 42.1 us -> 0 us
  Pallas kernels: 0 us -> 40.2 us
  blocking collectives: 68.4 us -> 31.5 us
  local copies, waits for them, and re-layouts: 52.3 us -> 16.1 us
  between operations: 13.9 us -> 0.86 us
    reduce_scatter x4 -> x0, waiting for transfers between devices: 346 us -> none  [the longest x1 124 us: shards(): lax.psum_scatter(grad_right_up, 'dp', scatter_dimension=1, tiled=True)]
    ppermute x0 -> x21, starting transfers between devices: none -> 52.4 us  [the longest x9 29.8 us: reduce_rows(): lax.ppermute(s, 'dp', dp_perm(r + 1, 0, 0))]
    dot_general x11 -> x0, matrix products: 42.1 us -> none  [product(): return jnp.einsum(form, left, right, preferred_element_type=jnp.float32)]
    pallas_call x0 -> x13, Pallas kernels: none -> 40.2 us  [the longest x2 17.6 us: middle_stage(): call(middle_kernel, (pairs,), [pl.BlockSpec((PEERS, 2, 2, LOCAL * SPREAD,...]
    all_to_all x2 -> x1, blocking collectives: 68.4 us -> 31.5 us  [exchange(): lax.all_to_all(array, 'block', split_axis=0, concat_axis=0, tiled=True)]
    ppermute x0 -> x21, waiting for transfers between devices: none -> 30.3 us  [the longest x9 19.5 us: reduce_rows(): lax.ppermute(s, 'dp', dp_perm(0, r + 1, 0))]
    mul x3 -> x0, local copies, waits for them, and re-layouts: 21.6 us -> none  [the longest x2 18.5 us: shards(): factor * product('cmt,dckt->cmdk', hidden, returned).reshape(local, BLK_H...]
    convert_element_type x4 -> x0, local copies, waits for them, and re-layouts: 12.9 us -> none  [the longest x1 4.52 us: shards(): lowered = product('cmj,cmt->cjt', down_left, hidden).astype(half)]
  transfers between devices with their start and end apart: 6 -> 24, of which waited for: 6 -> 11; matrix products, arithmetic and copies ran while one was open for 11% -> 0% of each run, Pallas kernels for 0% -> 16%
where the time goes in v1:
time: 223 us; the launch traced here: 220 us
  starting transfers between devices  70.4 us (32%)
  waiting for transfers between devices  59.8 us (27%)
  Pallas kernels  40.2 us (18%)
  blocking collectives  31.5 us (14%)
  local copies, waits for them, and re-layouts  16.1 us (7%)
    all_to_all x1, blocking collectives, exchange(): lax.all_to_all(array, 'block', split_axis=0, concat_axis=0, tiled=True)  31.5 us
    ppermute x9, starting transfers between devices, reduce_rows(): lax.ppermute(s, 'dp', dp_perm(r + 1, 0, 0))  29.8 us
    all_to_all x3, waiting for transfers between devices, exchange(): lax.all_to_all(array, 'block', split_axis=0, concat_axis=0, tiled=True)  29.5 us
    ppermute x9, starting transfers between devices, reduce_rows(): lax.ppermute(s, 'dp', dp_perm(0, r + 1, 0))  22.2 us
    ppermute x9, waiting for transfers between devices, reduce_rows(): lax.ppermute(s, 'dp', dp_perm(0, r + 1, 0))  19.5 us
    all_to_all x3, starting transfers between devices, exchange(): lax.all_to_all(array, 'block', split_axis=0, concat_axis=0, tiled=True)  18 us
    pallas_call x2, Pallas kernels, middle_stage(): call(middle_kernel, (pairs,), [pl.BlockSpec((PEERS, 2, 2, LOCAL * SPREAD,...  17.6 us
    unnamed x32, local copies, waits for them, and re-layouts  15.4 us
  transfers between devices with their start and end apart: 24, of which 11 were waited for; matrix products, arithmetic and copies ran while one was open for 0% of the time, Pallas kernels for 16%

profile of v1, /device:TPU:2, one launch (start us, length us, event | category | flops | bytes accessed | tf_op | source)
XLA Modules:
  0.0 220.4 jit_solution(3298986922943777469)
XLA Ops:
  0.7 1.2 copy-done
  2.0 1.0 copy-done.5
  3.0 1.0 copy-done.7
  4.1 1.2 copy-done.9
  5.3 4.1 %shard_map.101 = (bf16[8,2,4,64,256]{4,3,2,1,0:T(8,128)(2,1)}, bf16[8,2,4,64,256]{4,3,2,1,0:T(8,128)(2,1)}) custom-call(s32[3]{0:T(128)S(1)} %pad_add_fusion.me.refs_0_, bf16[1024,256]{1,0:T(8,128)(2,1)S(1)} %copy-done.5, bf16[1024,256]{1,0:T(8,128)(2,1)S(1)} %copy-done.7, bf16[8,128,512]{2,1,0:T(8,128)(2,1)S(1)} %copy-done, bf16[8,512,128]{2,1,0:T(8,128)(2,1)S(1)} %copy-done.9), custom_call_target="tpu_custom_call" | custom-call | flops 536870912 | bytes 7340032 | tf_op jit(solution)/shard_map/pallas_call | solution.py:89
  9.4 31.5 %all_to_all.20.got_ref = bf16[8,2,4,64,256]{4,3,2,1,0:T(8,128)(2,1)} all-to-all(bf16[8,2,4,64,256]{4,3,2,1,0:T(8,128)(2,1)} %get-tuple-element.42), channel_id=1, replica_groups=mesh['dp'=32,'block'=8] {'block'}, dimensions={0} | all-to-all | bytes 4194304 | tf_op jit(solution)/shard_map/all_to_all | solution.py:297
  40.9 5.3 %all-to-all-start = ((bf16[8,2,4,64,256]{4,3,2,1,0:T(8,128)(2,1)}), bf16[8,2,4,64,256]{4,3,2,1,0:T(8,128)(2,1)S(1)}, u32[]{:S(2)}, u32[]{:S(2)}) async-start(bf16[8,2,4,64,256]{4,3,2,1,0:T(8,128)(2,1)} %get-tuple-element.40), calls=%async_computation | async-start | bytes 4194304 | tf_op jit(solution)/shard_map/all_to_all | solution.py:297
  46.1 8.9 %shard_map.103 = (bf16[8,2,8,32,256]{4,3,2,1,0:T(8,128)(2,1)}, bf16[4,4,2,4,16,512]{5,4,3,2,1,0:T(8,128)(2,1)S(1)}, bf16[4,4,2,4,16,512]{5,4,3,2,1,0:T(8,128)(2,1)}) custom-call(s32[3]{0:T(128)S(1)} %pad_add_fusion.me.refs_0_, bf16[8,2,4,64,256]{4,3,2,1,0:T(8,128)(2,1)} %all_to_all.20.got_ref, bf16[8,512,512]{2,1,0:T(8,128)(2,1)} %up_ref.6, ...), custom_call_target="tpu_custom_call" | custom-call | flops 3221225472 | bytes 16777216 | tf_op jit(solution)/shard_map/pallas_call | solution.py:140
  55.0 1.3 copy-done.2
  56.3 13.5 %all-to-all-done.got_ref = bf16[8,2,4,64,256]{4,3,2,1,0:T(8,128)(2,1)S(1)} async-done(((bf16[8,2,4,64,256]{4,3,2,1,0:T(8,128)(2,1)}), bf16[8,2,4,64,256]{4,3,2,1,0:T(8,128)(2,1)S(1)}, u32[]{:S(2)}, u32[]{:S(2)}) %all-to-all-start) | async-done | bytes 2097184 | tf_op jit(solution)/shard_map/all_to_all | solution.py:297
  69.8 1.4 copy-done.14
  71.2 6.4 %all-to-all-start.3 = ((bf16[8,2,8,32,256]{4,3,2,1,0:T(8,128)(2,1)}), bf16[8,2,8,32,256]{4,3,2,1,0:T(8,128)(2,1)}, u32[]{:S(2)}, u32[]{:S(2)}) async-start(bf16[8,2,8,32,256]{4,3,2,1,0:T(8,128)(2,1)} %get-tuple-element.43), calls=%async_computation.3 | async-start | bytes 4194304 | tf_op jit(solution)/shard_map/all_to_all | solution.py:297
  77.5 8.7 %shard_map.102 = (bf16[8,2,8,32,256]{4,3,2,1,0:T(8,128)(2,1)S(1)}, bf16[4,4,2,4,16,512]{5,4,3,2,1,0:T(8,128)(2,1)S(1)}, bf16[4,4,2,4,16,512]{5,4,3,2,1,0:T(8,128)(2,1)}) custom-call(s32[3]{0:T(128)S(1)} %pad_add_fusion.me.refs_0_, bf16[8,2,4,64,256]{4,3,2,1,0:T(8,128)(2,1)} %copy-done.14, bf16[8,512,512]{2,1,0:T(8,128)(2,1)} %up_ref.6, ...), custom_call_target="tpu_custom_call" | custom-call | flops 3221225472 | bytes 16777216 | tf_op jit(solution)/shard_map/pallas_call | solution.py:140
  86.2 1.3 copy-done.4
  87.6 13.5 %all-to-all-done.3.two_ref = bf16[8,2,8,32,256]{4,3,2,1,0:T(8,128)(2,1)} async-done(((bf16[8,2,8,32,256]{4,3,2,1,0:T(8,128)(2,1)}), bf16[8,2,8,32,256]{4,3,2,1,0:T(8,128)(2,1)}, u32[]{:S(2)}, u32[]{:S(2)}) %all-to-all-start.3) | async-done | bytes 2097184 | tf_op jit(solution)/shard_map/all_to_all | solution.py:297
  101.1 6.3 %all-to-all-start.1 = ((bf16[8,2,8,32,256]{4,3,2,1,0:T(8,128)(2,1)}), bf16[8,2,8,32,256]{4,3,2,1,0:T(8,128)(2,1)}, u32[]{:S(2)}, u32[]{:S(2)}) async-start(bf16[8,2,8,32,256]{4,3,2,1,0:T(8,128)(2,1)} %copy-done.4), calls=%async_computation.1 | async-start | bytes 4194304 | tf_op jit(solution)/shard_map/all_to_all | solution.py:297
  107.9 6.5 %collective-permute-done.14.got_ref = bf16[4,4,8,16,512]{4,3,2,1,0:T(8,128)(2,1)S(1)} collective-permute-done((bf16[4,4,8,16,512]{4,3,2,1,0:T(8,128)(2,1)}, bf16[4,4,8,16,512]{4,3,2,1,0:T(8,128)(2,1)S(1)}, u32[]{:S(2)}, u32[]{:S(2)}) %collective-permute-start.14) | collective-permute-done | bytes 2097184 | tf_op jit(solution)/shard_map/ppermute | solution.py:288
  114.4 1.4 copy-done.15
  115.8 1.6 copy-done.3
  117.4 4.2 %shard_map.111 = (f32[4,8,16,512]{3,2,1,0:T(8,128)S(1)}, bf16[4,8,16,512]{3,2,1,0:T(8,128)(2,1)}, bf16[4,8,16,512]{3,2,1,0:T(8,128)(2,1)}, bf16[4,8,16,512]{3,2,1,0:T(8,128)(2,1)S(1)}) custom-call(s32[3]{0:T(128)S(1)} %pad_add_fusion.me.refs_0_, bf16[4,4,8,16,512]{4,3,2,1,0:T(8,128)(2,1)S(1)} %bitcast.11, bf16[4,4,8,16,512]{4,3,2,1,0:T(8,128)(2,1)} %copy-done.15), custom_call_target="tpu_custom_call" | custom-call | flops 1048576 | bytes 6291456 | tf_op jit(solution)/shard_map/pallas_call | solution.py:226
  121.7 1.0 copy-done.10
  123.5 2.2 %collective-permute-start.15 = (bf16[4,8,16,512]{3,2,1,0:T(8,128)(2,1)}, bf16[4,8,16,512]{3,2,1,0:T(8,128)(2,1)}, u32[]{:S(2)}, u32[]{:S(2)}) collective-permute-start(bf16[4,8,16,512]{3,2,1,0:T(8,128)(2,1)} %get-tuple-element.68), channel_id=1, source_target_pairs={{0,16},{8,24},{16,32},{24,40},{32,48},{40,56},{48,0},{56,8},{64,80... | collective-permute-start | bytes 1572872 | tf_op jit(solution)/shard_map/ppermute | solution.py:290
  125.7 2.9 %collective-permute-start.16 = (bf16[4,8,16,512]{3,2,1,0:T(8,128)(2,1)}, bf16[4,8,16,512]{3,2,1,0:T(8,128)(2,1)}, u32[]{:S(2)}, u32[]{:S(2)}) collective-permute-start(bf16[4,8,16,512]{3,2,1,0:T(8,128)(2,1)} %get-tuple-element.69), channel_id=1, source_target_pairs={{0,32},{8,40},{16,48},{24,56},{32,0},{40,8},{48,16},{56,24},{64,96... | collective-permute-start | bytes 1572872 | tf_op jit(solution)/shard_map/ppermute | solution.py:290
  128.6 2.5 %all-to-all-done.1.one_ref = bf16[8,2,8,32,256]{4,3,2,1,0:T(8,128)(2,1)} async-done(((bf16[8,2,8,32,256]{4,3,2,1,0:T(8,128)(2,1)}), bf16[8,2,8,32,256]{4,3,2,1,0:T(8,128)(2,1)}, u32[]{:S(2)}, u32[]{:S(2)}) %all-to-all-start.1) | async-done | bytes 2097184 | tf_op jit(solution)/shard_map/all_to_all | solution.py:297
  131.1 1.0 copy-done.6
  132.1 1.0 copy-done.8
  133.1 4.5 %shard_map.104 = (bf16[1024,256]{1,0:T(8,128)(2,1)}, bf16[4,4,2,2,16,512]{5,4,3,2,1,0:T(8,128)(2,1)S(1)}, bf16[4,4,2,2,16,512]{5,4,3,2,1,0:T(8,128)(2,1)S(1)}) custom-call(s32[3]{0:T(128)S(1)} %pad_add_fusion.me.refs_0_, bf16[8,2,8,32,256]{4,3,2,1,0:T(8,128)(2,1)} %all-to-all-done.1.one_ref, bf16[8,2,8,32,256]{4,3,2,1,0:T(8,128)(2,1)} %all-to-all-done.3.two_ref, ...), custom_call_target="tpu_custom_call" | custom-call | flops 805306368 | bytes 12582912 | tf_op jit(solution)/shard_map/pallas_call | solution.py:200
  137.7 3.7 %collective-permute-start.17 = (bf16[4,8,16,512]{3,2,1,0:T(8,128)(2,1)S(1)}, bf16[4,8,16,512]{3,2,1,0:T(8,128)(2,1)S(1)}, u32[]{:S(2)}, u32[]{:S(2)}) collective-permute-start(bf16[4,8,16,512]{3,2,1,0:T(8,128)(2,1)S(1)} %copy-done.13), channel_id=1, source_target_pairs={{0,48},{8,56},{16,0},{24,8},{32,16},{40,24},{48,32},{56,40},{64,11... | collective-permute-start | bytes 1572872 | tf_op jit(solution)/shard_map/ppermute | solution.py:290
  141.4 3.2 %shard_map.108 = (f32[4,8,16,512]{3,2,1,0:T(8,128)S(1)}, bf16[4,8,16,512]{3,2,1,0:T(8,128)(2,1)S(1)}, bf16[4,8,16,512]{3,2,1,0:T(8,128)(2,1)S(1)}, bf16[4,8,16,512]{3,2,1,0:T(8,128)(2,1)S(1)}) custom-call(s32[3]{0:T(128)S(1)} %pad_add_fusion.me.refs_0_, bf16[4,4,8,16,512]{4,3,2,1,0:T(8,128)(2,1)S(1)} %bitcast.10, ...), custom_call_target="tpu_custom_call" | custom-call | flops 1048576 | bytes 6291456 | tf_op jit(solution)/shard_map/pallas_call | solution.py:226
  144.7 7.3 %collective-permute-start.9 = (bf16[4,8,16,512]{3,2,1,0:T(8,128)(2,1)S(1)}, bf16[4,8,16,512]{3,2,1,0:T(8,128)(2,1)S(1)}, u32[]{:S(2)}, u32[]{:S(2)}) collective-permute-start(bf16[4,8,16,512]{3,2,1,0:T(8,128)(2,1)S(1)} %get-tuple-element.59), channel_id=1, source_target_pairs={{0,32},{8,40},{16,48},{24,56},{32,0},{40,8},{48,16},{56,24},{64,96... | collective-permute-start | bytes 1572872 | tf_op jit(solution)/shard_map/ppermute | solution.py:290
  152.1 0.8 collective-permute-done.16.b_ref
  152.9 12.0 %collective-permute-done.17.c_ref = bf16[4,8,16,512]{3,2,1,0:T(8,128)(2,1)S(1)} collective-permute-done((bf16[4,8,16,512]{3,2,1,0:T(8,128)(2,1)S(1)}, bf16[4,8,16,512]{3,2,1,0:T(8,128)(2,1)S(1)}, u32[]{:S(2)}, u32[]{:S(2)}) %collective-permute-start.17) | collective-permute-done | bytes 524320 | tf_op jit(solution)/shard_map/ppermute | solution.py:290
  164.9 1.9 shard_map.112
  166.9 3.3 %collective-permute-start.18 = (bf16[8,16,512]{2,1,0:T(8,128)(2,1)S(1)}, bf16[8,16,512]{2,1,0:T(8,128)(2,1)S(1)}, u32[]{:S(2)}, u32[]{:S(2)}) collective-permute-start(bf16[8,16,512]{2,1,0:T(8,128)(2,1)S(1)} %get-tuple-element.72), channel_id=1, source_target_pairs={{0,64},{8,72},{16,80},{24,88},{32,96},{40,104},{48,112},{56,120},{... | collective-permute-start | bytes 393224 | tf_op jit(solution)/shard_map/ppermute | solution.py:292
  170.2 4.5 %collective-permute-start.19 = (bf16[8,16,512]{2,1,0:T(8,128)(2,1)S(1)}, bf16[8,16,512]{2,1,0:T(8,128)(2,1)S(1)}, u32[]{:S(2)}, u32[]{:S(2)}) collective-permute-start(bf16[8,16,512]{2,1,0:T(8,128)(2,1)S(1)} %get-tuple-element.73), channel_id=1, source_target_pairs={{0,128},{8,136},{16,144},{24,152},{32,160},{40,168},{48,176},{56,1... | collective-permute-start | bytes 393224 | tf_op jit(solution)/shard_map/ppermute | solution.py:292
  174.7 5.2 %collective-permute-start.20 = (bf16[8,16,512]{2,1,0:T(8,128)(2,1)S(1)}, bf16[8,16,512]{2,1,0:T(8,128)(2,1)S(1)}, u32[]{:S(2)}, u32[]{:S(2)}) collective-permute-start(bf16[8,16,512]{2,1,0:T(8,128)(2,1)S(1)} %get-tuple-element.74), channel_id=1, source_target_pairs={{0,192},{8,200},{16,208},{24,216},{32,224},{40,232},{48,240},{56,2... | collective-permute-start | bytes 393224 | tf_op jit(solution)/shard_map/ppermute | solution.py:292
  179.9 1.0 shard_map.109
  181.0 5.3 %collective-permute-start.12 = (bf16[8,16,512]{2,1,0:T(8,128)(2,1)S(1)}, bf16[8,16,512]{2,1,0:T(8,128)(2,1)S(1)}, u32[]{:S(2)}, u32[]{:S(2)}) collective-permute-start(bf16[8,16,512]{2,1,0:T(8,128)(2,1)S(1)} %get-tuple-element.63), channel_id=1, source_target_pairs={{0,128},{8,136},{16,144},{24,152},{32,160},{40,168},{48,176},{56,1... | collective-permute-start | bytes 393224 | tf_op jit(solution)/shard_map/ppermute | solution.py:292
  186.3 2.9 %collective-permute-start.13 = (bf16[8,16,512]{2,1,0:T(8,128)(2,1)S(1)}, bf16[8,16,512]{2,1,0:T(8,128)(2,1)S(1)}, u32[]{:S(2)}, u32[]{:S(2)}) collective-permute-start(bf16[8,16,512]{2,1,0:T(8,128)(2,1)S(1)} %get-tuple-element.64), channel_id=1, source_target_pairs={{0,192},{8,200},{16,208},{24,216},{32,224},{40,232},{48,240},{56,2... | collective-permute-start | bytes 393224 | tf_op jit(solution)/shard_map/ppermute | solution.py:292
  189.9 1.0 shard_map.105
  191.0 5.8 %collective-permute-start.2 = (bf16[4,4,16,512]{3,2,1,0:T(8,128)(2,1)S(1)}, bf16[4,4,16,512]{3,2,1,0:T(8,128)(2,1)S(1)}, u32[]{:S(2)}, u32[]{:S(2)}) collective-permute-start(bf16[4,4,16,512]{3,2,1,0:T(8,128)(2,1)S(1)} %get-tuple-element.49), channel_id=1, source_target_pairs={{0,32},{8,40},{16,48},{24,56},{32,0},{40,8},{48,16},{56,24},{64,96... | collective-permute-start | bytes 786440 | tf_op jit(solution)/shard_map/ppermute | solution.py:290
  196.8 0.9 collective-permute-done.13.refs_4_
  198.3 3.8 %collective-permute-done.1.a_ref = bf16[4,4,16,512]{3,2,1,0:T(8,128)(2,1)S(1)} collective-permute-done((bf16[4,4,16,512]{3,2,1,0:T(8,128)(2,1)S(1)}, bf16[4,4,16,512]{3,2,1,0:T(8,128)(2,1)S(1)}, u32[]{:S(2)}, u32[]{:S(2)}) %collective-permute-start.1) | collective-permute-done | bytes 262176 | tf_op jit(solution)/shard_map/ppermute | solution.py:290
  202.2 2.8 %collective-permute-done.2.b_ref = bf16[4,4,16,512]{3,2,1,0:T(8,128)(2,1)S(1)} collective-permute-done((bf16[4,4,16,512]{3,2,1,0:T(8,128)(2,1)S(1)}, bf16[4,4,16,512]{3,2,1,0:T(8,128)(2,1)S(1)}, u32[]{:S(2)}, u32[]{:S(2)}) %collective-permute-start.2) | collective-permute-done | bytes 262176 | tf_op jit(solution)/shard_map/ppermute | solution.py:290
  206.6 3.5 %collective-permute-start.5 = (bf16[4,16,512]{2,1,0:T(8,128)(2,1)S(1)}, bf16[4,16,512]{2,1,0:T(8,128)(2,1)S(1)}, u32[]{:S(2)}, u32[]{:S(2)}) collective-permute-start(bf16[4,16,512]{2,1,0:T(8,128)(2,1)S(1)} %get-tuple-element.53), channel_id=1, source_target_pairs={{0,128},{8,136},{16,144},{24,152},{32,160},{40,168},{48,176},{56,1... | collective-permute-start | bytes 196616 | tf_op jit(solution)/shard_map/ppermute | solution.py:292
  210.2 4.0 %collective-permute-start.6 = (bf16[4,16,512]{2,1,0:T(8,128)(2,1)S(1)}, bf16[4,16,512]{2,1,0:T(8,128)(2,1)S(1)}, u32[]{:S(2)}, u32[]{:S(2)}) collective-permute-start(bf16[4,16,512]{2,1,0:T(8,128)(2,1)S(1)} %get-tuple-element.54), channel_id=1, source_target_pairs={{0,192},{8,200},{16,208},{24,216},{32,224},{40,232},{48,240},{56,2... | collective-permute-start | bytes 196616 | tf_op jit(solution)/shard_map/ppermute | solution.py:292
  214.2 0.8 pad_maximum_fusion
  215.7 2.8 %collective-permute-done.6.refs_4_ = bf16[4,16,512]{2,1,0:T(8,128)(2,1)S(1)} collective-permute-done((bf16[4,16,512]{2,1,0:T(8,128)(2,1)S(1)}, bf16[4,16,512]{2,1,0:T(8,128)(2,1)S(1)}, u32[]{:S(2)}, u32[]{:S(2)}) %collective-permute-start.6) | collective-permute-done | bytes 65568 | tf_op jit(solution)/shard_map/ppermute | solution.py:292
  (54 shorter events, 7.2 us)
Async XLA Ops:
  0.7 1.2 copy-start
  2.0 1.0 copy-start.5
  3.0 1.0 copy-start.7
  4.1 1.2 copy-start.9
  40.9 28.9 %all-to-all-start = ((bf16[8,2,4,64,256]{4,3,2,1,0:T(8,128)(2,1)}), bf16[8,2,4,64,256]{4,3,2,1,0:T(8,128)(2,1)S(1)}, u32[]{:S(2)}, u32[]{:S(2)}) async-start(bf16[8,2,4,64,256]{4,3,2,1,0:T(8,128)(2,1)} %get-tuple-element.40), calls=%async_computation | async-start | bytes 4194304 | tf_op jit(solution)/shard_map/all_to_all | solution.py:297
  55.0 1.3 copy-start.2
  69.8 1.4 copy-start.14
  71.2 29.9 %all-to-all-start.3 = ((bf16[8,2,8,32,256]{4,3,2,1,0:T(8,128)(2,1)}), bf16[8,2,8,32,256]{4,3,2,1,0:T(8,128)(2,1)}, u32[]{:S(2)}, u32[]{:S(2)}) async-start(bf16[8,2,8,32,256]{4,3,2,1,0:T(8,128)(2,1)} %get-tuple-element.43), calls=%async_computation.3 | async-start | bytes 4194304 | tf_op jit(solution)/shard_map/all_to_all | solution.py:297
  86.2 1.3 copy-start.4
  101.1 30.0 %all-to-all-start.1 = ((bf16[8,2,8,32,256]{4,3,2,1,0:T(8,128)(2,1)}), bf16[8,2,8,32,256]{4,3,2,1,0:T(8,128)(2,1)}, u32[]{:S(2)}, u32[]{:S(2)}) async-start(bf16[8,2,8,32,256]{4,3,2,1,0:T(8,128)(2,1)} %copy-done.4), calls=%async_computation.1 | async-start | bytes 4194304 | tf_op jit(solution)/shard_map/all_to_all | solution.py:297
  107.4 7.0 %collective-permute-start.14 = (bf16[4,4,8,16,512]{4,3,2,1,0:T(8,128)(2,1)}, bf16[4,4,8,16,512]{4,3,2,1,0:T(8,128)(2,1)S(1)}, u32[]{:S(2)}, u32[]{:S(2)}) collective-permute-start(bf16[4,4,8,16,512]{4,3,2,1,0:T(8,128)(2,1)} %bitcast.16), channel_id=1, source_target_pairs={{0,8},{8,0},{16,24},{24,16},{32,40},{40,32},{48,56},{56,48},{64,72... | collective-permute-start | bytes 6291464 | tf_op jit(solution)/shard_map/ppermute | solution.py:288
  107.4 34.0 %collective-permute-start.7 = (bf16[4,4,8,16,512]{4,3,2,1,0:T(8,128)(2,1)}, bf16[4,4,8,16,512]{4,3,2,1,0:T(8,128)(2,1)}, u32[]{:S(2)}, u32[]{:S(2)}) collective-permute-start(bf16[4,4,8,16,512]{4,3,2,1,0:T(8,128)(2,1)} %bitcast.15), channel_id=1, source_target_pairs={{0,8},{8,0},{16,24},{24,16},{32,40},{40,32},{48,56},{56,48},{64,72... | collective-permute-start | bytes 6291464 | tf_op jit(solution)/shard_map/ppermute | solution.py:288
  114.4 1.4 copy-start.15
  115.8 1.6 copy-start.3
  117.4 13.6 %copy-start.1 = (bf16[8,128,512]{2,1,0:T(8,128)(2,1)S(1)}, bf16[8,128,512]{2,1,0:T(8,128)(2,1)}, u32[]{:S(2)}) copy-start(bf16[8,128,512]{2,1,0:T(8,128)(2,1)} %up_ref.7) | copy-start | bytes 3145732
  121.7 1.0 copy-start.10
  122.6 0.8 copy-start.12
  123.5 21.3 %collective-permute-start.15 = (bf16[4,8,16,512]{3,2,1,0:T(8,128)(2,1)}, bf16[4,8,16,512]{3,2,1,0:T(8,128)(2,1)}, u32[]{:S(2)}, u32[]{:S(2)}) collective-permute-start(bf16[4,8,16,512]{3,2,1,0:T(8,128)(2,1)} %get-tuple-element.68), channel_id=1, source_target_pairs={{0,16},{8,24},{16,32},{24,40},{32,48},{40,56},{48,0},{56,8},{64,80... | collective-permute-start | bytes 1572872 | tf_op jit(solution)/shard_map/ppermute | solution.py:290
  125.7 27.2 %collective-permute-start.16 = (bf16[4,8,16,512]{3,2,1,0:T(8,128)(2,1)}, bf16[4,8,16,512]{3,2,1,0:T(8,128)(2,1)}, u32[]{:S(2)}, u32[]{:S(2)}) collective-permute-start(bf16[4,8,16,512]{3,2,1,0:T(8,128)(2,1)} %get-tuple-element.69), channel_id=1, source_target_pairs={{0,32},{8,40},{16,48},{24,56},{32,0},{40,8},{48,16},{56,24},{64,96... | collective-permute-start | bytes 1572872 | tf_op jit(solution)/shard_map/ppermute | solution.py:290
  131.1 1.0 copy-start.6
  132.1 1.0 copy-start.8
  133.1 4.5 %copy-start.13 = (bf16[4,8,16,512]{3,2,1,0:T(8,128)(2,1)S(1)}, bf16[4,8,16,512]{3,2,1,0:T(8,128)(2,1)}, u32[]{:S(2)}) copy-start(bf16[4,8,16,512]{3,2,1,0:T(8,128)(2,1)} %copy-done.12) | copy-start | bytes 1572868
  137.7 52.2 %collective-permute-start = (bf16[4,4,4,16,512]{4,3,2,1,0:T(8,128)(2,1)S(1)}, bf16[4,4,4,16,512]{4,3,2,1,0:T(8,128)(2,1)S(1)}, u32[]{:S(2)}, u32[]{:S(2)}) collective-permute-start(bf16[4,4,4,16,512]{4,3,2,1,0:T(8,128)(2,1)S(1)} %bitcast.13), channel_id=1, source_target_pairs={{0,8},{8,0},{16,24},{24,16},{32,40},{40,32},{48,56},{56,48},{64,72... | collective-permute-start | bytes 3145736 | tf_op jit(solution)/shard_map/ppermute | solution.py:288
  137.7 27.2 %collective-permute-start.17 = (bf16[4,8,16,512]{3,2,1,0:T(8,128)(2,1)S(1)}, bf16[4,8,16,512]{3,2,1,0:T(8,128)(2,1)S(1)}, u32[]{:S(2)}, u32[]{:S(2)}) collective-permute-start(bf16[4,8,16,512]{3,2,1,0:T(8,128)(2,1)S(1)} %copy-done.13), channel_id=1, source_target_pairs={{0,48},{8,56},{16,0},{24,8},{32,16},{40,24},{48,32},{56,40},{64,11... | collective-permute-start | bytes 1572872 | tf_op jit(solution)/shard_map/ppermute | solution.py:290
  141.4 23.5 %copy-start.11 = (f32[4,8,16,512]{3,2,1,0:T(8,128)S(1)}, f32[4,8,16,512]{3,2,1,0:T(8,128)}, u32[]{:S(2)}) copy-start(f32[4,8,16,512]{3,2,1,0:T(8,128)} %copy-done.10) | copy-start | bytes 3145732
  144.6 25.6 %collective-permute-start.8 = (bf16[4,8,16,512]{3,2,1,0:T(8,128)(2,1)S(1)}, bf16[4,8,16,512]{3,2,1,0:T(8,128)(2,1)S(1)}, u32[]{:S(2)}, u32[]{:S(2)}) collective-permute-start(bf16[4,8,16,512]{3,2,1,0:T(8,128)(2,1)S(1)} %get-tuple-element.58), channel_id=1, source_target_pairs={{0,16},{8,24},{16,32},{24,40},{32,48},{40,56},{48,0},{56,8},{64,80... | collective-permute-start | bytes 1572872 | tf_op jit(solution)/shard_map/ppermute | solution.py:290
  144.7 30.0 %collective-permute-start.9 = (bf16[4,8,16,512]{3,2,1,0:T(8,128)(2,1)S(1)}, bf16[4,8,16,512]{3,2,1,0:T(8,128)(2,1)S(1)}, u32[]{:S(2)}, u32[]{:S(2)}) collective-permute-start(bf16[4,8,16,512]{3,2,1,0:T(8,128)(2,1)S(1)} %get-tuple-element.59), channel_id=1, source_target_pairs={{0,32},{8,40},{16,48},{24,56},{32,0},{40,8},{48,16},{56,24},{64,96... | collective-permute-start | bytes 1572872 | tf_op jit(solution)/shard_map/ppermute | solution.py:290
  152.9 27.0 %collective-permute-start.10 = (bf16[4,8,16,512]{3,2,1,0:T(8,128)(2,1)S(1)}, bf16[4,8,16,512]{3,2,1,0:T(8,128)(2,1)S(1)}, u32[]{:S(2)}, u32[]{:S(2)}) collective-permute-start(bf16[4,8,16,512]{3,2,1,0:T(8,128)(2,1)S(1)} %get-tuple-element.60), channel_id=1, source_target_pairs={{0,48},{8,56},{16,0},{24,8},{32,16},{40,24},{48,32},{56,40},{64,11... | collective-permute-start | bytes 1572872 | tf_op jit(solution)/shard_map/ppermute | solution.py:290
  166.9 14.1 %collective-permute-start.18 = (bf16[8,16,512]{2,1,0:T(8,128)(2,1)S(1)}, bf16[8,16,512]{2,1,0:T(8,128)(2,1)S(1)}, u32[]{:S(2)}, u32[]{:S(2)}) collective-permute-start(bf16[8,16,512]{2,1,0:T(8,128)(2,1)S(1)} %get-tuple-element.72), channel_id=1, source_target_pairs={{0,64},{8,72},{16,80},{24,88},{32,96},{40,104},{48,112},{56,120},{... | collective-permute-start | bytes 393224 | tf_op jit(solution)/shard_map/ppermute | solution.py:292
  170.2 16.1 %collective-permute-start.19 = (bf16[8,16,512]{2,1,0:T(8,128)(2,1)S(1)}, bf16[8,16,512]{2,1,0:T(8,128)(2,1)S(1)}, u32[]{:S(2)}, u32[]{:S(2)}) collective-permute-start(bf16[8,16,512]{2,1,0:T(8,128)(2,1)S(1)} %get-tuple-element.73), channel_id=1, source_target_pairs={{0,128},{8,136},{16,144},{24,152},{32,160},{40,168},{48,176},{56,1... | collective-permute-start | bytes 393224 | tf_op jit(solution)/shard_map/ppermute | solution.py:292
  174.7 14.6 %collective-permute-start.20 = (bf16[8,16,512]{2,1,0:T(8,128)(2,1)S(1)}, bf16[8,16,512]{2,1,0:T(8,128)(2,1)S(1)}, u32[]{:S(2)}, u32[]{:S(2)}) collective-permute-start(bf16[8,16,512]{2,1,0:T(8,128)(2,1)S(1)} %get-tuple-element.74), channel_id=1, source_target_pairs={{0,192},{8,200},{16,208},{24,216},{32,224},{40,232},{48,240},{56,2... | collective-permute-start | bytes 393224 | tf_op jit(solution)/shard_map/ppermute | solution.py:292
  180.9 15.9 %collective-permute-start.11 = (bf16[8,16,512]{2,1,0:T(8,128)(2,1)S(1)}, bf16[8,16,512]{2,1,0:T(8,128)(2,1)S(1)}, u32[]{:S(2)}, u32[]{:S(2)}) collective-permute-start(bf16[8,16,512]{2,1,0:T(8,128)(2,1)S(1)} %get-tuple-element.62), channel_id=1, source_target_pairs={{0,64},{8,72},{16,80},{24,88},{32,96},{40,104},{48,112},{56,120},{... | collective-permute-start | bytes 393224 | tf_op jit(solution)/shard_map/ppermute | solution.py:292
  181.0 15.8 %collective-permute-start.12 = (bf16[8,16,512]{2,1,0:T(8,128)(2,1)S(1)}, bf16[8,16,512]{2,1,0:T(8,128)(2,1)S(1)}, u32[]{:S(2)}, u32[]{:S(2)}) collective-permute-start(bf16[8,16,512]{2,1,0:T(8,128)(2,1)S(1)} %get-tuple-element.63), channel_id=1, source_target_pairs={{0,128},{8,136},{16,144},{24,152},{32,160},{40,168},{48,176},{56,1... | collective-permute-start | bytes 393224 | tf_op jit(solution)/shard_map/ppermute | solution.py:292
  186.3 11.4 %collective-permute-start.13 = (bf16[8,16,512]{2,1,0:T(8,128)(2,1)S(1)}, bf16[8,16,512]{2,1,0:T(8,128)(2,1)S(1)}, u32[]{:S(2)}, u32[]{:S(2)}) collective-permute-start(bf16[8,16,512]{2,1,0:T(8,128)(2,1)S(1)} %get-tuple-element.64), channel_id=1, source_target_pairs={{0,192},{8,200},{16,208},{24,216},{32,224},{40,232},{48,240},{56,2... | collective-permute-start | bytes 393224 | tf_op jit(solution)/shard_map/ppermute | solution.py:292
  190.9 11.3 %collective-permute-start.1 = (bf16[4,4,16,512]{3,2,1,0:T(8,128)(2,1)S(1)}, bf16[4,4,16,512]{3,2,1,0:T(8,128)(2,1)S(1)}, u32[]{:S(2)}, u32[]{:S(2)}) collective-permute-start(bf16[4,4,16,512]{3,2,1,0:T(8,128)(2,1)S(1)} %get-tuple-element.48), channel_id=1, source_target_pairs={{0,16},{8,24},{16,32},{24,40},{32,48},{40,56},{48,0},{56,8},{64,80... | collective-permute-start | bytes 786440 | tf_op jit(solution)/shard_map/ppermute | solution.py:290
  191.0 14.0 %collective-permute-start.2 = (bf16[4,4,16,512]{3,2,1,0:T(8,128)(2,1)S(1)}, bf16[4,4,16,512]{3,2,1,0:T(8,128)(2,1)S(1)}, u32[]{:S(2)}, u32[]{:S(2)}) collective-permute-start(bf16[4,4,16,512]{3,2,1,0:T(8,128)(2,1)S(1)} %get-tuple-element.49), channel_id=1, source_target_pairs={{0,32},{8,40},{16,48},{24,56},{32,0},{40,8},{48,16},{56,24},{64,96... | collective-permute-start | bytes 786440 | tf_op jit(solution)/shard_map/ppermute | solution.py:290
  196.8 8.2 %collective-permute-start.3 = (bf16[4,4,16,512]{3,2,1,0:T(8,128)(2,1)S(1)}, bf16[4,4,16,512]{3,2,1,0:T(8,128)(2,1)S(1)}, u32[]{:S(2)}, u32[]{:S(2)}) collective-permute-start(bf16[4,4,16,512]{3,2,1,0:T(8,128)(2,1)S(1)} %get-tuple-element.50), channel_id=1, source_target_pairs={{0,48},{8,56},{16,0},{24,8},{32,16},{40,24},{48,32},{56,40},{64,11... | collective-permute-start | bytes 786440 | tf_op jit(solution)/shard_map/ppermute | solution.py:290
  205.8 9.2 %collective-permute-start.4 = (bf16[4,16,512]{2,1,0:T(8,128)(2,1)S(1)}, bf16[4,16,512]{2,1,0:T(8,128)(2,1)S(1)}, u32[]{:S(2)}, u32[]{:S(2)}) collective-permute-start(bf16[4,16,512]{2,1,0:T(8,128)(2,1)S(1)} %get-tuple-element.52), channel_id=1, source_target_pairs={{0,64},{8,72},{16,80},{24,88},{32,96},{40,104},{48,112},{56,120},{... | collective-permute-start | bytes 196616 | tf_op jit(solution)/shard_map/ppermute | solution.py:292
  206.6 9.1 %collective-permute-start.5 = (bf16[4,16,512]{2,1,0:T(8,128)(2,1)S(1)}, bf16[4,16,512]{2,1,0:T(8,128)(2,1)S(1)}, u32[]{:S(2)}, u32[]{:S(2)}) collective-permute-start(bf16[4,16,512]{2,1,0:T(8,128)(2,1)S(1)} %get-tuple-element.53), channel_id=1, source_target_pairs={{0,128},{8,136},{16,144},{24,152},{32,160},{40,168},{48,176},{56,1... | collective-permute-start | bytes 196616 | tf_op jit(solution)/shard_map/ppermute | solution.py:292
  210.2 8.3 %collective-permute-start.6 = (bf16[4,16,512]{2,1,0:T(8,128)(2,1)S(1)}, bf16[4,16,512]{2,1,0:T(8,128)(2,1)S(1)}, u32[]{:S(2)}, u32[]{:S(2)}) collective-permute-start(bf16[4,16,512]{2,1,0:T(8,128)(2,1)S(1)} %get-tuple-element.54), channel_id=1, source_target_pairs={{0,192},{8,200},{16,208},{24,216},{32,224},{40,232},{48,240},{56,2... | collective-permute-start | bytes 196616 | tf_op jit(solution)/shard_map/ppermute | solution.py:292

commit v2 on v1

v2 whole, which is shorter than its diff:
```python
import jax
import jax.numpy as jnp
from jax import lax
from jax.experimental import pallas as pl
from jax.experimental.pallas import tpu as pltpu
from jax.sharding import PartitionSpec as P

BLK_IN = 128
BLK_HID = 512
SPREAD = 8
LOCAL = 8
PEERS = 8
PAIR = 2 * SPREAD
VMEM_LIMIT = 63 * 1024 * 1024
ROWS = 16
PAIRS = LOCAL // 2
CHUNKS = (1, 3)

half = jnp.bfloat16
single = jnp.float32
root_two_pi = 0.7978845608028654

Z, Y, CORES = 4, 4, 2


def dp_perm(dz, dy, dc):
    pairs = []
    for z in range(Z):
        for y in range(Y):
            for c in range(CORES):
                source = (z * Y + y) * CORES + c
                target = ((z + dz) % Z * Y + (y + dy) % Y) * CORES + (c + dc) % CORES
                pairs.append((source, target))
    return pairs


def gelu_parts(pre):
    inner = root_two_pi * (pre + 0.044715 * pre * pre * pre)
    curve = jnp.tanh(inner)
    value = 0.5 * pre * (1.0 + curve)
    slope = 0.5 * (1.0 + curve) + 0.5 * pre * (1.0 - curve * curve) * root_two_pi * (
        1.0 + 3.0 * 0.044715 * pre * pre
    )
    return value, slope


def dot(left, right, over_left, over_right):
    return lax.dot_general(
        left, right, (((over_left,), (over_right,)), ((), ())), preferred_element_type=single
    )


def spread_pair(first, second):
    tokens = first.shape[-1]
    parts = [r.reshape(BLK_HID // SPREAD, SPREAD, tokens) for r in (first, second)]
    return jnp.concatenate(parts, axis=1).astype(half)


def call(
    kernel, grid, in_specs, out_specs, out_shape, scratch=(), after=(), carry=()
):
    first = 1 + len(in_specs)
    extra = len(after) + len(carry)
    outs = len(out_specs)
    untouched = pl.BlockSpec(memory_space=pl.ANY)

    def body(*refs):
        ends = first + extra + outs
        kernel(*refs[:first], *refs[first + extra : ends], *refs[ends + len(carry) :])

    run = pl.pallas_call(
        body,
        grid_spec=pltpu.PrefetchScalarGridSpec(
            num_scalar_prefetch=1,
            grid=grid,
            in_specs=list(in_specs) + [untouched] * extra,
            out_specs=list(out_specs) + [untouched] * len(carry),
            scratch_shapes=list(scratch),
        ),
        out_shape=list(out_shape) + [jax.ShapeDtypeStruct(c.shape, c.dtype) for c in carry],
        input_output_aliases={first + len(after) + i: outs + i for i in range(len(carry))},
        compiler_params=pltpu.CompilerParams(vmem_limit_bytes=VMEM_LIMIT),
    )
    return lambda *operands: run(*operands, *after, *carry)


def first_kernel(me, x_ref, g_ref, up_ref, down_ref, *out_refs):
    ups, downs = [], []
    for i in range(2):
        rows = slice(i * BLK_IN, (i + 1) * BLK_IN)
        ups.append(dot(up_ref[i], x_ref[rows], 0, 0))
        downs.append(dot(down_ref[i], g_ref[rows], 1, 0))
    for slot, pair in enumerate((ups, downs)):
        spread = spread_pair(*pair).reshape(PEERS, LOCAL, PAIR, -1)
        start = 0
        for pairs, out in zip(CHUNKS, out_refs):
            out[:, slot] = spread[:, start : start + 2 * pairs]
            start += 2 * pairs


def first_stage(me, inputs, grad_out, up_left, down_right):
    tokens = inputs.shape[1]
    return call(
        first_kernel,
        (PAIRS,),
        [
            pl.BlockSpec((2 * BLK_IN, tokens), lambda p, me: (p, 0)),
            pl.BlockSpec((2 * BLK_IN, tokens), lambda p, me: (p, 0)),
            pl.BlockSpec((2, BLK_IN, BLK_HID), lambda p, me: (p, 0, 0)),
            pl.BlockSpec((2, BLK_HID, BLK_IN), lambda p, me: (p, 0, 0)),
        ],
        [
            pl.BlockSpec((PEERS, 2, 2 * n, PAIR, tokens), lambda p, me: (0, 0, 0, p, 0))
            for n in CHUNKS
        ],
        [
            jax.ShapeDtypeStruct((PEERS, 2, 2 * n, LOCAL * SPREAD, tokens), half) for n in CHUNKS
        ],
    )(me, inputs, grad_out, up_left, down_right)


def place(me, held, own_ref, other_ref, index):
    for ry in range(Y):
        for rz in range(Z):
            group = ((me[2] + rz) % Z * Y + (me[1] + ry) % Y) * CORES
            own_ref[(ry, rz) + index] = held[group + me[0]]
            other_ref[(ry, rz) + index] = held[group + 1 - me[0]]


def middle_kernel(me, got_ref, up_ref, down_ref, back_ref, own_ref, other_ref, held):
    lows, mids = [], []
    for i in range(2):
        v = got_ref[:, 0, i].reshape(BLK_HID, -1)
        f = got_ref[:, 1, i].reshape(BLK_HID, -1)
        up, down = up_ref[i], down_ref[i]
        value, slope = gelu_parts(dot(up, v, 0, 0))
        hidden = value.astype(half)
        lows.append(dot(down, hidden, 0, 0))
        held[0] = dot(hidden, f, 1, 1).astype(half).reshape(-1, ROWS, BLK_HID)
        place(me, held.at[0], own_ref, other_ref, (0, i))
        back = (dot(down, f, 1, 0) * slope).astype(half)
        mids.append(dot(up, back, 1, 0))
        held[1] = dot(v, back, 1, 1).astype(half).reshape(-1, ROWS, BLK_HID)
        place(me, held.at[1], own_ref, other_ref, (1, i))
    back_ref[:, 0] = spread_pair(*lows).reshape(PEERS, LOCAL, PAIR, -1)
    back_ref[:, 1] = spread_pair(*mids).reshape(PEERS, LOCAL, PAIR, -1)


def middle_stage(me, chunk, got, up_right, down_left, **order):
    tokens = got.shape[-1]
    pairs = CHUNKS[chunk]
    start = sum(CHUNKS[:chunk])
    grads = jax.ShapeDtypeStruct((Y, Z, 2, 2 * pairs, ROWS, BLK_HID), half)
    grads_spec = pl.BlockSpec((Y, Z, 2, 2, ROWS, BLK_HID), lambda p, me: (0, 0, 0, p, 0, 0))
    weight = pl.BlockSpec((2, BLK_HID, BLK_HID), lambda p, me: (start + p, 0, 0))
    return call(
        middle_kernel,
        (pairs,),
        [
            pl.BlockSpec((PEERS, 2, 2, LOCAL * SPREAD, tokens), lambda p, me: (0, 0, p, 0, 0)),
            weight,
            weight,
        ],
        [
            pl.BlockSpec((PEERS, 2, LOCAL, PAIR, tokens), lambda p, me: (0, 0, 0, p, 0)),
            grads_spec,
            grads_spec,
        ],
        [
            jax.ShapeDtypeStruct((PEERS, 2, LOCAL, pairs * PAIR, tokens), half),
            grads,
            grads,
        ],
        scratch=[pltpu.VMEM((2, BLK_HID // ROWS, ROWS, BLK_HID), half)],
        **order,
    )(me, got, up_right, down_left)


def features(one_ref, two_ref, slot, i):
    both = jnp.concatenate([one_ref[:, slot, i], two_ref[:, slot, i]], axis=1)
    return both.reshape(BLK_HID, -1)


def outer_kernel(me, one_ref, two_ref, x_ref, g_ref, own_ref, other_ref, held, held_down):
    rows4 = BLK_IN // (Z * Y * CORES)
    evens, odds = [], []
    for i in range(4):
        rows = slice(i * BLK_IN, (i + 1) * BLK_IN)
        left = dot(x_ref[rows], features(one_ref, two_ref, 1, i), 1, 1)
        left = left.reshape(-1, 2 * rows4, BLK_HID)
        evens.append(left[:, :rows4])
        odds.append(left[:, rows4:])
        right = dot(features(one_ref, two_ref, 0, i), g_ref[rows], 1, 1).astype(half)
        held_down[:, :, i * BLK_IN : (i + 1) * BLK_IN] = right.reshape(-1, ROWS, BLK_IN)
    for core, parts in enumerate((evens, odds)):
        held[core] = jnp.concatenate(parts, axis=1).astype(half)
    for y in range(Y):
        for z in range(Z):
            chip = z * Y + y
            own_ref[y, z, 0, 0] = held[me[0], chip]
            other_ref[y, z, 0, 0] = held[1 - me[0], chip]
            own_ref[y, z, 1, 0] = held_down[chip * CORES + me[0]]
            other_ref[y, z, 1, 0] = held_down[chip * CORES + 1 - me[0]]


def got_specs(tokens):
    return [
        pl.BlockSpec((PEERS, 2, 4, n * PAIR, tokens), lambda p, me: (0, 0, p, 0, 0)) for n in CHUNKS
    ]


def outer_stage(me, one, two, inputs, grad_out, **order):
    tokens = inputs.shape[1]
    groups = LOCAL // 4
    grads = jax.ShapeDtypeStruct((Y, Z, 2, groups, ROWS, BLK_HID), half)
    grads_spec = pl.BlockSpec((Y, Z, 2, 1, ROWS, BLK_HID), lambda p, me: (0, 0, 0, p, 0, 0))
    feats = pl.BlockSpec((4 * BLK_IN, tokens), lambda p, me: (p, 0))
    return call(
        outer_kernel,
        (groups,),
        got_specs(tokens) + [feats, feats],
        [grads_spec, grads_spec],
        [grads, grads],
        scratch=[
            pltpu.VMEM((CORES, Z * Y, ROWS, BLK_HID), half),
            pltpu.VMEM((Z * Y * CORES, ROWS, BLK_HID), half),
        ],
        **order,
    )(me, one, two, inputs, grad_out)


def back_kernel(me, one_ref, two_ref, up_ref, in_ref):
    for i in range(4):
        rows = slice(i * BLK_IN, (i + 1) * BLK_IN)
        in_ref[rows] = dot(up_ref[i], features(one_ref, two_ref, 1, i), 1, 0).astype(half)


def back_stage(me, one, two, up_left, **order):
    tokens = one.shape[-1]
    return call(
        back_kernel,
        (LOCAL // 4,),
        got_specs(tokens) + [pl.BlockSpec((4, BLK_IN, BLK_HID), lambda p, me: (p, 0, 0))],
        [pl.BlockSpec((4 * BLK_IN, tokens), lambda p, me: (p, 0))],
        [jax.ShapeDtypeStruct((LOCAL * BLK_IN, tokens), half)],
        **order,
    )(me, one, two, up_left)


def flat(array):
    return array.reshape(Y, Z, -1, ROWS, BLK_HID)


def core_step(own, other):
    own = flat(own)
    got = lax.ppermute(flat(other), "dp", dp_perm(0, 0, 1))
    sums = [own[r].astype(single) + got[r].astype(single) for r in range(Y)]
    return sums[0], *[total.astype(half) for total in sums[1:]]


def gate(me, arrays, after=()):
    def kernel(me, out_ref):
        out_ref[...] = jnp.zeros_like(out_ref)

    return call(
        kernel,
        (1,),
        [],
        [pl.BlockSpec((8, 128), lambda p, me: (0, 0))],
        [jax.ShapeDtypeStruct((8, 128), single)],
        after=after,
        carry=arrays,
    )(me)[1:]


def add(keep, got):
    return keep + sum(part.astype(single) for part in got)


def line_step(keep, *sends):
    got = [lax.ppermute(s, "dp", dp_perm(0, r + 1, 0)) for r, s in enumerate(sends)]
    sums = [add(keep[r], [part[r] for part in got]) for r in range(Z)]
    return sums[0], *[total.astype(half) for total in sums[1:]]


def end_moves(keep, *sends):
    return [lax.ppermute(s, "dp", dp_perm(r + 1, 0, 0)) for r, s in enumerate(sends)]


def exchange(array):
    return lax.all_to_all(array, "block", split_axis=0, concat_axis=0, tiled=True)


def line_groups(of_y):
    spans = (Z, CORES) if of_y else (Y, CORES)
    groups = []
    for i in range(spans[0]):
        for c in range(CORES):
            lines = [(i, y) if of_y else (z, i) for y, z in zip(range(Y), range(Z))]
            groups.append([(z * Y + y) * CORES + c for z, y in lines])
    return groups


def share(array, of_y):
    got = lax.all_to_all(
        array, "dp", split_axis=0, concat_axis=0, tiled=True, axis_index_groups=line_groups(of_y)
    )
    return got.astype(single).sum(axis=0)


def shards(inputs, grad_out, up_left, up_right, down_left, down_right):
    tokens = inputs.shape[1]
    factor = float(tokens * lax.axis_size("dp")) ** (-0.5)
    dp = lax.axis_index("dp")
    me = jnp.stack([dp % CORES, dp // CORES % Y, dp // (CORES * Y)]).astype(jnp.int32)

    one, two = first_stage(me, inputs, grad_out, up_left, down_right)
    back1, own, other = middle_stage(me, 0, exchange(one), up_right, down_left)
    sums1 = line_step(*core_step(own, other))
    (back1,) = gate(me, [back1], sums1)
    back2, own, other, *sums1 = middle_stage(
        me, 1, exchange(two), up_right, down_left, carry=sums1
    )
    sums2 = core_step(own, other)
    back1, back2 = exchange(back1), exchange(back2)
    own, other = outer_stage(me, back1, back2, inputs, grad_out)
    outer = flat(own).astype(single)
    outer = outer + lax.ppermute(flat(other), "dp", dp_perm(0, 0, 1)).astype(single)
    sums2 = line_step(*sums2)
    got1 = end_moves(*sums1)
    outer, *sums2 = gate(me, [outer.astype(half), *sums2], got1)
    got2 = end_moves(*sums2)
    (grad_in,) = back_stage(me, back1, back2, up_left, after=(outer,))
    outer = share(share(outer, True).astype(half), False) * factor
    outer = outer.reshape(2, -1, ROWS, BLK_HID)
    grads = [
        (factor * add(sums[0], got)).reshape(2, -1, ROWS, BLK_HID)
        for sums, got in ((sums1, got1), (sums2, got2))
    ]
    grad_left_down, grad_right_up = [
        jnp.concatenate([g[k] for g in grads], axis=0) for k in range(2)
    ]
    rows4 = BLK_IN // (Z * Y * CORES)
    grad_left_up = outer[0].reshape(LOCAL, rows4, BLK_HID)
    grad_right_down = (
        outer[1].reshape(LOCAL // 4, ROWS, 4, BLK_IN).transpose(0, 2, 1, 3).reshape(LOCAL, ROWS, BLK_IN)
    )
    return grad_in, grad_left_up, grad_right_up, grad_left_down, grad_right_down


def solution(mesh):
    in_specs = (
        P("block", "dp"),
        P("block", "dp"),
        P("block", None, None),
        P("block", None, None),
        P("block", None, None),
        P("block", None, None),
    )
    out_specs = (
        P("block", "dp"),
        P("block", "dp", None),
        P("block", "dp", None),
        P("block", "dp", None),
        P("block", "dp", None),
    )
    return jax.shard_map(shards, mesh=mesh, in_specs=in_specs, out_specs=out_specs, check_vma=False)
```

time: 223 us -> 191 us (0.86)
  local copies, waits for them, and re-layouts: 16.1 us -> 2.96 us
  other arithmetic: 1.55 us -> 14.5 us
  starting transfers between devices: 70.4 us -> 57.6 us
  blocking collectives: 31.5 us -> 20.2 us
  Pallas kernels: 40.2 us -> 36.6 us
  waiting for transfers between devices: 59.8 us -> 56.9 us
    ppermute x21 -> x15, starting transfers between devices: 52.4 us -> 31.1 us  [the longest x6 19.5 us: end_moves(): lax.ppermute(s, 'dp', dp_perm(r + 1, 0, 0))]
    unnamed x32, local copies, waits for them, and re-layouts: 15.4 us -> 0.67 us
    all_to_all x1, blocking collectives: 31.5 us -> 20.2 us  [exchange(): lax.all_to_all(array, 'block', split_axis=0, concat_axis=0, tiled=True)]
    ppermute x21 -> x15, waiting for transfers between devices: 30.3 us -> 21.6 us  [the longest x6 11.1 us: line_step(): lax.ppermute(s, 'dp', dp_perm(0, r + 1, 0))]
    all_to_all x0 -> x2, waiting for transfers between devices: none -> 8.47 us  [share(): lax.all_to_all(array, 'dp', split_axis=0, concat_axis=0, tiled=True, axis...]
    all_to_all x0 -> x2, starting transfers between devices: none -> 7.78 us  [share(): lax.all_to_all(array, 'dp', split_axis=0, concat_axis=0, tiled=True, axis...]
    convert_element_type x0 -> x3, other arithmetic: none -> 4.71 us  [the longest x2 3.27 us: core_step(): return (sums[0], *[total.astype(half) for total in sums[1:]])]
    add x0 -> x2, other arithmetic: none -> 4.34 us  [add(): return keep + sum((part.astype(single) for part in got))]
  transfers between devices with their start and end apart: 24 -> 20, of which waited for: 11 -> 11; matrix products, arithmetic and copies ran while one was open for 0% -> 8% of each run, Pallas kernels for 16% -> 15%
where the time goes in v2:
time: 191 us; the launch traced here: 190 us
  starting transfers between devices  57.6 us (30%)
  waiting for transfers between devices  56.9 us (30%)
  Pallas kernels  36.6 us (19%)
  blocking collectives  20.2 us (11%)
  other arithmetic  14.5 us (8%)
  local copies, waits for them, and re-layouts  2.96 us (2%)
    pallas_call x7, Pallas kernels, call(): return lambda *operands: run(*operands, *after, *carry)  36.6 us
    all_to_all x3, waiting for transfers between devices, exchange(): lax.all_to_all(array, 'block', split_axis=0, concat_axis=0, tiled=True)  26.9 us
    all_to_all x1, blocking collectives, exchange(): lax.all_to_all(array, 'block', split_axis=0, concat_axis=0, tiled=True)  20.2 us
    ppermute x6, starting transfers between devices, end_moves(): lax.ppermute(s, 'dp', dp_perm(r + 1, 0, 0))  19.5 us
    all_to_all x3, starting transfers between devices, exchange(): lax.all_to_all(array, 'block', split_axis=0, concat_axis=0, tiled=True)  18.7 us
    ppermute x6, starting transfers between devices, line_step(): lax.ppermute(s, 'dp', dp_perm(0, r + 1, 0))  11.6 us
    ppermute x6, waiting for transfers between devices, line_step(): lax.ppermute(s, 'dp', dp_perm(0, r + 1, 0))  11.1 us
    all_to_all x2, waiting for transfers between devices, share(): lax.all_to_all(array, 'dp', split_axis=0, concat_axis=0, tiled=True, axis...  8.47 us
  transfers between devices with their start and end apart: 20, of which 11 were waited for; matrix products, arithmetic and copies ran while one was open for 8% of the time, Pallas kernels for 15%

profile of v2, /device:TPU:2, one launch (start us, length us, event | category | flops | bytes accessed | tf_op | source)
XLA Modules:
  0.0 189.7 jit_solution(2275533863841628715)
XLA Ops:
  0.7 0.6 pad_add_fusion.refs_0_
  1.3 6.1 %shard_map.101 = (bf16[8,2,2,64,256]{4,3,2,1,0:T(8,128)(2,1)}, bf16[8,2,6,64,256]{4,3,2,1,0:T(8,128)(2,1)}) custom-call(s32[3]{0:T(128)} %pad_add_fusion.refs_0_, bf16[1024,256]{1,0:T(8,128)(2,1)} %refs_3_.8, bf16[1024,256]{1,0:T(8,128)(2,1)} %refs_4_.3, bf16[8,128,512]{2,1,0:T(8,128)(2,1)} %refs_3_.9, bf16[8,512,128]{2,1,0:T(8,128)(2,1)} %refs_4_.2), custom_call_target="tpu_custom_call" | custom-call | tf_op jit(solution)/shard_map/pallas_call | solution.py:84
  7.4 20.2 %all_to_all.30.refs_1_ = bf16[8,2,2,64,256]{4,3,2,1,0:T(8,128)(2,1)} all-to-all(bf16[8,2,2,64,256]{4,3,2,1,0:T(8,128)(2,1)} %get-tuple-element.25), channel_id=1, replica_groups=mesh['dp'=32,'block'=8] {'block'}, dimensions={0} | all-to-all | bytes 2097152 | tf_op jit(solution)/shard_map/all_to_all | solution.py:291
  27.6 6.1 %all-to-all-start.2 = ((bf16[8,2,6,64,256]{4,3,2,1,0:T(8,128)(2,1)}), bf16[8,2,6,64,256]{4,3,2,1,0:T(8,128)(2,1)}, u32[]{:S(2)}, u32[]{:S(2)}) async-start(bf16[8,2,6,64,256]{4,3,2,1,0:T(8,128)(2,1)} %get-tuple-element.30), calls=%async_computation.2 | async-start | bytes 6291456 | tf_op jit(solution)/shard_map/all_to_all | solution.py:291
  33.7 6.6 %shard_map.102 = (bf16[8,2,8,16,256]{4,3,2,1,0:T(8,128)(2,1)}, bf16[4,4,2,2,16,512]{5,4,3,2,1,0:T(8,128)(2,1)}, bf16[4,4,2,2,16,512]{5,4,3,2,1,0:T(8,128)(2,1)}) custom-call(s32[3]{0:T(128)} %pad_add_fusion.refs_0_, bf16[8,2,2,64,256]{4,3,2,1,0:T(8,128)(2,1)} %all_to_all.30.refs_1_, bf16[8,512,512]{2,1,0:T(8,128)(2,1)} %refs_2_.5, bf16[8,512,512]{2,1,0:T(8,128)(2,1)} %refs_3_.7), custom_call_target="tpu_custom_call" | custom-call | tf_op jit(solution)/shard_map/pallas_call | solution.py:84
  40.3 1.3 fusion.22
  41.6 1.6 collective-permute-done
  43.2 0.4 fusion.6
  43.6 1.8 collective-permute-start.1
  45.4 2.9 %collective-permute-start.2 = (bf16[4,4,16,512]{3,2,1,0:T(8,128)(2,1)S(1)}, bf16[4,4,16,512]{3,2,1,0:T(8,128)(2,1)S(1)}, u32[]{:S(2)}, u32[]{:S(2)}) collective-permute-start(bf16[4,4,16,512]{3,2,1,0:T(8,128)(2,1)S(1)} %get-tuple-element.63), channel_id=1, source_target_pairs={{0,32},{8,40},{16,48},{24,56},{32,0},{40,8},{48,16},{56,24},{64,96... | collective-permute-start | bytes 786440 | tf_op jit(solution)/shard_map/ppermute | solution.py:281
  48.3 1.3 collective-permute-start.3
  49.7 3.8 %collective-permute-done.1 = bf16[4,4,16,512]{3,2,1,0:T(8,128)(2,1)S(1)} collective-permute-done((bf16[4,4,16,512]{3,2,1,0:T(8,128)(2,1)S(1)}, bf16[4,4,16,512]{3,2,1,0:T(8,128)(2,1)S(1)}, u32[]{:S(2)}, u32[]{:S(2)}) %collective-permute-start.1) | collective-permute-done | bytes 262176 | tf_op jit(solution)/shard_map/ppermute | solution.py:281
  53.5 6.8 %collective-permute-done.2 = bf16[4,4,16,512]{3,2,1,0:T(8,128)(2,1)S(1)} collective-permute-done((bf16[4,4,16,512]{3,2,1,0:T(8,128)(2,1)S(1)}, bf16[4,4,16,512]{3,2,1,0:T(8,128)(2,1)S(1)}, u32[]{:S(2)}, u32[]{:S(2)}) %collective-permute-start.2) | collective-permute-done | bytes 262176 | tf_op jit(solution)/shard_map/ppermute | solution.py:281
  60.3 0.8 fusion.20
  61.1 1.3 shard_map.103
  62.4 6.8 %all-to-all-done.2.refs_1_ = bf16[8,2,6,64,256]{4,3,2,1,0:T(8,128)(2,1)} async-done(((bf16[8,2,6,64,256]{4,3,2,1,0:T(8,128)(2,1)}), bf16[8,2,6,64,256]{4,3,2,1,0:T(8,128)(2,1)}, u32[]{:S(2)}, u32[]{:S(2)}) %all-to-all-start.2) | async-done | bytes 3145760 | tf_op jit(solution)/shard_map/all_to_all | solution.py:291
  69.1 5.9 %all-to-all-start.1 = ((bf16[8,2,8,16,256]{4,3,2,1,0:T(8,128)(2,1)}), bf16[8,2,8,16,256]{4,3,2,1,0:T(8,128)(2,1)}, u32[]{:S(2)}, u32[]{:S(2)}) async-start(bf16[8,2,8,16,256]{4,3,2,1,0:T(8,128)(2,1)} %get-tuple-element.29), calls=%async_computation.1 | async-start | bytes 2097152 | tf_op jit(solution)/shard_map/all_to_all | solution.py:291
  75.0 12.1 %shard_map.104 = (bf16[8,2,8,48,256]{4,3,2,1,0:T(8,128)(2,1)}, bf16[4,4,2,6,16,512]{5,4,3,2,1,0:T(8,128)(2,1)}, bf16[4,4,2,6,16,512]{5,4,3,2,1,0:T(8,128)(2,1)},...) custom-call(s32[3]{0:T(128)} %pad_add_fusion.refs_0_, ...), custom_call_target="tpu_custom_call", output_to_operand_aliasing={{3}: (4, {}), {4}: (5, {}), {5}: (6, {}), {6}: (7, {})} | custom-call | tf_op jit(solution)/shard_map/pallas_call | solution.py:84
  87.2 0.4 all-to-all-done.1.refs_1_
  87.5 6.7 %all-to-all-start.3 = ((bf16[8,2,8,48,256]{4,3,2,1,0:T(8,128)(2,1)}), bf16[8,2,8,48,256]{4,3,2,1,0:T(8,128)(2,1)}, u32[]{:S(2)}, u32[]{:S(2)}) async-start(bf16[8,2,8,48,256]{4,3,2,1,0:T(8,128)(2,1)} %get-tuple-element.31), calls=%async_computation.3 | async-start | bytes 6291456 | tf_op jit(solution)/shard_map/all_to_all | solution.py:291
  94.6 5.5 %collective-permute-done.8 = bf16[4,4,12,16,512]{4,3,2,1,0:T(8,128)(2,1)S(1)} collective-permute-done((bf16[4,4,12,16,512]{4,3,2,1,0:T(8,128)(2,1)}, bf16[4,4,12,16,512]{4,3,2,1,0:T(8,128)(2,1)S(1)}, u32[]{:S(2)}, u32[]{:S(2)}) %collective-permute-start.8) | collective-permute-done | bytes 3145760 | tf_op jit(solution)/shard_map/ppermute | solution.py:256
  100.1 2.9 %fusion.3 = (bf16[4,12,16,512]{3,2,1,0:T(8,128)(2,1)S(1)}, bf16[4,12,16,512]{3,2,1,0:T(8,128)(2,1)}, bf16[4,12,16,512]{3,2,1,0:T(8,128)(2,1)}, f32[4,12,16,512]{3,2,1,0:T(8,128)}) fusion(bf16[4,12,16,512]{3,2,1,0:T(8,128)(2,1)S(1)} %bitcast.81, bf16[4,4,12,16,512]{4,3,2,1,0:T(8,128)(2,1)S(1)} %collective-permute-done.8, ...), kind=kLoop, calls=%fused_computation.7 | loop fusion | flops 5898240 | bytes 10223616 | tf_op jit(solution)/shard_map/convert_element_type | solution.py:258
  102.9 3.5 %collective-permute-start.10 = (bf16[4,12,16,512]{3,2,1,0:T(8,128)(2,1)}, bf16[4,12,16,512]{3,2,1,0:T(8,128)(2,1)}, u32[]{:S(2)}, u32[]{:S(2)}) collective-permute-start(bf16[4,12,16,512]{3,2,1,0:T(8,128)(2,1)} %get-tuple-element.51), channel_id=1, source_target_pairs={{0,32},{8,40},{16,48},{24,56},{32,0},{40,8},{48,16},{56,24},{64,96... | collective-permute-start | bytes 2359304 | tf_op jit(solution)/shard_map/ppermute | solution.py:281
  106.5 1.0 collective-permute-start.11
  107.5 1.0 collective-permute-start.9
  108.5 19.7 %all-to-all-done.3.refs_2_ = bf16[8,2,8,48,256]{4,3,2,1,0:T(8,128)(2,1)} async-done(((bf16[8,2,8,48,256]{4,3,2,1,0:T(8,128)(2,1)}), bf16[8,2,8,48,256]{4,3,2,1,0:T(8,128)(2,1)}, u32[]{:S(2)}, u32[]{:S(2)}) %all-to-all-start.3) | async-done | bytes 3145760 | tf_op jit(solution)/shard_map/all_to_all | solution.py:291
  128.3 4.9 %shard_map.105 = (bf16[4,4,2,2,16,512]{5,4,3,2,1,0:T(8,128)(2,1)}, bf16[4,4,2,2,16,512]{5,4,3,2,1,0:T(8,128)(2,1)}) custom-call(s32[3]{0:T(128)} %pad_add_fusion.refs_0_, bf16[8,2,8,16,256]{4,3,2,1,0:T(8,128)(2,1)} %all-to-all-done.1.refs_1_, bf16[8,2,8,48,256]{4,3,2,1,0:T(8,128)(2,1)} %all-to-all-done.3.refs_2_, bf16[1024,256]{1,0:T(8,128)(2,1)} %refs_3_.8, ...), custom_call_target="tpu_custom_call" | custom-call | tf_op jit(solution)/shard_map/pallas_call | solution.py:84
  133.2 3.7 %collective-permute-start.4 = (bf16[4,16,512]{2,1,0:T(8,128)(2,1)S(1)}, bf16[4,16,512]{2,1,0:T(8,128)(2,1)S(1)}, u32[]{:S(2)}, u32[]{:S(2)}) collective-permute-start(bf16[4,16,512]{2,1,0:T(8,128)(2,1)S(1)} %copy-done.9), channel_id=1, source_target_pairs={{0,64},{8,72},{16,80},{24,88},{32,96},{40,104},{48,112},{56,120},{... | collective-permute-start | bytes 196616 | tf_op jit(solution)/shard_map/ppermute | solution.py:287
  136.9 4.5 %collective-permute-start.5 = (bf16[4,16,512]{2,1,0:T(8,128)(2,1)S(1)}, bf16[4,16,512]{2,1,0:T(8,128)(2,1)S(1)}, u32[]{:S(2)}, u32[]{:S(2)}) collective-permute-start(bf16[4,16,512]{2,1,0:T(8,128)(2,1)S(1)} %copy-done.8), channel_id=1, source_target_pairs={{0,128},{8,136},{16,144},{24,152},{32,160},{40,168},{48,176},{56,1... | collective-permute-start | bytes 196616 | tf_op jit(solution)/shard_map/ppermute | solution.py:287
  141.4 0.5 collective-permute-done.11
  141.9 5.4 %collective-permute-start.6 = (bf16[4,16,512]{2,1,0:T(8,128)(2,1)S(1)}, bf16[4,16,512]{2,1,0:T(8,128)(2,1)S(1)}, u32[]{:S(2)}, u32[]{:S(2)}) collective-permute-start(bf16[4,16,512]{2,1,0:T(8,128)(2,1)S(1)} %copy-done.7), channel_id=1, source_target_pairs={{0,192},{8,200},{16,208},{24,216},{32,224},{40,232},{48,240},{56,2... | collective-permute-start | bytes 196616 | tf_op jit(solution)/shard_map/ppermute | solution.py:287
  147.3 3.5 %fusion.13 = (bf16[12,16,512]{2,1,0:T(8,128)(2,1)}, bf16[12,16,512]{2,1,0:T(8,128)(2,1)}, bf16[12,16,512]{2,1,0:T(8,128)(2,1)}, f32[12,16,512]{2,1,0:T(8,128)}) fusion(f32[4,12,16,512]{3,2,1,0:T(8,128)} %get-tuple-element.52, bf16[4,12,16,512]{3,2,1,0:T(8,128)(2,1)} %collective-permute-done.11, bf16[4,12,16,512]{3,2,1,0:T(8,128)(2,1)} %collective-permute-done.10, ...), kind=kLoop, calls=%fused_computation.38 | loop fusion | flops 2654208 | bytes 4915200 | tf_op jit(solution)/shard_map/add | solution.py:277
  150.9 1.4 fusion.refs_4_
  152.3 0.6 copy-done.10
  153.0 1.4 shard_map.106
  154.4 4.4 %all-to-all-start.4 = ((bf16[4,4,4,16,512]{4,3,2,1,0:T(8,128)(2,1)}), bf16[4,4,4,16,512]{4,3,2,1,0:T(8,128)(2,1)}, u32[]{:S(2)}, u32[]{:S(2)}) async-start(bf16[4,4,4,16,512]{4,3,2,1,0:T(8,128)(2,1)} %get-tuple-element.39.refs_4_), calls=%async_computation.4 | async-start | bytes 2097152 | tf_op jit(solution)/shard_map/all_to_all | solution.py:305
  158.9 4.7 %collective-permute-start.13 = (bf16[12,16,512]{2,1,0:T(8,128)(2,1)S(1)}, bf16[12,16,512]{2,1,0:T(8,128)(2,1)}, u32[]{:S(2)}, u32[]{:S(2)}) collective-permute-start(bf16[12,16,512]{2,1,0:T(8,128)(2,1)S(1)} %copy-done.5), channel_id=1, source_target_pairs={{0,128},{8,136},{16,144},{24,152},{32,160},{40,168},{48,176},{56,1... | collective-permute-start | bytes 589832 | tf_op jit(solution)/shard_map/ppermute | solution.py:287
  163.7 1.1 collective-permute-start.14
  164.8 4.2 %shard_map.107 = bf16[1024,256]{1,0:T(8,128)(2,1)} custom-call(s32[3]{0:T(128)} %pad_add_fusion.refs_0_, bf16[8,2,8,16,256]{4,3,2,1,0:T(8,128)(2,1)} %all-to-all-done.1.refs_1_, bf16[8,2,8,48,256]{4,3,2,1,0:T(8,128)(2,1)} %all-to-all-done.3.refs_2_, bf16[8,128,512]{2,1,0:T(8,128)(2,1)} %refs_3_.9, bf16[4,4,4,16,512]{4,3,2,1,0:T(8,128)(2,1)} %get-tuple-element.39.refs_4_), custom_call_target="tpu_custom_call" | custom-call | tf_op jit(solution)/shard_map/pallas_call | solution.py:84
  168.9 4.5 %all-to-all-done.4 = bf16[4,4,4,16,512]{4,3,2,1,0:T(8,128)(2,1)} async-done(((bf16[4,4,4,16,512]{4,3,2,1,0:T(8,128)(2,1)}), bf16[4,4,4,16,512]{4,3,2,1,0:T(8,128)(2,1)}, u32[]{:S(2)}, u32[]{:S(2)}) %all-to-all-start.4) | async-done | bytes 1048608 | tf_op jit(solution)/shard_map/all_to_all | solution.py:305
  173.5 2.2 %reduce_sum.21 = bf16[4,4,16,512]{3,2,1,0:T(8,128)(2,1)} reduce(bf16[4,4,4,16,512]{4,3,2,1,0:T(8,128)(2,1)} %all-to-all-done.4, bf16[]{:T(256)} %constant.54.clone.1), dimensions={0}, to_apply=%region_0.1 | reduce | flops 393216 | bytes 1310722 | tf_op jit(solution)/shard_map/reduce_sum | solution.py:308
  175.7 3.4 %all-to-all-start.5 = ((bf16[4,4,16,512]{3,2,1,0:T(8,128)(2,1)}), bf16[4,4,16,512]{3,2,1,0:T(8,128)(2,1)S(1)}, u32[]{:S(2)}, u32[]{:S(2)}) async-start(bf16[4,4,16,512]{3,2,1,0:T(8,128)(2,1)} %reduce_sum.21), calls=%async_computation.5 | async-start | bytes 524288 | tf_op jit(solution)/shard_map/all_to_all | solution.py:305
  179.1 3.3 %collective-permute-done.14 = bf16[12,16,512]{2,1,0:T(8,128)(2,1)} collective-permute-done((bf16[12,16,512]{2,1,0:T(8,128)(2,1)S(1)}, bf16[12,16,512]{2,1,0:T(8,128)(2,1)}, u32[]{:S(2)}, u32[]{:S(2)}) %collective-permute-start.14) | collective-permute-done | bytes 196640 | tf_op jit(solution)/shard_map/ppermute | solution.py:287
  182.4 1.1 add_multiply_fusion
  183.6 0.8 pad_maximum_fusion
  184.4 3.9 %all-to-all-done.5 = bf16[4,4,16,512]{3,2,1,0:T(8,128)(2,1)S(1)} async-done(((bf16[4,4,16,512]{3,2,1,0:T(8,128)(2,1)}), bf16[4,4,16,512]{3,2,1,0:T(8,128)(2,1)S(1)}, u32[]{:S(2)}, u32[]{:S(2)}) %all-to-all-start.5) | async-done | bytes 262176 | tf_op jit(solution)/shard_map/all_to_all | solution.py:305
  188.5 0.7 reshape_squeeze.4
  189.1 0.6 pad_maximum_fusion.2
  (52 shorter events, 0.7 us)
Async XLA Ops:
  27.6 41.5 %all-to-all-start.2 = ((bf16[8,2,6,64,256]{4,3,2,1,0:T(8,128)(2,1)}), bf16[8,2,6,64,256]{4,3,2,1,0:T(8,128)(2,1)}, u32[]{:S(2)}, u32[]{:S(2)}) async-start(bf16[8,2,6,64,256]{4,3,2,1,0:T(8,128)(2,1)} %get-tuple-element.30), calls=%async_computation.2 | async-start | bytes 6291456 | tf_op jit(solution)/shard_map/all_to_all | solution.py:291
  40.3 2.9 %collective-permute-start = (bf16[4,4,4,16,512]{4,3,2,1,0:T(8,128)(2,1)}, bf16[4,4,4,16,512]{4,3,2,1,0:T(8,128)(2,1)S(1)}, u32[]{:S(2)}, u32[]{:S(2)}) collective-permute-start(bf16[4,4,4,16,512]{4,3,2,1,0:T(8,128)(2,1)} %bitcast.93), channel_id=1, source_target_pairs={{0,8},{8,0},{16,24},{24,16},{32,40},{40,32},{48,56},{56,48},{64,72... | collective-permute-start | bytes 3145736 | tf_op jit(solution)/shard_map/ppermute | solution.py:256
  43.6 9.8 %collective-permute-start.1 = (bf16[4,4,16,512]{3,2,1,0:T(8,128)(2,1)S(1)}, bf16[4,4,16,512]{3,2,1,0:T(8,128)(2,1)S(1)}, u32[]{:S(2)}, u32[]{:S(2)}) collective-permute-start(bf16[4,4,16,512]{3,2,1,0:T(8,128)(2,1)S(1)} %get-tuple-element.61), channel_id=1, source_target_pairs={{0,16},{8,24},{16,32},{24,40},{32,48},{40,56},{48,0},{56,8},{64,80... | collective-permute-start | bytes 786440 | tf_op jit(solution)/shard_map/ppermute | solution.py:281
  45.4 14.8 %collective-permute-start.2 = (bf16[4,4,16,512]{3,2,1,0:T(8,128)(2,1)S(1)}, bf16[4,4,16,512]{3,2,1,0:T(8,128)(2,1)S(1)}, u32[]{:S(2)}, u32[]{:S(2)}) collective-permute-start(bf16[4,4,16,512]{3,2,1,0:T(8,128)(2,1)S(1)} %get-tuple-element.63), channel_id=1, source_target_pairs={{0,32},{8,40},{16,48},{24,56},{32,0},{40,8},{48,16},{56,24},{64,96... | collective-permute-start | bytes 786440 | tf_op jit(solution)/shard_map/ppermute | solution.py:281
  48.3 11.9 %collective-permute-start.3 = (bf16[4,4,16,512]{3,2,1,0:T(8,128)(2,1)S(1)}, bf16[4,4,16,512]{3,2,1,0:T(8,128)(2,1)S(1)}, u32[]{:S(2)}, u32[]{:S(2)}) collective-permute-start(bf16[4,4,16,512]{3,2,1,0:T(8,128)(2,1)S(1)} %get-tuple-element.62), channel_id=1, source_target_pairs={{0,48},{8,56},{16,0},{24,8},{32,16},{40,24},{48,32},{56,40},{64,11... | collective-permute-start | bytes 786440 | tf_op jit(solution)/shard_map/ppermute | solution.py:281
  69.1 18.4 %all-to-all-start.1 = ((bf16[8,2,8,16,256]{4,3,2,1,0:T(8,128)(2,1)}), bf16[8,2,8,16,256]{4,3,2,1,0:T(8,128)(2,1)}, u32[]{:S(2)}, u32[]{:S(2)}) async-start(bf16[8,2,8,16,256]{4,3,2,1,0:T(8,128)(2,1)} %get-tuple-element.29), calls=%async_computation.1 | async-start | bytes 2097152 | tf_op jit(solution)/shard_map/all_to_all | solution.py:291
  87.5 6.7 %copy-start.1 = (bf16[4,4,2,6,16,512]{5,4,3,2,1,0:T(8,128)(2,1)S(1)}, bf16[4,4,2,6,16,512]{5,4,3,2,1,0:T(8,128)(2,1)}, u32[]{:S(2)}) copy-start(bf16[4,4,2,6,16,512]{5,4,3,2,1,0:T(8,128)(2,1)} %get-tuple-element.37) | copy-start | bytes 9437188
  87.5 40.7 %all-to-all-start.3 = ((bf16[8,2,8,48,256]{4,3,2,1,0:T(8,128)(2,1)}), bf16[8,2,8,48,256]{4,3,2,1,0:T(8,128)(2,1)}, u32[]{:S(2)}, u32[]{:S(2)}) async-start(bf16[8,2,8,48,256]{4,3,2,1,0:T(8,128)(2,1)} %get-tuple-element.31), calls=%async_computation.3 | async-start | bytes 6291456 | tf_op jit(solution)/shard_map/all_to_all | solution.py:291
  94.2 5.9 %collective-permute-start.8 = (bf16[4,4,12,16,512]{4,3,2,1,0:T(8,128)(2,1)}, bf16[4,4,12,16,512]{4,3,2,1,0:T(8,128)(2,1)S(1)}, u32[]{:S(2)}, u32[]{:S(2)}) collective-permute-start(bf16[4,4,12,16,512]{4,3,2,1,0:T(8,128)(2,1)} %bitcast.91), channel_id=1, source_target_pairs={{0,8},{8,0},{16,24},{24,16},{32,40},{40,32},{48,56},{56,48},{64,72... | collective-permute-start | bytes 9437192 | tf_op jit(solution)/shard_map/ppermute | solution.py:256
  102.9 34.0 %collective-permute-start.10 = (bf16[4,12,16,512]{3,2,1,0:T(8,128)(2,1)}, bf16[4,12,16,512]{3,2,1,0:T(8,128)(2,1)}, u32[]{:S(2)}, u32[]{:S(2)}) collective-permute-start(bf16[4,12,16,512]{3,2,1,0:T(8,128)(2,1)} %get-tuple-element.51), channel_id=1, source_target_pairs={{0,32},{8,40},{16,48},{24,56},{32,0},{40,8},{48,16},{56,24},{64,96... | collective-permute-start | bytes 2359304 | tf_op jit(solution)/shard_map/ppermute | solution.py:281
  106.5 35.4 %collective-permute-start.11 = (bf16[4,12,16,512]{3,2,1,0:T(8,128)(2,1)}, bf16[4,12,16,512]{3,2,1,0:T(8,128)(2,1)}, u32[]{:S(2)}, u32[]{:S(2)}) collective-permute-start(bf16[4,12,16,512]{3,2,1,0:T(8,128)(2,1)} %get-tuple-element.50), channel_id=1, source_target_pairs={{0,48},{8,56},{16,0},{24,8},{32,16},{40,24},{48,32},{56,40},{64,11... | collective-permute-start | bytes 2359304 | tf_op jit(solution)/shard_map/ppermute | solution.py:281
  107.5 25.7 %copy-start.9 = (bf16[4,16,512]{2,1,0:T(8,128)(2,1)S(1)}, bf16[4,16,512]{2,1,0:T(8,128)(2,1)}, u32[]{:S(2)}) copy-start(bf16[4,16,512]{2,1,0:T(8,128)(2,1)} %get-tuple-element.32) | copy-start | bytes 196612
  107.5 29.4 %copy-start.8 = (bf16[4,16,512]{2,1,0:T(8,128)(2,1)S(1)}, bf16[4,16,512]{2,1,0:T(8,128)(2,1)}, u32[]{:S(2)}) copy-start(bf16[4,16,512]{2,1,0:T(8,128)(2,1)} %get-tuple-element.33) | copy-start | bytes 196612
  107.5 34.4 %copy-start.7 = (bf16[4,16,512]{2,1,0:T(8,128)(2,1)S(1)}, bf16[4,16,512]{2,1,0:T(8,128)(2,1)}, u32[]{:S(2)}) copy-start(bf16[4,16,512]{2,1,0:T(8,128)(2,1)} %get-tuple-element.34) | copy-start | bytes 196612
  107.5 39.8 %collective-permute-start.9 = (bf16[4,12,16,512]{3,2,1,0:T(8,128)(2,1)S(1)}, bf16[4,12,16,512]{3,2,1,0:T(8,128)(2,1)}, u32[]{:S(2)}, u32[]{:S(2)}) collective-permute-start(bf16[4,12,16,512]{3,2,1,0:T(8,128)(2,1)S(1)} %get-tuple-element.49), channel_id=1, source_target_pairs={{0,16},{8,24},{16,32},{24,40},{32,48},{40,56},{48,0},{56,8},{64,80... | collective-permute-start | bytes 2359304 | tf_op jit(solution)/shard_map/ppermute | solution.py:281
  133.2 17.7 %collective-permute-start.7 = (bf16[4,4,4,16,512]{4,3,2,1,0:T(8,128)(2,1)}, bf16[4,4,4,16,512]{4,3,2,1,0:T(8,128)(2,1)S(1)}, u32[]{:S(2)}, u32[]{:S(2)}) collective-permute-start(bf16[4,4,4,16,512]{4,3,2,1,0:T(8,128)(2,1)} %bitcast.92), channel_id=1, source_target_pairs={{0,8},{8,0},{16,24},{24,16},{32,40},{40,32},{48,56},{56,48},{64,72... | collective-permute-start | bytes 3145736 | tf_op jit(solution)/shard_map/ppermute | solution.py:328
  133.2 19.1 %collective-permute-start.4 = (bf16[4,16,512]{2,1,0:T(8,128)(2,1)S(1)}, bf16[4,16,512]{2,1,0:T(8,128)(2,1)S(1)}, u32[]{:S(2)}, u32[]{:S(2)}) collective-permute-start(bf16[4,16,512]{2,1,0:T(8,128)(2,1)S(1)} %copy-done.9), channel_id=1, source_target_pairs={{0,64},{8,72},{16,80},{24,88},{32,96},{40,104},{48,112},{56,120},{... | collective-permute-start | bytes 196616 | tf_op jit(solution)/shard_map/ppermute | solution.py:287
  136.9 15.4 %collective-permute-start.5 = (bf16[4,16,512]{2,1,0:T(8,128)(2,1)S(1)}, bf16[4,16,512]{2,1,0:T(8,128)(2,1)S(1)}, u32[]{:S(2)}, u32[]{:S(2)}) collective-permute-start(bf16[4,16,512]{2,1,0:T(8,128)(2,1)S(1)} %copy-done.8), channel_id=1, source_target_pairs={{0,128},{8,136},{16,144},{24,152},{32,160},{40,168},{48,176},{56,1... | collective-permute-start | bytes 196616 | tf_op jit(solution)/shard_map/ppermute | solution.py:287
  141.9 10.4 %collective-permute-start.6 = (bf16[4,16,512]{2,1,0:T(8,128)(2,1)S(1)}, bf16[4,16,512]{2,1,0:T(8,128)(2,1)S(1)}, u32[]{:S(2)}, u32[]{:S(2)}) collective-permute-start(bf16[4,16,512]{2,1,0:T(8,128)(2,1)S(1)} %copy-done.7), channel_id=1, source_target_pairs={{0,192},{8,200},{16,208},{24,216},{32,224},{40,232},{48,240},{56,2... | collective-permute-start | bytes 196616 | tf_op jit(solution)/shard_map/ppermute | solution.py:287
  147.3 3.5 %copy-start.3 = (bf16[4,4,2,2,16,512]{5,4,3,2,1,0:T(8,128)(2,1)S(1)}, bf16[4,4,2,2,16,512]{5,4,3,2,1,0:T(8,128)(2,1)}, u32[]{:S(2)}) copy-start(bf16[4,4,2,2,16,512]{5,4,3,2,1,0:T(8,128)(2,1)} %get-tuple-element.35) | copy-start | bytes 3145732
  152.3 0.6 copy-start.10
  152.3 0.6 copy-start.12
  152.3 0.6 copy-start.14
  153.0 5.8 %copy-start.2 = (f32[4,16,512]{2,1,0:T(8,128)S(1)}, f32[4,16,512]{2,1,0:T(8,128)}, u32[]{:S(2)}) copy-start(f32[4,16,512]{2,1,0:T(8,128)} %get-tuple-element.40) | copy-start | bytes 393220
  153.0 5.8 %copy-start.11 = (bf16[4,16,512]{2,1,0:T(8,128)(2,1)S(1)}, bf16[4,16,512]{2,1,0:T(8,128)(2,1)}, u32[]{:S(2)}) copy-start(bf16[4,16,512]{2,1,0:T(8,128)(2,1)} %copy-done.10) | copy-start | bytes 196612
  153.0 5.8 %copy-start.13 = (bf16[4,16,512]{2,1,0:T(8,128)(2,1)S(1)}, bf16[4,16,512]{2,1,0:T(8,128)(2,1)}, u32[]{:S(2)}) copy-start(bf16[4,16,512]{2,1,0:T(8,128)(2,1)} %copy-done.12) | copy-start | bytes 196612
  153.0 5.8 %copy-start.15 = (bf16[4,16,512]{2,1,0:T(8,128)(2,1)S(1)}, bf16[4,16,512]{2,1,0:T(8,128)(2,1)}, u32[]{:S(2)}) copy-start(bf16[4,16,512]{2,1,0:T(8,128)(2,1)} %copy-done.14) | copy-start | bytes 196612
  154.4 4.5 %copy-start.6 = (bf16[12,16,512]{2,1,0:T(8,128)(2,1)S(1)}, bf16[12,16,512]{2,1,0:T(8,128)(2,1)}, u32[]{:S(2)}) copy-start(bf16[12,16,512]{2,1,0:T(8,128)(2,1)} %get-tuple-element.42) | copy-start | bytes 589828
  154.4 4.6 %copy-start.5 = (bf16[12,16,512]{2,1,0:T(8,128)(2,1)S(1)}, bf16[12,16,512]{2,1,0:T(8,128)(2,1)}, u32[]{:S(2)}) copy-start(bf16[12,16,512]{2,1,0:T(8,128)(2,1)} %get-tuple-element.43) | copy-start | bytes 589828
  154.4 9.3 %copy-start.4 = (bf16[12,16,512]{2,1,0:T(8,128)(2,1)S(1)}, bf16[12,16,512]{2,1,0:T(8,128)(2,1)}, u32[]{:S(2)}) copy-start(bf16[12,16,512]{2,1,0:T(8,128)(2,1)} %get-tuple-element.44) | copy-start | bytes 589828
  154.4 19.1 %all-to-all-start.4 = ((bf16[4,4,4,16,512]{4,3,2,1,0:T(8,128)(2,1)}), bf16[4,4,4,16,512]{4,3,2,1,0:T(8,128)(2,1)}, u32[]{:S(2)}, u32[]{:S(2)}) async-start(bf16[4,4,4,16,512]{4,3,2,1,0:T(8,128)(2,1)} %get-tuple-element.39.refs_4_), calls=%async_computation.4 | async-start | bytes 2097152 | tf_op jit(solution)/shard_map/all_to_all | solution.py:305
  158.8 20.3 %collective-permute-start.12 = (bf16[12,16,512]{2,1,0:T(8,128)(2,1)S(1)}, bf16[12,16,512]{2,1,0:T(8,128)(2,1)S(1)}, u32[]{:S(2)}, u32[]{:S(2)}) collective-permute-start(bf16[12,16,512]{2,1,0:T(8,128)(2,1)S(1)} %copy-done.6), channel_id=1, source_target_pairs={{0,64},{8,72},{16,80},{24,88},{32,96},{40,104},{48,112},{56,120},{... | collective-permute-start | bytes 589832 | tf_op jit(solution)/shard_map/ppermute | solution.py:287
  158.9 20.2 %collective-permute-start.13 = (bf16[12,16,512]{2,1,0:T(8,128)(2,1)S(1)}, bf16[12,16,512]{2,1,0:T(8,128)(2,1)}, u32[]{:S(2)}, u32[]{:S(2)}) collective-permute-start(bf16[12,16,512]{2,1,0:T(8,128)(2,1)S(1)} %copy-done.5), channel_id=1, source_target_pairs={{0,128},{8,136},{16,144},{24,152},{32,160},{40,168},{48,176},{56,1... | collective-permute-start | bytes 589832 | tf_op jit(solution)/shard_map/ppermute | solution.py:287
  163.7 18.8 %collective-permute-start.14 = (bf16[12,16,512]{2,1,0:T(8,128)(2,1)S(1)}, bf16[12,16,512]{2,1,0:T(8,128)(2,1)}, u32[]{:S(2)}, u32[]{:S(2)}) collective-permute-start(bf16[12,16,512]{2,1,0:T(8,128)(2,1)S(1)} %copy-done.4), channel_id=1, source_target_pairs={{0,192},{8,200},{16,208},{24,216},{32,224},{40,232},{48,240},{56,2... | collective-permute-start | bytes 589832 | tf_op jit(solution)/shard_map/ppermute | solution.py:287
  168.9 13.5 %copy-start = (f32[12,16,512]{2,1,0:T(8,128)S(1)}, f32[12,16,512]{2,1,0:T(8,128)}, u32[]{:S(2)}) copy-start(f32[12,16,512]{2,1,0:T(8,128)} %get-tuple-element.41) | copy-start | bytes 1179652
  175.7 12.7 %all-to-all-start.5 = ((bf16[4,4,16,512]{3,2,1,0:T(8,128)(2,1)}), bf16[4,4,16,512]{3,2,1,0:T(8,128)(2,1)S(1)}, u32[]{:S(2)}, u32[]{:S(2)}) async-start(bf16[4,4,16,512]{3,2,1,0:T(8,128)(2,1)} %reduce_sum.21), calls=%async_computation.5 | async-start | bytes 524288 | tf_op jit(solution)/shard_map/all_to_all | solution.py:305

commit v3 on v2

--- a/solution.py
+++ b/solution.py
@@ -56,73 +56,77 @@
     return jnp.concatenate(parts, axis=1).astype(half)
 
 
+def position():
+    dp = lax.axis_index("dp")
+    return lax.rem(dp, CORES), lax.rem(lax.div(dp, CORES), Y), lax.div(dp, CORES * Y)
+
+
 def call(
-    kernel, grid, in_specs, out_specs, out_shape, scratch=(), after=(), carry=()
+    kernel, grid, in_specs, out_specs, out_shape, scratch=(), after=(), carry=(), vmem=VMEM_LIMIT
 ):
-    first = 1 + len(in_specs)
+    first = len(in_specs)
     extra = len(after) + len(carry)
     outs = len(out_specs)
     untouched = pl.BlockSpec(memory_space=pl.ANY)
 
     def body(*refs):
         ends = first + extra + outs
-        kernel(*refs[:first], *refs[first + extra : ends], *refs[ends + len(carry) :])
+        kernel(position(), *refs[:first], *refs[first + extra : ends], *refs[ends + len(carry) :])
 
     run = pl.pallas_call(
         body,
-        grid_spec=pltpu.PrefetchScalarGridSpec(
-            num_scalar_prefetch=1,
-            grid=grid,
-            in_specs=list(in_specs) + [untouched] * extra,
-            out_specs=list(out_specs) + [untouched] * len(carry),
-            scratch_shapes=list(scratch),
-        ),
+        grid=grid,
+        in_specs=list(in_specs) + [untouched] * extra,
+        out_specs=list(out_specs) + [untouched] * len(carry),
+        scratch_shapes=list(scratch),
         out_shape=list(out_shape) + [jax.ShapeDtypeStruct(c.shape, c.dtype) for c in carry],
         input_output_aliases={first + len(after) + i: outs + i for i in range(len(carry))},
-        compiler_params=pltpu.CompilerParams(vmem_limit_bytes=VMEM_LIMIT),
+        compiler_params=pltpu.CompilerParams(vmem_limit_bytes=vmem),
     )
     return lambda *operands: run(*operands, *after, *carry)
 
 
-def first_kernel(me, x_ref, g_ref, up_ref, down_ref, *out_refs):
-    ups, downs = [], []
-    for i in range(2):
-        rows = slice(i * BLK_IN, (i + 1) * BLK_IN)
-        ups.append(dot(up_ref[i], x_ref[rows], 0, 0))
-        downs.append(dot(down_ref[i], g_ref[rows], 1, 0))
-    for slot, pair in enumerate((ups, downs)):
-        spread = spread_pair(*pair).reshape(PEERS, LOCAL, PAIR, -1)
-        start = 0
-        for pairs, out in zip(CHUNKS, out_refs):
-            out[:, slot] = spread[:, start : start + 2 * pairs]
-            start += 2 * pairs
-
-
-def first_stage(me, inputs, grad_out, up_left, down_right):
+def first_kernel(chunk, x_ref, g_ref, up_ref, down_ref, out_ref):
+    start = 2 * sum(CHUNKS[:chunk])
+    for pair in range(2):
+        ups, downs = [], []
+        for i in (2 * pair, 2 * pair + 1):
+            rows = slice(i * BLK_IN, (i + 1) * BLK_IN)
+            ups.append(dot(up_ref[i], x_ref[rows], 0, 0))
+            downs.append(dot(down_ref[i], g_ref[rows], 1, 0))
+        where = slice(pair * PAIR, (pair + 1) * PAIR)
+        for slot, both in enumerate((ups, downs)):
+            spread = spread_pair(*both).reshape(PEERS, LOCAL, PAIR, -1)
+            out_ref[:, slot, :, where] = spread[:, start : start + 2 * CHUNKS[chunk]]
+
+
+def first_stage(chunk, inputs, grad_out, up_left, down_right, **order):
     tokens = inputs.shape[1]
-    return call(
-        first_kernel,
-        (PAIRS,),
+    n = CHUNKS[chunk]
+
+    def kernel(me, *refs):
+        first_kernel(chunk, *refs)
+
+    (out,) = call(
+        kernel,
+        (PAIRS // 2,),
         [
-            pl.BlockSpec((2 * BLK_IN, tokens), lambda p, me: (p, 0)),
-            pl.BlockSpec((2 * BLK_IN, tokens), lambda p, me: (p, 0)),
-            pl.BlockSpec((2, BLK_IN, BLK_HID), lambda p, me: (p, 0, 0)),
-            pl.BlockSpec((2, BLK_HID, BLK_IN), lambda p, me: (p, 0, 0)),
-        ],
-        [
-            pl.BlockSpec((PEERS, 2, 2 * n, PAIR, tokens), lambda p, me: (0, 0, 0, p, 0))
-            for n in CHUNKS
-        ],
-        [
-            jax.ShapeDtypeStruct((PEERS, 2, 2 * n, LOCAL * SPREAD, tokens), half) for n in CHUNKS
-        ],
-    )(me, inputs, grad_out, up_left, down_right)
+            pl.BlockSpec((4 * BLK_IN, tokens), lambda p: (p, 0)),
+            pl.BlockSpec((4 * BLK_IN, tokens), lambda p: (p, 0)),
+            pl.BlockSpec((4, BLK_IN, BLK_HID), lambda p: (p, 0, 0)),
+            pl.BlockSpec((4, BLK_HID, BLK_IN), lambda p: (p, 0, 0)),
+        ],
+        [pl.BlockSpec((PEERS, 2, 2 * n, 2 * PAIR, tokens), lambda p: (0, 0, 0, p, 0))],
+        [jax.ShapeDtypeStruct((PEERS, 2, 2 * n, LOCAL * SPREAD, tokens), half)],
+        **order,
+    )(inputs, grad_out, up_left, down_right)
+    return out
 
 
 def place(me, held, own_ref, other_ref, index):
     for ry in range(Y):
         for rz in range(Z):
-            group = ((me[2] + rz) % Z * Y + (me[1] + ry) % Y) * CORES
+            group = (lax.rem(me[2] + rz, Z) * Y + lax.rem(me[1] + ry, Y)) * CORES
             own_ref[(ry, rz) + index] = held[group + me[0]]
             other_ref[(ry, rz) + index] = held[group + 1 - me[0]]
 
@@ -146,23 +150,23 @@
     back_ref[:, 1] = spread_pair(*mids).reshape(PEERS, LOCAL, PAIR, -1)
 
 
-def middle_stage(me, chunk, got, up_right, down_left, **order):
+def middle_stage(chunk, got, up_right, down_left, **order):
     tokens = got.shape[-1]
     pairs = CHUNKS[chunk]
     start = sum(CHUNKS[:chunk])
     grads = jax.ShapeDtypeStruct((Y, Z, 2, 2 * pairs, ROWS, BLK_HID), half)
-    grads_spec = pl.BlockSpec((Y, Z, 2, 2, ROWS, BLK_HID), lambda p, me: (0, 0, 0, p, 0, 0))
-    weight = pl.BlockSpec((2, BLK_HID, BLK_HID), lambda p, me: (start + p, 0, 0))
+    grads_spec = pl.BlockSpec((Y, Z, 2, 2, ROWS, BLK_HID), lambda p: (0, 0, 0, p, 0, 0))
+    weight = pl.BlockSpec((2, BLK_HID, BLK_HID), lambda p: (start + p, 0, 0))
     return call(
         middle_kernel,
         (pairs,),
         [
-            pl.BlockSpec((PEERS, 2, 2, LOCAL * SPREAD, tokens), lambda p, me: (0, 0, p, 0, 0)),
+            pl.BlockSpec((PEERS, 2, 2, LOCAL * SPREAD, tokens), lambda p: (0, 0, p, 0, 0)),
             weight,
             weight,
         ],
         [
-            pl.BlockSpec((PEERS, 2, LOCAL, PAIR, tokens), lambda p, me: (0, 0, 0, p, 0)),
+            pl.BlockSpec((PEERS, 2, LOCAL, PAIR, tokens), lambda p: (0, 0, 0, p, 0)),
             grads_spec,
             grads_spec,
         ],
@@ -173,7 +177,7 @@
         ],
         scratch=[pltpu.VMEM((2, BLK_HID // ROWS, ROWS, BLK_HID), half)],
         **order,
-    )(me, got, up_right, down_left)
+    )(got, up_right, down_left)
 
 
 def features(one_ref, two_ref, slot, i):
@@ -194,27 +198,27 @@
         held_down[:, :, i * BLK_IN : (i + 1) * BLK_IN] = right.reshape(-1, ROWS, BLK_IN)
     for core, parts in enumerate((evens, odds)):
         held[core] = jnp.concatenate(parts, axis=1).astype(half)
-    for y in range(Y):
+    for ry in range(Y):
         for z in range(Z):
-            chip = z * Y + y
-            own_ref[y, z, 0, 0] = held[me[0], chip]
-            other_ref[y, z, 0, 0] = held[1 - me[0], chip]
-            own_ref[y, z, 1, 0] = held_down[chip * CORES + me[0]]
-            other_ref[y, z, 1, 0] = held_down[chip * CORES + 1 - me[0]]
+            chip = z * Y + lax.rem(me[1] + ry, Y)
+            own_ref[ry, z, 0, 0] = held[me[0], chip]
+            other_ref[ry, z, 0, 0] = held[1 - me[0], chip]
+            own_ref[ry, z, 1, 0] = held_down[chip * CORES + me[0]]
+            other_ref[ry, z, 1, 0] = held_down[chip * CORES + 1 - me[0]]
 
 
 def got_specs(tokens):
     return [
-        pl.BlockSpec((PEERS, 2, 4, n * PAIR, tokens), lambda p, me: (0, 0, p, 0, 0)) for n in CHUNKS
+        pl.BlockSpec((PEERS, 2, 4, n * PAIR, tokens), lambda p: (0, 0, p, 0, 0)) for n in CHUNKS
     ]
 
 
-def outer_stage(me, one, two, inputs, grad_out, **order):
+def outer_stage(one, two, inputs, grad_out, **order):
     tokens = inputs.shape[1]
     groups = LOCAL // 4
     grads = jax.ShapeDtypeStruct((Y, Z, 2, groups, ROWS, BLK_HID), half)
-    grads_spec = pl.BlockSpec((Y, Z, 2, 1, ROWS, BLK_HID), lambda p, me: (0, 0, 0, p, 0, 0))
-    feats = pl.BlockSpec((4 * BLK_IN, tokens), lambda p, me: (p, 0))
+    grads_spec = pl.BlockSpec((Y, Z, 2, 1, ROWS, BLK_HID), lambda p: (0, 0, 0, p, 0, 0))
+    feats = pl.BlockSpec((4 * BLK_IN, tokens), lambda p: (p, 0))
     return call(
         outer_kernel,
         (groups,),
@@ -226,7 +230,7 @@
             pltpu.VMEM((Z * Y * CORES, ROWS, BLK_HID), half),
         ],
         **order,
-    )(me, one, two, inputs, grad_out)
+    )(one, two, inputs, grad_out)
 
 
 def back_kernel(me, one_ref, two_ref, up_ref, in_ref):
@@ -235,16 +239,16 @@
         in_ref[rows] = dot(up_ref[i], features(one_ref, two_ref, 1, i), 1, 0).astype(half)
 
 
-def back_stage(me, one, two, up_left, **order):
+def back_stage(one, two, up_left, **order):
     tokens = one.shape[-1]
     return call(
         back_kernel,
         (LOCAL // 4,),
-        got_specs(tokens) + [pl.BlockSpec((4, BLK_IN, BLK_HID), lambda p, me: (p, 0, 0))],
-        [pl.BlockSpec((4 * BLK_IN, tokens), lambda p, me: (p, 0))],
+        got_specs(tokens) + [pl.BlockSpec((4, BLK_IN, BLK_HID), lambda p: (p, 0, 0))],
+        [pl.BlockSpec((4 * BLK_IN, tokens), lambda p: (p, 0))],
         [jax.ShapeDtypeStruct((LOCAL * BLK_IN, tokens), half)],
         **order,
-    )(me, one, two, up_left)
+    )(one, two, up_left)
 
 
 def flat(array):
@@ -258,7 +262,7 @@
     return sums[0], *[total.astype(half) for total in sums[1:]]
 
 
-def gate(me, arrays, after=()):
+def gate(arrays, after=()):
     def kernel(me, out_ref):
         out_ref[...] = jnp.zeros_like(out_ref)
 
@@ -266,11 +270,12 @@
         kernel,
         (1,),
         [],
-        [pl.BlockSpec((8, 128), lambda p, me: (0, 0))],
+        [pl.BlockSpec((8, 128), lambda p: (0, 0))],
         [jax.ShapeDtypeStruct((8, 128), single)],
         after=after,
         carry=arrays,
-    )(me)[1:]
+        vmem=1 << 20,
+    )()[1:]
 
 
 def add(keep, got):
@@ -311,31 +316,34 @@
 def shards(inputs, grad_out, up_left, up_right, down_left, down_right):
     tokens = inputs.shape[1]
     factor = float(tokens * lax.axis_size("dp")) ** (-0.5)
-    dp = lax.axis_index("dp")
-    me = jnp.stack([dp % CORES, dp // CORES % Y, dp // (CORES * Y)]).astype(jnp.int32)
-
-    one, two = first_stage(me, inputs, grad_out, up_left, down_right)
-    back1, own, other = middle_stage(me, 0, exchange(one), up_right, down_left)
+
+    operands = (inputs, grad_out, up_left, down_right)
+    one = first_stage(0, *operands)
+    two = first_stage(1, *operands, after=(one,))
+    back1, own, other = middle_stage(0, exchange(one), up_right, down_left)
     sums1 = line_step(*core_step(own, other))
-    (back1,) = gate(me, [back1], sums1)
+    (back1,) = gate([back1], sums1)
     back2, own, other, *sums1 = middle_stage(
-        me, 1, exchange(two), up_right, down_left, carry=sums1
+        1, exchange(two), up_right, down_left, carry=sums1
     )
     sums2 = core_step(own, other)
     back1, back2 = exchange(back1), exchange(back2)
-    own, other = outer_stage(me, back1, back2, inputs, grad_out)
-    outer = flat(own).astype(single)
-    outer = outer + lax.ppermute(flat(other), "dp", dp_perm(0, 0, 1)).astype(single)
-    sums2 = line_step(*sums2)
     got1 = end_moves(*sums1)
-    outer, *sums2 = gate(me, [outer.astype(half), *sums2], got1)
+    own, other = outer_stage(back1, back2, inputs, grad_out, after=got1[::2])
+    keep, *sends = core_step(own, other)
+    gated = gate([*sends, *line_step(*sums2)], got1[1:2])
+    sends, sums2 = gated[: len(sends)], gated[len(sends) :]
+    outer = add(keep, [lax.ppermute(s, "dp", dp_perm(0, r + 1, 0)) for r, s in enumerate(sends)])
     got2 = end_moves(*sums2)
-    (grad_in,) = back_stage(me, back1, back2, up_left, after=(outer,))
-    outer = share(share(outer, True).astype(half), False) * factor
+    outer = outer.astype(half)
+    grad_in, keep1, keep2 = back_stage(
+        back1, back2, up_left, after=(outer,), carry=(sums1[0], sums2[0])
+    )
+    outer = share(outer, False) * factor
     outer = outer.reshape(2, -1, ROWS, BLK_HID)
     grads = [
-        (factor * add(sums[0], got)).reshape(2, -1, ROWS, BLK_HID)
-        for sums, got in ((sums1, got1), (sums2, got2))
+        (factor * add(keep, got)).reshape(2, -1, ROWS, BLK_HID)
+        for keep, got in ((keep1, got1), (keep2, got2))
     ]
     grad_left_down, grad_right_up = [
         jnp.concatenate([g[k] for g in grads], axis=0) for k in range(2)

time: 191 us -> 185 us (0.969); the launches traced: 190 us -> 181 us
  blocking collectives: 20.2 us -> 0 us
  waiting for transfers between devices: 56.9 us -> 71.2 us
  Pallas kernels: 36.6 us -> 34.1 us
    ppermute x6, waiting for transfers between devices: 3.32 us -> 30.9 us  [end_moves(): lax.ppermute(s, 'dp', dp_perm(r + 1, 0, 0))]
    all_to_all x1 -> x0, blocking collectives: 20.2 us -> none  [exchange(): lax.all_to_all(array, 'block', split_axis=0, concat_axis=0, tiled=True)]
    all_to_all x2 -> x1, waiting for transfers between devices: 8.47 us -> 0.01 us  [share(): lax.all_to_all(array, 'dp', split_axis=0, concat_axis=0, tiled=True, axis...]
    all_to_all x3 -> x4, waiting for transfers between devices: 26.9 us -> 18.5 us  [exchange(): lax.all_to_all(array, 'block', split_axis=0, concat_axis=0, tiled=True)]
    ppermute x6, starting transfers between devices: 19.5 us -> 12.6 us  [end_moves(): lax.ppermute(s, 'dp', dp_perm(r + 1, 0, 0))]
    all_to_all x3 -> x4, starting transfers between devices: 18.7 us -> 25.5 us  [exchange(): lax.all_to_all(array, 'block', split_axis=0, concat_axis=0, tiled=True)]
    ppermute x1 -> x3, starting transfers between devices: 0.01 us -> 5.71 us  [shards(): lax.ppermute(s, 'dp', dp_perm(0, r + 1, 0))]
    all_to_all x2 -> x1, starting transfers between devices: 7.78 us -> 4.33 us  [share(): lax.all_to_all(array, 'dp', split_axis=0, concat_axis=0, tiled=True, axis...]
  transfers between devices with their start and end apart: 20 -> 23, of which waited for: 11 -> 12; matrix products, arithmetic and copies ran while one was open for 8% -> 7% of each run, Pallas kernels for 15% -> 16%
where the time goes in v3:
time: 185 us; the launch traced here: 181 us
  waiting for transfers between devices  71.2 us (38%)
  starting transfers between devices  59.5 us (32%)
  Pallas kernels  34.1 us (18%)
  other arithmetic  12.8 us (7%)
  local copies, waits for them, and re-layouts  3.06 us (2%)
    pallas_call x8, Pallas kernels, call(): return lambda *operands: run(*operands, *after, *carry)  34.1 us
    ppermute x6, waiting for transfers between devices, end_moves(): lax.ppermute(s, 'dp', dp_perm(r + 1, 0, 0))  30.9 us
    all_to_all x4, starting transfers between devices, exchange(): lax.all_to_all(array, 'block', split_axis=0, concat_axis=0, tiled=True)  25.5 us
    all_to_all x4, waiting for transfers between devices, exchange(): lax.all_to_all(array, 'block', split_axis=0, concat_axis=0, tiled=True)  18.5 us
    ppermute x6, starting transfers between devices, end_moves(): lax.ppermute(s, 'dp', dp_perm(r + 1, 0, 0))  12.6 us
    ppermute x6, starting transfers between devices, line_step(): lax.ppermute(s, 'dp', dp_perm(0, r + 1, 0))  11.4 us
    ppermute x6, waiting for transfers between devices, line_step(): lax.ppermute(s, 'dp', dp_perm(0, r + 1, 0))  11.4 us
    ppermute x3, waiting for transfers between devices, core_step(): got = lax.ppermute(flat(other), 'dp', dp_perm(0, 0, 1))  7.14 us
  transfers between devices with their start and end apart: 23, of which 12 were waited for; matrix products, arithmetic and copies ran while one was open for 7% of the time, Pallas kernels for 16%

profile of v3, /device:TPU:2, one launch (start us, length us, event | category | flops | bytes accessed | tf_op | source)
XLA Modules:
  0.0 181.4 jit_solution(17794919015750124952)
XLA Ops:
  0.6 3.7 %shard_map.101.refs_4_ = bf16[8,2,2,64,256]{4,3,2,1,0:T(8,128)(2,1)} custom-call(bf16[1024,256]{1,0:T(8,128)(2,1)} %refs_2_.10, bf16[1024,256]{1,0:T(8,128)(2,1)} %refs_3_.5, bf16[8,128,512]{2,1,0:T(8,128)(2,1)} %refs_2_.11, bf16[8,512,128]{2,1,0:T(8,128)(2,1)} %refs_3_.4), custom_call_target="tpu_custom_call" | custom-call | tf_op jit(solution)/shard_map/pallas_call | solution.py:86
  4.3 6.4 %all-to-all-start = ((bf16[8,2,2,64,256]{4,3,2,1,0:T(8,128)(2,1)}), bf16[8,2,2,64,256]{4,3,2,1,0:T(8,128)(2,1)}, u32[]{:S(2)}, u32[]{:S(2)}) async-start(bf16[8,2,2,64,256]{4,3,2,1,0:T(8,128)(2,1)} %shard_map.101.refs_4_), calls=%async_computation | async-start | bytes 2097152 | tf_op jit(solution)/shard_map/all_to_all | solution.py:296
  10.7 4.0 %shard_map.104 = bf16[8,2,6,64,256]{4,3,2,1,0:T(8,128)(2,1)} custom-call(bf16[1024,256]{1,0:T(8,128)(2,1)} %refs_2_.10, bf16[1024,256]{1,0:T(8,128)(2,1)} %refs_3_.5, bf16[8,128,512]{2,1,0:T(8,128)(2,1)} %refs_2_.11, bf16[8,512,128]{2,1,0:T(8,128)(2,1)} %refs_3_.4, bf16[8,2,2,64,256]{4,3,2,1,0:T(8,128)(2,1)} %shard_map.101.refs_4_), custom_call_target="tpu_custom_call" | custom-call | tf_op jit(solution)/shard_map/pallas_call | solution.py:86
  14.8 9.5 %all-to-all-done.refs_0_ = bf16[8,2,2,64,256]{4,3,2,1,0:T(8,128)(2,1)} async-done(((bf16[8,2,2,64,256]{4,3,2,1,0:T(8,128)(2,1)}), bf16[8,2,2,64,256]{4,3,2,1,0:T(8,128)(2,1)}, u32[]{:S(2)}, u32[]{:S(2)}) %all-to-all-start) | async-done | bytes 1048608 | tf_op jit(solution)/shard_map/all_to_all | solution.py:296
  24.2 6.4 %all-to-all-start.2 = ((bf16[8,2,6,64,256]{4,3,2,1,0:T(8,128)(2,1)}), bf16[8,2,6,64,256]{4,3,2,1,0:T(8,128)(2,1)}, u32[]{:S(2)}, u32[]{:S(2)}) async-start(bf16[8,2,6,64,256]{4,3,2,1,0:T(8,128)(2,1)} %shard_map.104), calls=%async_computation.2 | async-start | bytes 6291456 | tf_op jit(solution)/shard_map/all_to_all | solution.py:296
  30.6 5.8 %shard_map.102 = (bf16[8,2,8,16,256]{4,3,2,1,0:T(8,128)(2,1)}, bf16[4,4,2,2,16,512]{5,4,3,2,1,0:T(8,128)(2,1)}, bf16[4,4,2,2,16,512]{5,4,3,2,1,0:T(8,128)(2,1)}) custom-call(bf16[8,2,2,64,256]{4,3,2,1,0:T(8,128)(2,1)} %all-to-all-done.refs_0_, bf16[8,512,512]{2,1,0:T(8,128)(2,1)} %refs_1_.7, bf16[8,512,512]{2,1,0:T(8,128)(2,1)} %refs_2_.9), custom_call_target="tpu_custom_call" | custom-call | tf_op jit(solution)/shard_map/pallas_call | solution.py:86
  36.5 1.3 fusion.27
  37.7 1.6 collective-permute-done
  39.7 1.7 collective-permute-start.1
  41.4 2.9 %collective-permute-start.2 = (bf16[4,4,16,512]{3,2,1,0:T(8,128)(2,1)S(1)}, bf16[4,4,16,512]{3,2,1,0:T(8,128)(2,1)S(1)}, u32[]{:S(2)}, u32[]{:S(2)}) collective-permute-start(bf16[4,4,16,512]{3,2,1,0:T(8,128)(2,1)S(1)} %get-tuple-element.76), channel_id=1, source_target_pairs={{0,32},{8,40},{16,48},{24,56},{32,0},{40,8},{48,16},{56,24},{64,96... | collective-permute-start | bytes 786440 | tf_op jit(solution)/shard_map/ppermute | solution.py:286
  44.3 1.3 collective-permute-start.3
  45.6 3.8 %collective-permute-done.1 = bf16[4,4,16,512]{3,2,1,0:T(8,128)(2,1)S(1)} collective-permute-done((bf16[4,4,16,512]{3,2,1,0:T(8,128)(2,1)S(1)}, bf16[4,4,16,512]{3,2,1,0:T(8,128)(2,1)S(1)}, u32[]{:S(2)}, u32[]{:S(2)}) %collective-permute-start.1) | collective-permute-done | bytes 262176 | tf_op jit(solution)/shard_map/ppermute | solution.py:286
  49.4 6.8 %collective-permute-done.2 = bf16[4,4,16,512]{3,2,1,0:T(8,128)(2,1)S(1)} collective-permute-done((bf16[4,4,16,512]{3,2,1,0:T(8,128)(2,1)S(1)}, bf16[4,4,16,512]{3,2,1,0:T(8,128)(2,1)S(1)}, u32[]{:S(2)}, u32[]{:S(2)}) %collective-permute-start.2) | collective-permute-done | bytes 262176 | tf_op jit(solution)/shard_map/ppermute | solution.py:286
  56.2 0.8 fusion.24
  57.7 8.0 %all-to-all-done.2.refs_0_ = bf16[8,2,6,64,256]{4,3,2,1,0:T(8,128)(2,1)} async-done(((bf16[8,2,6,64,256]{4,3,2,1,0:T(8,128)(2,1)}), bf16[8,2,6,64,256]{4,3,2,1,0:T(8,128)(2,1)}, u32[]{:S(2)}, u32[]{:S(2)}) %all-to-all-start.2) | async-done | bytes 3145760 | tf_op jit(solution)/shard_map/all_to_all | solution.py:296
  65.7 5.9 %all-to-all-start.1 = ((bf16[8,2,8,16,256]{4,3,2,1,0:T(8,128)(2,1)}), bf16[8,2,8,16,256]{4,3,2,1,0:T(8,128)(2,1)}, u32[]{:S(2)}, u32[]{:S(2)}) async-start(bf16[8,2,8,16,256]{4,3,2,1,0:T(8,128)(2,1)} %get-tuple-element.31), calls=%async_computation.1 | async-start | bytes 2097152 | tf_op jit(solution)/shard_map/all_to_all | solution.py:296
  71.7 11.5 %shard_map.105 = (bf16[8,2,8,48,256]{4,3,2,1,0:T(8,128)(2,1)}, bf16[4,4,2,6,16,512]{5,4,3,2,1,0:T(8,128)(2,1)}, bf16[4,4,2,6,16,512]{5,4,3,2,1,0:T(8,128)(2,1)},...) custom-call(bf16[8,2,6,64,256]{4,3,2,1,0:T(8,128)(2,1)} %all-to-all-, ...), custom_call_target="tpu_custom_call", output_to_operand_aliasing={{3}: (3, {}), {4}: (4, {}), {5}: (5, {}), {6}: (6, {})} | custom-call | tf_op jit(solution)/shard_map/pallas_call | solution.py:86
  83.2 1.0 all-to-all-done.1.refs_0_
  84.1 6.7 %all-to-all-start.3 = ((bf16[8,2,8,48,256]{4,3,2,1,0:T(8,128)(2,1)}), bf16[8,2,8,48,256]{4,3,2,1,0:T(8,128)(2,1)}, u32[]{:S(2)}, u32[]{:S(2)}) async-start(bf16[8,2,8,48,256]{4,3,2,1,0:T(8,128)(2,1)} %get-tuple-element.32), calls=%async_computation.3 | async-start | bytes 6291456 | tf_op jit(solution)/shard_map/all_to_all | solution.py:296
  91.2 5.5 %collective-permute-done.8 = bf16[4,4,12,16,512]{4,3,2,1,0:T(8,128)(2,1)S(1)} collective-permute-done((bf16[4,4,12,16,512]{4,3,2,1,0:T(8,128)(2,1)}, bf16[4,4,12,16,512]{4,3,2,1,0:T(8,128)(2,1)S(1)}, u32[]{:S(2)}, u32[]{:S(2)}) %collective-permute-start.8) | collective-permute-done | bytes 3145760 | tf_op jit(solution)/shard_map/ppermute | solution.py:260
  96.7 2.9 %fusion.2 = (bf16[4,12,16,512]{3,2,1,0:T(8,128)(2,1)S(1)}, bf16[4,12,16,512]{3,2,1,0:T(8,128)(2,1)}, bf16[4,12,16,512]{3,2,1,0:T(8,128)(2,1)}, f32[4,12,16,512]{3,2,1,0:T(8,128)}) fusion(bf16[4,12,16,512]{3,2,1,0:T(8,128)(2,1)S(1)} %bitcast.104, bf16[4,4,12,16,512]{4,3,2,1,0:T(8,128)(2,1)S(1)} %collective-permute-done.8, ...), kind=kLoop, calls=%fused_computation.5 | loop fusion | flops 5898240 | bytes 10223616 | tf_op jit(solution)/shard_map/convert_element_type | solution.py:262
  99.6 3.5 %collective-permute-start.10 = (bf16[4,12,16,512]{3,2,1,0:T(8,128)(2,1)}, bf16[4,12,16,512]{3,2,1,0:T(8,128)(2,1)}, u32[]{:S(2)}, u32[]{:S(2)}) collective-permute-start(bf16[4,12,16,512]{3,2,1,0:T(8,128)(2,1)} %get-tuple-element.57), channel_id=1, source_target_pairs={{0,32},{8,40},{16,48},{24,56},{32,0},{40,8},{48,16},{56,24},{64,96... | collective-permute-start | bytes 2359304 | tf_op jit(solution)/shard_map/ppermute | solution.py:286
  103.0 1.1 collective-permute-start.11
  104.1 1.0 collective-permute-start.9
  105.1 3.3 %collective-permute-start.4 = (bf16[4,16,512]{2,1,0:T(8,128)(2,1)S(1)}, bf16[4,16,512]{2,1,0:T(8,128)(2,1)S(1)}, u32[]{:S(2)}, u32[]{:S(2)}) collective-permute-start(bf16[4,16,512]{2,1,0:T(8,128)(2,1)S(1)} %copy-done.5), channel_id=1, source_target_pairs={{0,64},{8,72},{16,80},{24,88},{32,96},{40,104},{48,112},{56,120},{... | collective-permute-start | bytes 196616 | tf_op jit(solution)/shard_map/ppermute | solution.py:292
  108.4 2.2 %collective-permute-start.5 = (bf16[4,16,512]{2,1,0:T(8,128)(2,1)S(1)}, bf16[4,16,512]{2,1,0:T(8,128)(2,1)S(1)}, u32[]{:S(2)}, u32[]{:S(2)}) collective-permute-start(bf16[4,16,512]{2,1,0:T(8,128)(2,1)S(1)} %copy-done.3), channel_id=1, source_target_pairs={{0,192},{8,200},{16,208},{24,216},{32,224},{40,232},{48,240},{56,2... | collective-permute-start | bytes 196616 | tf_op jit(solution)/shard_map/ppermute | solution.py:292
  110.6 20.7 %collective-permute-done.4.refs_4_ = bf16[4,16,512]{2,1,0:T(8,128)(2,1)S(1)} collective-permute-done((bf16[4,16,512]{2,1,0:T(8,128)(2,1)S(1)}, bf16[4,16,512]{2,1,0:T(8,128)(2,1)S(1)}, u32[]{:S(2)}, u32[]{:S(2)}) %collective-permute-start.4) | collective-permute-done | bytes 65568 | tf_op jit(solution)/shard_map/ppermute | solution.py:292
  131.9 4.3 %shard_map.106 = (bf16[4,4,2,2,16,512]{5,4,3,2,1,0:T(8,128)(2,1)}, bf16[4,4,2,2,16,512]{5,4,3,2,1,0:T(8,128)(2,1)}) custom-call(bf16[8,2,8,16,256]{4,3,2,1,0:T(8,128)(2,1)} %all-to-all-done.1.refs_0_, bf16[8,2,8,48,256]{4,3,2,1,0:T(8,128)(2,1)} %all-to-all-done.3.refs_1_, bf16[1024,256]{1,0:T(8,128)(2,1)} %refs_2_.10, bf16[1024,256]{1,0:T(8,128)(2,1)} %refs_3_.5, ...), custom_call_target="tpu_custom_call" | custom-call | tf_op jit(solution)/shard_map/pallas_call | solution.py:86
  136.2 1.5 collective-permute-start.7
  137.7 0.8 collective-permute-done.11
  138.5 2.7 %fusion.17 = (bf16[12,16,512]{2,1,0:T(8,128)(2,1)S(1)}, bf16[12,16,512]{2,1,0:T(8,128)(2,1)S(1)}, bf16[12,16,512]{2,1,0:T(8,128)(2,1)S(1)}, f32[12,16,512]{2,1,0:T(8,128)S(1)}) fusion(f32[4,12,16,512]{3,2,1,0:T(8,128)} %get-tuple-element.58, bf16[4,12,16,512]{3,2,1,0:T(8,128)(2,1)} %collective-permute-done.11, ...), kind=kLoop, calls=%fused_computation.49 | loop fusion | flops 2654208 | bytes 4915200 | tf_op jit(solution)/shard_map/add | solution.py:282
  141.6 4.5 %collective-permute-done.7.refs_0_ = bf16[4,16,512]{2,1,0:T(8,128)(2,1)S(1)} collective-permute-done((bf16[4,16,512]{2,1,0:T(8,128)(2,1)}, bf16[4,16,512]{2,1,0:T(8,128)(2,1)S(1)}, u32[]{:S(2)}, u32[]{:S(2)}) %collective-permute-start.7) | collective-permute-done | bytes 65568 | tf_op jit(solution)/shard_map/ppermute | solution.py:292
  146.8 1.5 collective-permute-start.12
  148.3 2.9 %collective-permute-start.13 = (bf16[4,4,16,512]{3,2,1,0:T(8,128)(2,1)S(1)}, bf16[4,4,16,512]{3,2,1,0:T(8,128)(2,1)S(1)}, u32[]{:S(2)}, u32[]{:S(2)}) collective-permute-start(bf16[4,4,16,512]{3,2,1,0:T(8,128)(2,1)S(1)} %get-tuple-element.41), channel_id=1, source_target_pairs={{0,32},{8,40},{16,48},{24,56},{32,0},{40,8},{48,16},{56,24},{64,96... | collective-permute-start | bytes 786440 | tf_op jit(solution)/shard_map/ppermute | solution.py:336
  151.1 1.3 collective-permute-start.14
  152.5 4.0 %collective-permute-start.16 = (bf16[12,16,512]{2,1,0:T(8,128)(2,1)S(1)}, bf16[12,16,512]{2,1,0:T(8,128)(2,1)}, u32[]{:S(2)}, u32[]{:S(2)}) collective-permute-start(bf16[12,16,512]{2,1,0:T(8,128)(2,1)S(1)} %get-tuple-element.49), channel_id=1, source_target_pairs={{0,128},{8,136},{16,144},{24,152},{32,160},{40,168},{48,176},{56,1... | collective-permute-start | bytes 589832 | tf_op jit(solution)/shard_map/ppermute | solution.py:292
  156.5 1.6 collective-permute-start.17
  158.1 3.3 %collective-permute-done.13 = bf16[4,4,16,512]{3,2,1,0:T(8,128)(2,1)S(1)} collective-permute-done((bf16[4,4,16,512]{3,2,1,0:T(8,128)(2,1)S(1)}, bf16[4,4,16,512]{3,2,1,0:T(8,128)(2,1)S(1)}, u32[]{:S(2)}, u32[]{:S(2)}) %collective-permute-start.13) | collective-permute-done | bytes 262176 | tf_op jit(solution)/shard_map/ppermute | solution.py:336
  161.4 0.9 fusion.7.refs_3_
  162.3 4.3 %all-to-all-start.4 = ((bf16[4,4,16,512]{3,2,1,0:T(8,128)(2,1)}), bf16[4,4,16,512]{3,2,1,0:T(8,128)(2,1)}, u32[]{:S(2)}, u32[]{:S(2)}) async-start(bf16[4,4,16,512]{3,2,1,0:T(8,128)(2,1)} %fusion.7.refs_3_), calls=%async_computation.4 | async-start | bytes 524288 | tf_op jit(solution)/shard_map/all_to_all | solution.py:310
  166.7 3.5 %shard_map.108 = (bf16[1024,256]{1,0:T(8,128)(2,1)}, f32[4,16,512]{2,1,0:T(8,128)}, f32[12,16,512]{2,1,0:T(8,128)}) custom-call(bf16[8,2,8,16,256]{4,3,2,1,0:T(8,128)(2,1)} %all-to-all-done.1.refs_0_, bf16[8,2,8,48,256]{4,3,2,1,0:T(8,128)(2,1)} %all-to-all-done.3.refs_1_, ...), custom_call_target="tpu_custom_call", output_to_operand_aliasing={{1}: (4, {}), {2}: (5, {})} | custom-call | tf_op jit(solution)/shard_map/pallas_call | solution.py:86
  170.2 1.0 add_multiply_fusion.1
  171.2 5.7 %collective-permute-done.17 = bf16[12,16,512]{2,1,0:T(8,128)(2,1)} collective-permute-done((bf16[12,16,512]{2,1,0:T(8,128)(2,1)S(1)}, bf16[12,16,512]{2,1,0:T(8,128)(2,1)}, u32[]{:S(2)}, u32[]{:S(2)}) %collective-permute-start.17) | collective-permute-done | bytes 196640 | tf_op jit(solution)/shard_map/ppermute | solution.py:292
  176.9 1.3 add_multiply_fusion
  178.3 0.8 pad_maximum_fusion
  179.1 1.0 convert_reduce_fusion
  180.1 0.7 reshape_squeeze.4
  180.8 0.6 pad_maximum_fusion.2
  (48 shorter events, 3.2 us)
Async XLA Ops:
  4.3 19.9 %all-to-all-start = ((bf16[8,2,2,64,256]{4,3,2,1,0:T(8,128)(2,1)}), bf16[8,2,2,64,256]{4,3,2,1,0:T(8,128)(2,1)}, u32[]{:S(2)}, u32[]{:S(2)}) async-start(bf16[8,2,2,64,256]{4,3,2,1,0:T(8,128)(2,1)} %shard_map.101.refs_4_), calls=%async_computation | async-start | bytes 2097152 | tf_op jit(solution)/shard_map/all_to_all | solution.py:296
  24.2 41.5 %all-to-all-start.2 = ((bf16[8,2,6,64,256]{4,3,2,1,0:T(8,128)(2,1)}), bf16[8,2,6,64,256]{4,3,2,1,0:T(8,128)(2,1)}, u32[]{:S(2)}, u32[]{:S(2)}) async-start(bf16[8,2,6,64,256]{4,3,2,1,0:T(8,128)(2,1)} %shard_map.104), calls=%async_computation.2 | async-start | bytes 6291456 | tf_op jit(solution)/shard_map/all_to_all | solution.py:296
  36.4 2.9 %collective-permute-start = (bf16[4,4,4,16,512]{4,3,2,1,0:T(8,128)(2,1)}, bf16[4,4,4,16,512]{4,3,2,1,0:T(8,128)(2,1)S(1)}, u32[]{:S(2)}, u32[]{:S(2)}) collective-permute-start(bf16[4,4,4,16,512]{4,3,2,1,0:T(8,128)(2,1)} %bitcast.119), channel_id=1, source_target_pairs={{0,8},{8,0},{16,24},{24,16},{32,40},{40,32},{48,56},{56,48},{64,72... | collective-permute-start | bytes 3145736 | tf_op jit(solution)/shard_map/ppermute | solution.py:260
  39.7 9.7 %collective-permute-start.1 = (bf16[4,4,16,512]{3,2,1,0:T(8,128)(2,1)S(1)}, bf16[4,4,16,512]{3,2,1,0:T(8,128)(2,1)S(1)}, u32[]{:S(2)}, u32[]{:S(2)}) collective-permute-start(bf16[4,4,16,512]{3,2,1,0:T(8,128)(2,1)S(1)} %get-tuple-element.74), channel_id=1, source_target_pairs={{0,16},{8,24},{16,32},{24,40},{32,48},{40,56},{48,0},{56,8},{64,80... | collective-permute-start | bytes 786440 | tf_op jit(solution)/shard_map/ppermute | solution.py:286
  41.4 14.8 %collective-permute-start.2 = (bf16[4,4,16,512]{3,2,1,0:T(8,128)(2,1)S(1)}, bf16[4,4,16,512]{3,2,1,0:T(8,128)(2,1)S(1)}, u32[]{:S(2)}, u32[]{:S(2)}) collective-permute-start(bf16[4,4,16,512]{3,2,1,0:T(8,128)(2,1)S(1)} %get-tuple-element.76), channel_id=1, source_target_pairs={{0,32},{8,40},{16,48},{24,56},{32,0},{40,8},{48,16},{56,24},{64,96... | collective-permute-start | bytes 786440 | tf_op jit(solution)/shard_map/ppermute | solution.py:286
  44.3 11.9 %collective-permute-start.3 = (bf16[4,4,16,512]{3,2,1,0:T(8,128)(2,1)S(1)}, bf16[4,4,16,512]{3,2,1,0:T(8,128)(2,1)S(1)}, u32[]{:S(2)}, u32[]{:S(2)}) collective-permute-start(bf16[4,4,16,512]{3,2,1,0:T(8,128)(2,1)S(1)} %get-tuple-element.75), channel_id=1, source_target_pairs={{0,48},{8,56},{16,0},{24,8},{32,16},{40,24},{48,32},{56,40},{64,11... | collective-permute-start | bytes 786440 | tf_op jit(solution)/shard_map/ppermute | solution.py:286
  57.0 8.7 %copy-start.1 = (f32[4,16,512]{2,1,0:T(8,128)}, f32[4,16,512]{2,1,0:T(8,128)S(1)}, u32[]{:S(2)}) copy-start(f32[4,16,512]{2,1,0:T(8,128)S(1)} %get-tuple-element.66.refs_0_.refs_3_) | copy-start | bytes 393220
  57.0 8.7 %copy-start.2 = (bf16[4,16,512]{2,1,0:T(8,128)(2,1)}, bf16[4,16,512]{2,1,0:T(8,128)(2,1)S(1)}, u32[]{:S(2)}) copy-start(bf16[4,16,512]{2,1,0:T(8,128)(2,1)S(1)} %get-tuple-element.63.refs_3_.refs_6_) | copy-start | bytes 196612
  57.0 8.7 %copy-start.4 = (bf16[4,16,512]{2,1,0:T(8,128)(2,1)}, bf16[4,16,512]{2,1,0:T(8,128)(2,1)S(1)}, u32[]{:S(2)}) copy-start(bf16[4,16,512]{2,1,0:T(8,128)(2,1)S(1)} %get-tuple-element.65.refs_1_.refs_4_) | copy-start | bytes 196612
  65.7 18.4 %all-to-all-start.1 = ((bf16[8,2,8,16,256]{4,3,2,1,0:T(8,128)(2,1)}), bf16[8,2,8,16,256]{4,3,2,1,0:T(8,128)(2,1)}, u32[]{:S(2)}, u32[]{:S(2)}) async-start(bf16[8,2,8,16,256]{4,3,2,1,0:T(8,128)(2,1)} %get-tuple-element.31), calls=%async_computation.1 | async-start | bytes 2097152 | tf_op jit(solution)/shard_map/all_to_all | solution.py:296
  84.1 6.7 %copy-start.7 = (bf16[4,4,2,6,16,512]{5,4,3,2,1,0:T(8,128)(2,1)S(1)}, bf16[4,4,2,6,16,512]{5,4,3,2,1,0:T(8,128)(2,1)}, u32[]{:S(2)}) copy-start(bf16[4,4,2,6,16,512]{5,4,3,2,1,0:T(8,128)(2,1)} %get-tuple-element.38) | copy-start | bytes 9437188
  84.1 47.1 %all-to-all-start.3 = ((bf16[8,2,8,48,256]{4,3,2,1,0:T(8,128)(2,1)}), bf16[8,2,8,48,256]{4,3,2,1,0:T(8,128)(2,1)}, u32[]{:S(2)}, u32[]{:S(2)}) async-start(bf16[8,2,8,48,256]{4,3,2,1,0:T(8,128)(2,1)} %get-tuple-element.32), calls=%async_computation.3 | async-start | bytes 6291456 | tf_op jit(solution)/shard_map/all_to_all | solution.py:296
  90.8 5.9 %collective-permute-start.8 = (bf16[4,4,12,16,512]{4,3,2,1,0:T(8,128)(2,1)}, bf16[4,4,12,16,512]{4,3,2,1,0:T(8,128)(2,1)S(1)}, u32[]{:S(2)}, u32[]{:S(2)}) collective-permute-start(bf16[4,4,12,16,512]{4,3,2,1,0:T(8,128)(2,1)} %bitcast.117), channel_id=1, source_target_pairs={{0,8},{8,0},{16,24},{24,16},{32,40},{40,32},{48,56},{56,48},{64,72... | collective-permute-start | bytes 9437192 | tf_op jit(solution)/shard_map/ppermute | solution.py:260
  96.7 8.4 %copy-start.5 = (bf16[4,16,512]{2,1,0:T(8,128)(2,1)S(1)}, bf16[4,16,512]{2,1,0:T(8,128)(2,1)}, u32[]{:S(2)}) copy-start(bf16[4,16,512]{2,1,0:T(8,128)(2,1)} %get-tuple-element.33) | copy-start | bytes 196612
  96.7 11.6 %copy-start.3 = (bf16[4,16,512]{2,1,0:T(8,128)(2,1)S(1)}, bf16[4,16,512]{2,1,0:T(8,128)(2,1)}, u32[]{:S(2)}) copy-start(bf16[4,16,512]{2,1,0:T(8,128)(2,1)} %get-tuple-element.34) | copy-start | bytes 196612
  99.6 38.1 %collective-permute-start.10 = (bf16[4,12,16,512]{3,2,1,0:T(8,128)(2,1)}, bf16[4,12,16,512]{3,2,1,0:T(8,128)(2,1)}, u32[]{:S(2)}, u32[]{:S(2)}) collective-permute-start(bf16[4,12,16,512]{3,2,1,0:T(8,128)(2,1)} %get-tuple-element.57), channel_id=1, source_target_pairs={{0,32},{8,40},{16,48},{24,56},{32,0},{40,8},{48,16},{56,24},{64,96... | collective-permute-start | bytes 2359304 | tf_op jit(solution)/shard_map/ppermute | solution.py:286
  103.0 35.4 %collective-permute-start.11 = (bf16[4,12,16,512]{3,2,1,0:T(8,128)(2,1)}, bf16[4,12,16,512]{3,2,1,0:T(8,128)(2,1)}, u32[]{:S(2)}, u32[]{:S(2)}) collective-permute-start(bf16[4,12,16,512]{3,2,1,0:T(8,128)(2,1)} %get-tuple-element.56), channel_id=1, source_target_pairs={{0,48},{8,56},{16,0},{24,8},{32,16},{40,24},{48,32},{56,40},{64,11... | collective-permute-start | bytes 2359304 | tf_op jit(solution)/shard_map/ppermute | solution.py:286
  104.1 34.4 %collective-permute-start.9 = (bf16[4,12,16,512]{3,2,1,0:T(8,128)(2,1)S(1)}, bf16[4,12,16,512]{3,2,1,0:T(8,128)(2,1)}, u32[]{:S(2)}, u32[]{:S(2)}) collective-permute-start(bf16[4,12,16,512]{3,2,1,0:T(8,128)(2,1)S(1)} %get-tuple-element.55), channel_id=1, source_target_pairs={{0,16},{8,24},{16,32},{24,40},{32,48},{40,56},{48,0},{56,8},{64,80... | collective-permute-start | bytes 2359304 | tf_op jit(solution)/shard_map/ppermute | solution.py:286
  105.1 26.2 %collective-permute-start.4 = (bf16[4,16,512]{2,1,0:T(8,128)(2,1)S(1)}, bf16[4,16,512]{2,1,0:T(8,128)(2,1)S(1)}, u32[]{:S(2)}, u32[]{:S(2)}) collective-permute-start(bf16[4,16,512]{2,1,0:T(8,128)(2,1)S(1)} %copy-done.5), channel_id=1, source_target_pairs={{0,64},{8,72},{16,80},{24,88},{32,96},{40,104},{48,112},{56,120},{... | collective-permute-start | bytes 196616 | tf_op jit(solution)/shard_map/ppermute | solution.py:292
  108.4 22.9 %collective-permute-start.5 = (bf16[4,16,512]{2,1,0:T(8,128)(2,1)S(1)}, bf16[4,16,512]{2,1,0:T(8,128)(2,1)S(1)}, u32[]{:S(2)}, u32[]{:S(2)}) collective-permute-start(bf16[4,16,512]{2,1,0:T(8,128)(2,1)S(1)} %copy-done.3), channel_id=1, source_target_pairs={{0,192},{8,200},{16,208},{24,216},{32,224},{40,232},{48,240},{56,2... | collective-permute-start | bytes 196616 | tf_op jit(solution)/shard_map/ppermute | solution.py:292
  131.2 0.6 copy-start.9
  131.2 0.6 copy-start.10
  136.2 5.1 %collective-permute-start.6 = (bf16[4,4,4,16,512]{4,3,2,1,0:T(8,128)(2,1)}, bf16[4,4,4,16,512]{4,3,2,1,0:T(8,128)(2,1)S(1)}, u32[]{:S(2)}, u32[]{:S(2)}) collective-permute-start(bf16[4,4,4,16,512]{4,3,2,1,0:T(8,128)(2,1)} %bitcast.118), channel_id=1, source_target_pairs={{0,8},{8,0},{16,24},{24,16},{32,40},{40,32},{48,56},{56,48},{64,72... | collective-permute-start | bytes 3145736 | tf_op jit(solution)/shard_map/ppermute | solution.py:260
  136.2 10.0 %collective-permute-start.7 = (bf16[4,16,512]{2,1,0:T(8,128)(2,1)}, bf16[4,16,512]{2,1,0:T(8,128)(2,1)S(1)}, u32[]{:S(2)}, u32[]{:S(2)}) collective-permute-start(bf16[4,16,512]{2,1,0:T(8,128)(2,1)} %get-tuple-element.37), channel_id=1, source_target_pairs={{0,128},{8,136},{16,144},{24,152},{32,160},{40,168},{48,176},{56,1... | collective-permute-start | bytes 196616 | tf_op jit(solution)/shard_map/ppermute | solution.py:292
  138.5 2.7 %copy-start.8 = (bf16[4,4,2,2,16,512]{5,4,3,2,1,0:T(8,128)(2,1)S(1)}, bf16[4,4,2,2,16,512]{5,4,3,2,1,0:T(8,128)(2,1)}, u32[]{:S(2)}) copy-start(bf16[4,4,2,2,16,512]{5,4,3,2,1,0:T(8,128)(2,1)} %get-tuple-element.35) | copy-start | bytes 3145732
  146.2 15.2 %copy-start.6 = (bf16[4,16,512]{2,1,0:T(8,128)(2,1)}, bf16[4,16,512]{2,1,0:T(8,128)(2,1)S(1)}, u32[]{:S(2)}) copy-start(bf16[4,16,512]{2,1,0:T(8,128)(2,1)S(1)} %collective-permute-done.7.refs_0_) | copy-start | bytes 196612
  146.8 19.9 %copy-start = (f32[12,16,512]{2,1,0:T(8,128)}, f32[12,16,512]{2,1,0:T(8,128)S(1)}, u32[]{:S(2)}) copy-start(f32[12,16,512]{2,1,0:T(8,128)S(1)} %get-tuple-element.44.refs_5_) | copy-start | bytes 1179652
  146.8 9.7 %collective-permute-start.12 = (bf16[4,4,16,512]{3,2,1,0:T(8,128)(2,1)S(1)}, bf16[4,4,16,512]{3,2,1,0:T(8,128)(2,1)S(1)}, u32[]{:S(2)}, u32[]{:S(2)}) collective-permute-start(bf16[4,4,16,512]{3,2,1,0:T(8,128)(2,1)S(1)} %get-tuple-element.40), channel_id=1, source_target_pairs={{0,16},{8,24},{16,32},{24,40},{32,48},{40,56},{48,0},{56,8},{64,80... | collective-permute-start | bytes 786440 | tf_op jit(solution)/shard_map/ppermute | solution.py:336
  148.3 13.1 %collective-permute-start.13 = (bf16[4,4,16,512]{3,2,1,0:T(8,128)(2,1)S(1)}, bf16[4,4,16,512]{3,2,1,0:T(8,128)(2,1)S(1)}, u32[]{:S(2)}, u32[]{:S(2)}) collective-permute-start(bf16[4,4,16,512]{3,2,1,0:T(8,128)(2,1)S(1)} %get-tuple-element.41), channel_id=1, source_target_pairs={{0,32},{8,40},{16,48},{24,56},{32,0},{40,8},{48,16},{56,24},{64,96... | collective-permute-start | bytes 786440 | tf_op jit(solution)/shard_map/ppermute | solution.py:336
  151.1 10.3 %collective-permute-start.14 = (bf16[4,4,16,512]{3,2,1,0:T(8,128)(2,1)S(1)}, bf16[4,4,16,512]{3,2,1,0:T(8,128)(2,1)S(1)}, u32[]{:S(2)}, u32[]{:S(2)}) collective-permute-start(bf16[4,4,16,512]{3,2,1,0:T(8,128)(2,1)S(1)} %get-tuple-element.42), channel_id=1, source_target_pairs={{0,48},{8,56},{16,0},{24,8},{32,16},{40,24},{48,32},{56,40},{64,11... | collective-permute-start | bytes 786440 | tf_op jit(solution)/shard_map/ppermute | solution.py:336
  152.5 18.7 %collective-permute-start.15 = (bf16[12,16,512]{2,1,0:T(8,128)(2,1)S(1)}, bf16[12,16,512]{2,1,0:T(8,128)(2,1)}, u32[]{:S(2)}, u32[]{:S(2)}) collective-permute-start(bf16[12,16,512]{2,1,0:T(8,128)(2,1)S(1)} %get-tuple-element.48), channel_id=1, source_target_pairs={{0,64},{8,72},{16,80},{24,88},{32,96},{40,104},{48,112},{56,120},{... | collective-permute-start | bytes 589832 | tf_op jit(solution)/shard_map/ppermute | solution.py:292
  152.5 18.7 %collective-permute-start.16 = (bf16[12,16,512]{2,1,0:T(8,128)(2,1)S(1)}, bf16[12,16,512]{2,1,0:T(8,128)(2,1)}, u32[]{:S(2)}, u32[]{:S(2)}) collective-permute-start(bf16[12,16,512]{2,1,0:T(8,128)(2,1)S(1)} %get-tuple-element.49), channel_id=1, source_target_pairs={{0,128},{8,136},{16,144},{24,152},{32,160},{40,168},{48,176},{56,1... | collective-permute-start | bytes 589832 | tf_op jit(solution)/shard_map/ppermute | solution.py:292
  156.5 20.4 %collective-permute-start.17 = (bf16[12,16,512]{2,1,0:T(8,128)(2,1)S(1)}, bf16[12,16,512]{2,1,0:T(8,128)(2,1)}, u32[]{:S(2)}, u32[]{:S(2)}) collective-permute-start(bf16[12,16,512]{2,1,0:T(8,128)(2,1)S(1)} %get-tuple-element.50), channel_id=1, source_target_pairs={{0,192},{8,200},{16,208},{24,216},{32,224},{40,232},{48,240},{56,2... | collective-permute-start | bytes 589832 | tf_op jit(solution)/shard_map/ppermute | solution.py:292
  162.3 16.8 %all-to-all-start.4 = ((bf16[4,4,16,512]{3,2,1,0:T(8,128)(2,1)}), bf16[4,4,16,512]{3,2,1,0:T(8,128)(2,1)}, u32[]{:S(2)}, u32[]{:S(2)}) async-start(bf16[4,4,16,512]{3,2,1,0:T(8,128)(2,1)} %fusion.7.refs_3_), calls=%async_computation.4 | async-start | bytes 524288 | tf_op jit(solution)/shard_map/all_to_all | solution.py:310

commit v4 on v3

--- a/solution.py
+++ b/solution.py
@@ -123,15 +123,19 @@
     return out
 
 
-def place(me, held, own_ref, other_ref, index):
+def place(me, held, own_ref, near_ref, far_ref, index):
     for ry in range(Y):
         for rz in range(Z):
             group = (lax.rem(me[2] + rz, Z) * Y + lax.rem(me[1] + ry, Y)) * CORES
             own_ref[(ry, rz) + index] = held[group + me[0]]
-            other_ref[(ry, rz) + index] = held[group + 1 - me[0]]
-
-
-def middle_kernel(me, got_ref, up_ref, down_ref, back_ref, own_ref, other_ref, held):
+            other = held[group + 1 - me[0]]
+            if ry == 0:
+                near_ref[(0, rz) + index] = other
+            else:
+                far_ref[(ry - 1, rz) + index] = other
+
+
+def middle_kernel(me, got_ref, up_ref, down_ref, back_ref, own_ref, near_ref, far_ref, held):
     lows, mids = [], []
     for i in range(2):
         v = got_ref[:, 0, i].reshape(BLK_HID, -1)
@@ -141,11 +145,11 @@
         hidden = value.astype(half)
         lows.append(dot(down, hidden, 0, 0))
         held[0] = dot(hidden, f, 1, 1).astype(half).reshape(-1, ROWS, BLK_HID)
-        place(me, held.at[0], own_ref, other_ref, (0, i))
+        place(me, held.at[0], own_ref, near_ref, far_ref, (0, i))
         back = (dot(down, f, 1, 0) * slope).astype(half)
         mids.append(dot(up, back, 1, 0))
         held[1] = dot(v, back, 1, 1).astype(half).reshape(-1, ROWS, BLK_HID)
-        place(me, held.at[1], own_ref, other_ref, (1, i))
+        place(me, held.at[1], own_ref, near_ref, far_ref, (1, i))
     back_ref[:, 0] = spread_pair(*lows).reshape(PEERS, LOCAL, PAIR, -1)
     back_ref[:, 1] = spread_pair(*mids).reshape(PEERS, LOCAL, PAIR, -1)
 
@@ -154,8 +158,11 @@
     tokens = got.shape[-1]
     pairs = CHUNKS[chunk]
     start = sum(CHUNKS[:chunk])
-    grads = jax.ShapeDtypeStruct((Y, Z, 2, 2 * pairs, ROWS, BLK_HID), half)
-    grads_spec = pl.BlockSpec((Y, Z, 2, 2, ROWS, BLK_HID), lambda p: (0, 0, 0, p, 0, 0))
+    sizes = (Y, 1, Y - 1)
+    grads = [jax.ShapeDtypeStruct((n, Z, 2, 2 * pairs, ROWS, BLK_HID), half) for n in sizes]
+    grads_specs = [
+        pl.BlockSpec((n, Z, 2, 2, ROWS, BLK_HID), lambda p: (0, 0, 0, p, 0, 0)) for n in sizes
+    ]
     weight = pl.BlockSpec((2, BLK_HID, BLK_HID), lambda p: (start + p, 0, 0))
     return call(
         middle_kernel,
@@ -167,13 +174,11 @@
         ],
         [
             pl.BlockSpec((PEERS, 2, LOCAL, PAIR, tokens), lambda p: (0, 0, 0, p, 0)),
-            grads_spec,
-            grads_spec,
+            *grads_specs,
         ],
         [
             jax.ShapeDtypeStruct((PEERS, 2, LOCAL, pairs * PAIR, tokens), half),
-            grads,
-            grads,
+            *grads,
         ],
         scratch=[pltpu.VMEM((2, BLK_HID // ROWS, ROWS, BLK_HID), half)],
         **order,
@@ -185,7 +190,7 @@
     return both.reshape(BLK_HID, -1)
 
 
-def outer_kernel(me, one_ref, two_ref, x_ref, g_ref, own_ref, other_ref, held, held_down):
+def outer_kernel(me, one_ref, two_ref, x_ref, g_ref, own_ref, near_ref, far_ref, held, held_down):
     rows4 = BLK_IN // (Z * Y * CORES)
     evens, odds = [], []
     for i in range(4):
@@ -202,9 +207,10 @@
         for z in range(Z):
             chip = z * Y + lax.rem(me[1] + ry, Y)
             own_ref[ry, z, 0, 0] = held[me[0], chip]
-            other_ref[ry, z, 0, 0] = held[1 - me[0], chip]
             own_ref[ry, z, 1, 0] = held_down[chip * CORES + me[0]]
-            other_ref[ry, z, 1, 0] = held_down[chip * CORES + 1 - me[0]]
+            other_ref, at = (near_ref, 0) if ry == 0 else (far_ref, ry - 1)
+            other_ref[at, z, 0, 0] = held[1 - me[0], chip]
+            other_ref[at, z, 1, 0] = held_down[chip * CORES + 1 - me[0]]
 
 
 def got_specs(tokens):
@@ -216,15 +222,18 @@
 def outer_stage(one, two, inputs, grad_out, **order):
     tokens = inputs.shape[1]
     groups = LOCAL // 4
-    grads = jax.ShapeDtypeStruct((Y, Z, 2, groups, ROWS, BLK_HID), half)
-    grads_spec = pl.BlockSpec((Y, Z, 2, 1, ROWS, BLK_HID), lambda p: (0, 0, 0, p, 0, 0))
+    sizes = (Y, 1, Y - 1)
+    grads = [jax.ShapeDtypeStruct((n, Z, 2, groups, ROWS, BLK_HID), half) for n in sizes]
+    grads_specs = [
+        pl.BlockSpec((n, Z, 2, 1, ROWS, BLK_HID), lambda p: (0, 0, 0, p, 0, 0)) for n in sizes
+    ]
     feats = pl.BlockSpec((4 * BLK_IN, tokens), lambda p: (p, 0))
     return call(
         outer_kernel,
         (groups,),
         got_specs(tokens) + [feats, feats],
-        [grads_spec, grads_spec],
-        [grads, grads],
+        grads_specs,
+        grads,
         scratch=[
             pltpu.VMEM((CORES, Z * Y, ROWS, BLK_HID), half),
             pltpu.VMEM((Z * Y * CORES, ROWS, BLK_HID), half),
@@ -252,14 +261,15 @@
 
 
 def flat(array):
-    return array.reshape(Y, Z, -1, ROWS, BLK_HID)
-
-
-def core_step(own, other):
+    return array.reshape(array.shape[0], Z, -1, ROWS, BLK_HID)
+
+
+def core_step(own, near, far):
     own = flat(own)
-    got = lax.ppermute(flat(other), "dp", dp_perm(0, 0, 1))
-    sums = [own[r].astype(single) + got[r].astype(single) for r in range(Y)]
-    return sums[0], *[total.astype(half) for total in sums[1:]]
+    got = [lax.ppermute(flat(part), "dp", dp_perm(0, 0, 1)) for part in (far, near)]
+    keep = own[0].astype(single) + got[1][0].astype(single)
+    sends = [own[r + 1].astype(single) + got[0][r].astype(single) for r in range(Y - 1)]
+    return keep, *[total.astype(half) for total in sends]
 
 
 def gate(arrays, after=()):
@@ -320,18 +330,20 @@
     operands = (inputs, grad_out, up_left, down_right)
     one = first_stage(0, *operands)
     two = first_stage(1, *operands, after=(one,))
-    back1, own, other = middle_stage(0, exchange(one), up_right, down_left)
-    sums1 = line_step(*core_step(own, other))
+    back1, *rows = middle_stage(0, exchange(one), up_right, down_left)
+    sums1 = line_step(*core_step(*rows))
     (back1,) = gate([back1], sums1)
-    back2, own, other, *sums1 = middle_stage(
+    back2, own, near, far, *sums1 = middle_stage(
         1, exchange(two), up_right, down_left, carry=sums1
     )
-    sums2 = core_step(own, other)
+    sums2 = core_step(own, near, far)
     back1, back2 = exchange(back1), exchange(back2)
     got1 = end_moves(*sums1)
-    own, other = outer_stage(back1, back2, inputs, grad_out, after=got1[::2])
-    keep, *sends = core_step(own, other)
-    gated = gate([*sends, *line_step(*sums2)], got1[1:2])
+    own, near, far = outer_stage(
+        back1, back2, inputs, grad_out, after=[*got1[::2], sums2[0]]
+    )
+    keep, *sends = core_step(own, near, far)
+    gated = gate([*sends, *line_step(*sums2)])
     sends, sums2 = gated[: len(sends)], gated[len(sends) :]
     outer = add(keep, [lax.ppermute(s, "dp", dp_perm(0, r + 1, 0)) for r, s in enumerate(sends)])
     got2 = end_moves(*sums2)

time: 185 us -> 186 us (level); the launches traced: 181 us -> 185 us
  starting transfers between devices: 59.5 us -> 67.9 us
  waiting for transfers between devices: 71.2 us -> 64.5 us
    ppermute x6, starting transfers between devices: 12.6 us -> 20.3 us  [end_moves(): lax.ppermute(s, 'dp', dp_perm(r + 1, 0, 0))]
    ppermute x3, waiting for transfers between devices: 3.28 us -> 0.03 us  [shards(): lax.ppermute(s, 'dp', dp_perm(0, r + 1, 0))]
    ppermute x3 -> x6, waiting for transfers between devices: 7.14 us -> 4.65 us  [core_step(): lax.ppermute(flat(part), 'dp', dp_perm(0, 0, 1))]
  transfers between devices with their start and end apart: 23 -> 26, of which waited for: 12 -> 11; matrix products, arithmetic and copies ran while one was open for 7% -> 7% of each run, Pallas kernels for 16% -> 16%
where the time goes in v4:
time: 186 us; the launch traced here: 185 us
  starting transfers between devices  67.9 us (37%)
  waiting for transfers between devices  64.5 us (35%)
  Pallas kernels  33.9 us (18%)
  other arithmetic  13.6 us (7%)
  local copies, waits for them, and re-layouts  3.91 us (2%)
    pallas_call x8, Pallas kernels, call(): return lambda *operands: run(*operands, *after, *carry)  33.9 us
    ppermute x6, waiting for transfers between devices, end_moves(): lax.ppermute(s, 'dp', dp_perm(r + 1, 0, 0))  29.4 us
    all_to_all x4, starting transfers between devices, exchange(): lax.all_to_all(array, 'block', split_axis=0, concat_axis=0, tiled=True)  25.5 us
    ppermute x6, starting transfers between devices, end_moves(): lax.ppermute(s, 'dp', dp_perm(r + 1, 0, 0))  20.3 us
    all_to_all x4, waiting for transfers between devices, exchange(): lax.all_to_all(array, 'block', split_axis=0, concat_axis=0, tiled=True)  19.1 us
    ppermute x6, waiting for transfers between devices, line_step(): lax.ppermute(s, 'dp', dp_perm(0, r + 1, 0))  11.3 us
    ppermute x6, starting transfers between devices, line_step(): lax.ppermute(s, 'dp', dp_perm(0, r + 1, 0))  10.8 us
    ppermute x3, starting transfers between devices, shards(): lax.ppermute(s, 'dp', dp_perm(0, r + 1, 0))  5.83 us
  transfers between devices with their start and end apart: 26, of which 11 were waited for; matrix products, arithmetic and copies ran while one was open for 7% of the time, Pallas kernels for 16%

profile of v4, /device:TPU:2, one launch (start us, length us, event | category | flops | bytes accessed | tf_op | source)
XLA Modules:
  0.0 184.6 jit_solution(12004652807139829054)
XLA Ops:
  0.6 3.7 %shard_map.101.refs_4_ = bf16[8,2,2,64,256]{4,3,2,1,0:T(8,128)(2,1)} custom-call(bf16[1024,256]{1,0:T(8,128)(2,1)} %refs_2_.10, bf16[1024,256]{1,0:T(8,128)(2,1)} %refs_3_.5, bf16[8,128,512]{2,1,0:T(8,128)(2,1)} %refs_2_.11, bf16[8,512,128]{2,1,0:T(8,128)(2,1)} %refs_3_.4), custom_call_target="tpu_custom_call" | custom-call | tf_op jit(solution)/shard_map/pallas_call | solution.py:86
  4.3 6.4 %all-to-all-start = ((bf16[8,2,2,64,256]{4,3,2,1,0:T(8,128)(2,1)}), bf16[8,2,2,64,256]{4,3,2,1,0:T(8,128)(2,1)}, u32[]{:S(2)}, u32[]{:S(2)}) async-start(bf16[8,2,2,64,256]{4,3,2,1,0:T(8,128)(2,1)} %shard_map.101.refs_4_), calls=%async_computation | async-start | bytes 2097152 | tf_op jit(solution)/shard_map/all_to_all | solution.py:306
  10.7 4.0 %shard_map.104 = bf16[8,2,6,64,256]{4,3,2,1,0:T(8,128)(2,1)} custom-call(bf16[1024,256]{1,0:T(8,128)(2,1)} %refs_2_.10, bf16[1024,256]{1,0:T(8,128)(2,1)} %refs_3_.5, bf16[8,128,512]{2,1,0:T(8,128)(2,1)} %refs_2_.11, bf16[8,512,128]{2,1,0:T(8,128)(2,1)} %refs_3_.4, bf16[8,2,2,64,256]{4,3,2,1,0:T(8,128)(2,1)} %shard_map.101.refs_4_), custom_call_target="tpu_custom_call" | custom-call | tf_op jit(solution)/shard_map/pallas_call | solution.py:86
  14.7 9.5 %all-to-all-done.refs_0_ = bf16[8,2,2,64,256]{4,3,2,1,0:T(8,128)(2,1)} async-done(((bf16[8,2,2,64,256]{4,3,2,1,0:T(8,128)(2,1)}), bf16[8,2,2,64,256]{4,3,2,1,0:T(8,128)(2,1)}, u32[]{:S(2)}, u32[]{:S(2)}) %all-to-all-start) | async-done | bytes 1048608 | tf_op jit(solution)/shard_map/all_to_all | solution.py:306
  24.2 6.4 %all-to-all-start.2 = ((bf16[8,2,6,64,256]{4,3,2,1,0:T(8,128)(2,1)}), bf16[8,2,6,64,256]{4,3,2,1,0:T(8,128)(2,1)}, u32[]{:S(2)}, u32[]{:S(2)}) async-start(bf16[8,2,6,64,256]{4,3,2,1,0:T(8,128)(2,1)} %shard_map.104), calls=%async_computation.2 | async-start | bytes 6291456 | tf_op jit(solution)/shard_map/all_to_all | solution.py:306
  30.6 5.8 %shard_map.102 = (bf16[8,2,8,16,256]{4,3,2,1,0:T(8,128)(2,1)}, bf16[4,4,2,2,16,512]{5,4,3,2,1,0:T(8,128)(2,1)}, bf16[1,4,2,2,16,512]{5,4,3,2,1,0:T(8,128)(2,1)}, bf16[3,4,2,2,16,512]{5,4,3,2,1,0:T(8,128)(2,1)}) custom-call(bf16[8,2,2,64,256]{4,3,2,1,0:T(8,128)(2,1)} %all-to-all-done.refs_0_, bf16[8,512,512]{2,1,0:T(8,128)(2,1)} %refs_1_.7, ...), custom_call_target="tpu_custom_call" | custom-call | tf_op jit(solution)/shard_map/pallas_call | solution.py:86
  36.9 1.3 fusion.27
  38.2 0.7 collective-permute-done.1
  39.2 1.7 collective-permute-start.2
  40.9 1.7 collective-permute-start.4
  42.5 2.0 %collective-permute-start.3 = (bf16[4,4,16,512]{3,2,1,0:T(8,128)(2,1)S(1)}, bf16[4,4,16,512]{3,2,1,0:T(8,128)(2,1)S(1)}, u32[]{:S(2)}, u32[]{:S(2)}) collective-permute-start(bf16[4,4,16,512]{3,2,1,0:T(8,128)(2,1)S(1)} %get-tuple-element.85), channel_id=1, source_target_pairs={{0,32},{8,40},{16,48},{24,56},{32,0},{40,8},{48,16},{56,24},{64,96... | collective-permute-start | bytes 786440 | tf_op jit(solution)/shard_map/ppermute | solution.py:296
  44.6 4.3 %collective-permute-done.2 = bf16[4,4,16,512]{3,2,1,0:T(8,128)(2,1)S(1)} collective-permute-done((bf16[4,4,16,512]{3,2,1,0:T(8,128)(2,1)S(1)}, bf16[4,4,16,512]{3,2,1,0:T(8,128)(2,1)S(1)}, u32[]{:S(2)}, u32[]{:S(2)}) %collective-permute-start.2) | collective-permute-done | bytes 262176 | tf_op jit(solution)/shard_map/ppermute | solution.py:296
  48.9 5.0 %collective-permute-done.4 = bf16[4,4,16,512]{3,2,1,0:T(8,128)(2,1)S(1)} collective-permute-done((bf16[4,4,16,512]{3,2,1,0:T(8,128)(2,1)S(1)}, bf16[4,4,16,512]{3,2,1,0:T(8,128)(2,1)S(1)}, u32[]{:S(2)}, u32[]{:S(2)}) %collective-permute-start.4) | collective-permute-done | bytes 262176 | tf_op jit(solution)/shard_map/ppermute | solution.py:296
  53.9 1.8 collective-permute-done.3
  55.7 0.8 fusion.24
  57.1 8.6 %all-to-all-done.2.refs_0_ = bf16[8,2,6,64,256]{4,3,2,1,0:T(8,128)(2,1)} async-done(((bf16[8,2,6,64,256]{4,3,2,1,0:T(8,128)(2,1)}), bf16[8,2,6,64,256]{4,3,2,1,0:T(8,128)(2,1)}, u32[]{:S(2)}, u32[]{:S(2)}) %all-to-all-start.2) | async-done | bytes 3145760 | tf_op jit(solution)/shard_map/all_to_all | solution.py:306
  65.7 5.9 %all-to-all-start.1 = ((bf16[8,2,8,16,256]{4,3,2,1,0:T(8,128)(2,1)}), bf16[8,2,8,16,256]{4,3,2,1,0:T(8,128)(2,1)}, u32[]{:S(2)}, u32[]{:S(2)}) async-start(bf16[8,2,8,16,256]{4,3,2,1,0:T(8,128)(2,1)} %get-tuple-element.35), calls=%async_computation.1 | async-start | bytes 2097152 | tf_op jit(solution)/shard_map/all_to_all | solution.py:306
  71.7 11.4 %shard_map.105 = (bf16[8,2,8,48,256]{4,3,2,1,0:T(8,128)(2,1)}, bf16[4,4,2,6,16,512]{5,4,3,2,1,0:T(8,128)(2,1)}, bf16[1,4,2,6,16,512]{5,4,3,2,1,0:T(8,128)(2,1)},...) custom-call(bf16[8,2,6,64,256]{4,3,2,1,0:T(8,128)(2,1)} %all-to-all-, ...), custom_call_target="tpu_custom_call", output_to_operand_aliasing={{4}: (3, {}), {5}: (4, {}), {6}: (5, {}), {7}: (6, {})} | custom-call | tf_op jit(solution)/shard_map/pallas_call | solution.py:86
  83.1 1.0 all-to-all-done.1.refs_0_
  84.1 6.7 %all-to-all-start.3 = ((bf16[8,2,8,48,256]{4,3,2,1,0:T(8,128)(2,1)}), bf16[8,2,8,48,256]{4,3,2,1,0:T(8,128)(2,1)}, u32[]{:S(2)}, u32[]{:S(2)}) async-start(bf16[8,2,8,48,256]{4,3,2,1,0:T(8,128)(2,1)} %get-tuple-element.36), calls=%async_computation.3 | async-start | bytes 6291456 | tf_op jit(solution)/shard_map/all_to_all | solution.py:306
  91.7 3.9 %collective-permute-done.10 = bf16[3,4,12,16,512]{4,3,2,1,0:T(8,128)(2,1)S(1)} collective-permute-done((bf16[3,4,12,16,512]{4,3,2,1,0:T(8,128)(2,1)}, bf16[3,4,12,16,512]{4,3,2,1,0:T(8,128)(2,1)S(1)}, u32[]{:S(2)}, u32[]{:S(2)}) %collective-permute-start.10) | collective-permute-done | bytes 2359328 | tf_op jit(solution)/shard_map/ppermute | solution.py:269
  95.6 2.3 %fusion.2 = (bf16[4,12,16,512]{3,2,1,0:T(8,128)(2,1)}, bf16[4,12,16,512]{3,2,1,0:T(8,128)(2,1)}, bf16[4,12,16,512]{3,2,1,0:T(8,128)(2,1)}) fusion(bf16[4,12,16,512]{3,2,1,0:T(8,128)(2,1)S(1)} %bitcast.101, bf16[3,4,12,16,512]{4,3,2,1,0:T(8,128)(2,1)S(1)} %collective-permute-done.10, bf16[4,12,16,512]{3,2,1,0:T(8,128)(2,1)S(1)} %bitcast.102, ...), kind=kLoop, calls=%fused_computation.5 | loop fusion | flops 4718592 | bytes 7077888 | tf_op jit(solution)/shard_map/convert_element_type | solution.py:272
  97.8 1.8 %collective-permute-start.11 = (bf16[4,12,16,512]{3,2,1,0:T(8,128)(2,1)}, bf16[4,12,16,512]{3,2,1,0:T(8,128)(2,1)S(1)}, u32[]{:S(2)}, u32[]{:S(2)}) collective-permute-start(bf16[4,12,16,512]{3,2,1,0:T(8,128)(2,1)} %get-tuple-element.65), channel_id=1, source_target_pairs={{0,16},{8,24},{16,32},{24,40},{32,48},{40,56},{48,0},{56,8},{64,80... | collective-permute-start | bytes 2359304 | tf_op jit(solution)/shard_map/ppermute | solution.py:296
  99.7 1.4 collective-permute-start.13
  101.1 2.2 %collective-permute-start.12 = (bf16[4,12,16,512]{3,2,1,0:T(8,128)(2,1)}, bf16[4,12,16,512]{3,2,1,0:T(8,128)(2,1)}, u32[]{:S(2)}, u32[]{:S(2)}) collective-permute-start(bf16[4,12,16,512]{3,2,1,0:T(8,128)(2,1)} %get-tuple-element.67), channel_id=1, source_target_pairs={{0,32},{8,40},{16,48},{24,56},{32,0},{40,8},{48,16},{56,24},{64,96... | collective-permute-start | bytes 2359304 | tf_op jit(solution)/shard_map/ppermute | solution.py:296
  103.3 3.3 %collective-permute-start.5 = (bf16[4,16,512]{2,1,0:T(8,128)(2,1)S(1)}, bf16[4,16,512]{2,1,0:T(8,128)(2,1)S(1)}, u32[]{:S(2)}, u32[]{:S(2)}) collective-permute-start(bf16[4,16,512]{2,1,0:T(8,128)(2,1)S(1)} %copy-done.5), channel_id=1, source_target_pairs={{0,64},{8,72},{16,80},{24,88},{32,96},{40,104},{48,112},{56,120},{... | collective-permute-start | bytes 196616 | tf_op jit(solution)/shard_map/ppermute | solution.py:302
  106.6 2.2 %collective-permute-start.6 = (bf16[4,16,512]{2,1,0:T(8,128)(2,1)S(1)}, bf16[4,16,512]{2,1,0:T(8,128)(2,1)S(1)}, u32[]{:S(2)}, u32[]{:S(2)}) collective-permute-start(bf16[4,16,512]{2,1,0:T(8,128)(2,1)S(1)} %copy-done.3), channel_id=1, source_target_pairs={{0,192},{8,200},{16,208},{24,216},{32,224},{40,232},{48,240},{56,2... | collective-permute-start | bytes 196616 | tf_op jit(solution)/shard_map/ppermute | solution.py:302
  108.8 1.5 convert_add_fusion.3.refs_6_
  110.4 20.9 %collective-permute-done.5.refs_4_ = bf16[4,16,512]{2,1,0:T(8,128)(2,1)S(1)} collective-permute-done((bf16[4,16,512]{2,1,0:T(8,128)(2,1)S(1)}, bf16[4,16,512]{2,1,0:T(8,128)(2,1)S(1)}, u32[]{:S(2)}, u32[]{:S(2)}) %collective-permute-start.5) | collective-permute-done | bytes 65568 | tf_op jit(solution)/shard_map/ppermute | solution.py:302
  131.9 4.3 %shard_map.106 = (bf16[4,4,2,2,16,512]{5,4,3,2,1,0:T(8,128)(2,1)}, bf16[1,4,2,2,16,512]{5,4,3,2,1,0:T(8,128)(2,1)}, bf16[3,4,2,2,16,512]{5,4,3,2,1,0:T(8,128)(2,1)}) custom-call(bf16[8,2,8,16,256]{4,3,2,1,0:T(8,128)(2,1)} %all-to-all-done.1.refs_0_, bf16[8,2,8,48,256]{4,3,2,1,0:T(8,128)(2,1)} %all-to-all-done.3.refs_1_, bf16[1024,256]{1,0:T(8,128)(2,1)} %refs_2_.10, ...), custom_call_target="tpu_custom_call" | custom-call | tf_op jit(solution)/shard_map/pallas_call | solution.py:86
  136.3 0.9 copy-done.8
  137.3 2.6 %fusion.17 = (bf16[12,16,512]{2,1,0:T(8,128)(2,1)S(1)}, bf16[12,16,512]{2,1,0:T(8,128)(2,1)S(1)}, bf16[12,16,512]{2,1,0:T(8,128)(2,1)S(1)}, f32[12,16,512]{2,1,0:T(8,128)S(1)}) fusion(f32[4,12,16,512]{3,2,1,0:T(8,128)} %convert_add_fusion.3.refs_6_, bf16[4,12,16,512]{3,2,1,0:T(8,128)(2,1)} %collective-permute-done.13, ...), kind=kLoop, calls=%fused_computation.46 | loop fusion | flops 2654208 | bytes 4915200 | tf_op jit(solution)/shard_map/add | solution.py:292
  141.4 1.6 collective-permute-start.14
  142.9 2.9 %collective-permute-start.15 = (bf16[4,4,16,512]{3,2,1,0:T(8,128)(2,1)S(1)}, bf16[4,4,16,512]{3,2,1,0:T(8,128)(2,1)S(1)}, u32[]{:S(2)}, u32[]{:S(2)}) collective-permute-start(bf16[4,4,16,512]{3,2,1,0:T(8,128)(2,1)S(1)} %get-tuple-element.46), channel_id=1, source_target_pairs={{0,32},{8,40},{16,48},{24,56},{32,0},{40,8},{48,16},{56,24},{64,96... | collective-permute-start | bytes 786440 | tf_op jit(solution)/shard_map/ppermute | solution.py:348
  145.8 1.3 collective-permute-start.16
  147.2 4.3 %collective-permute-start.17 = (bf16[4,16,512]{2,1,0:T(8,128)(2,1)}, bf16[4,16,512]{2,1,0:T(8,128)(2,1)}, u32[]{:S(2)}, u32[]{:S(2)}) collective-permute-start(bf16[4,16,512]{2,1,0:T(8,128)(2,1)} %get-tuple-element.52), channel_id=1, source_target_pairs={{0,128},{8,136},{16,144},{24,152},{32,160},{40,168},{48,176},{56,1... | collective-permute-start | bytes 196616 | tf_op jit(solution)/shard_map/ppermute | solution.py:302
  151.5 1.5 collective-permute-start.18
  153.0 4.7 %collective-permute-start.19 = (bf16[12,16,512]{2,1,0:T(8,128)(2,1)S(1)}, bf16[12,16,512]{2,1,0:T(8,128)(2,1)}, u32[]{:S(2)}, u32[]{:S(2)}) collective-permute-start(bf16[12,16,512]{2,1,0:T(8,128)(2,1)S(1)} %get-tuple-element.55), channel_id=1, source_target_pairs={{0,128},{8,136},{16,144},{24,152},{32,160},{40,168},{48,176},{56,1... | collective-permute-start | bytes 589832 | tf_op jit(solution)/shard_map/ppermute | solution.py:302
  157.7 4.3 %collective-permute-start.20 = (bf16[12,16,512]{2,1,0:T(8,128)(2,1)S(1)}, bf16[12,16,512]{2,1,0:T(8,128)(2,1)}, u32[]{:S(2)}, u32[]{:S(2)}) collective-permute-start(bf16[12,16,512]{2,1,0:T(8,128)(2,1)S(1)} %get-tuple-element.56), channel_id=1, source_target_pairs={{0,192},{8,200},{16,208},{24,216},{32,224},{40,232},{48,240},{56,2... | collective-permute-start | bytes 589832 | tf_op jit(solution)/shard_map/ppermute | solution.py:302
  162.0 0.9 fusion.7.refs_3_
  162.9 4.1 %all-to-all-start.4 = ((bf16[4,4,16,512]{3,2,1,0:T(8,128)(2,1)}), bf16[4,4,16,512]{3,2,1,0:T(8,128)(2,1)}, u32[]{:S(2)}, u32[]{:S(2)}) async-start(bf16[4,4,16,512]{3,2,1,0:T(8,128)(2,1)} %fusion.7.refs_3_), calls=%async_computation.4 | async-start | bytes 524288 | tf_op jit(solution)/shard_map/all_to_all | solution.py:320
  167.0 3.5 %shard_map.108 = (bf16[1024,256]{1,0:T(8,128)(2,1)}, f32[4,16,512]{2,1,0:T(8,128)}, f32[12,16,512]{2,1,0:T(8,128)}) custom-call(bf16[8,2,8,16,256]{4,3,2,1,0:T(8,128)(2,1)} %all-to-all-done.1.refs_0_, bf16[8,2,8,48,256]{4,3,2,1,0:T(8,128)(2,1)} %all-to-all-done.3.refs_1_, ...), custom_call_target="tpu_custom_call", output_to_operand_aliasing={{1}: (4, {}), {2}: (5, {})} | custom-call | tf_op jit(solution)/shard_map/pallas_call | solution.py:86
  170.5 1.0 add_multiply_fusion.1
  171.5 8.5 %collective-permute-done.20 = bf16[12,16,512]{2,1,0:T(8,128)(2,1)} collective-permute-done((bf16[12,16,512]{2,1,0:T(8,128)(2,1)S(1)}, bf16[12,16,512]{2,1,0:T(8,128)(2,1)}, u32[]{:S(2)}, u32[]{:S(2)}) %collective-permute-start.20) | collective-permute-done | bytes 196640 | tf_op jit(solution)/shard_map/ppermute | solution.py:302
  180.1 1.3 add_multiply_fusion
  181.4 0.8 pad_maximum_fusion
  182.3 1.0 convert_reduce_fusion
  183.3 0.7 reshape_squeeze.4
  (58 shorter events, 5.4 us)
Async XLA Ops:
  4.3 19.9 %all-to-all-start = ((bf16[8,2,2,64,256]{4,3,2,1,0:T(8,128)(2,1)}), bf16[8,2,2,64,256]{4,3,2,1,0:T(8,128)(2,1)}, u32[]{:S(2)}, u32[]{:S(2)}) async-start(bf16[8,2,2,64,256]{4,3,2,1,0:T(8,128)(2,1)} %shard_map.101.refs_4_), calls=%async_computation | async-start | bytes 2097152 | tf_op jit(solution)/shard_map/all_to_all | solution.py:306
  24.2 41.5 %all-to-all-start.2 = ((bf16[8,2,6,64,256]{4,3,2,1,0:T(8,128)(2,1)}), bf16[8,2,6,64,256]{4,3,2,1,0:T(8,128)(2,1)}, u32[]{:S(2)}, u32[]{:S(2)}) async-start(bf16[8,2,6,64,256]{4,3,2,1,0:T(8,128)(2,1)} %shard_map.104), calls=%async_computation.2 | async-start | bytes 6291456 | tf_op jit(solution)/shard_map/all_to_all | solution.py:306
  36.4 2.5 %collective-permute-start.1 = (bf16[3,4,4,16,512]{4,3,2,1,0:T(8,128)(2,1)}, bf16[3,4,4,16,512]{4,3,2,1,0:T(8,128)(2,1)S(1)}, u32[]{:S(2)}, u32[]{:S(2)}) collective-permute-start(bf16[3,4,4,16,512]{4,3,2,1,0:T(8,128)(2,1)} %bitcast.117), channel_id=1, source_target_pairs={{0,8},{8,0},{16,24},{24,16},{32,40},{40,32},{48,56},{56,48},{64,72... | collective-permute-start | bytes 2359304 | tf_op jit(solution)/shard_map/ppermute | solution.py:269
  36.4 8.1 %collective-permute-start = (bf16[1,4,4,16,512]{4,3,2,1,0:T(8,128)(2,1)}, bf16[1,4,4,16,512]{4,3,2,1,0:T(8,128)(2,1)S(1)}, u32[]{:S(2)}, u32[]{:S(2)}) collective-permute-start(bf16[1,4,4,16,512]{4,3,2,1,0:T(8,128)(2,1)} %bitcast.119), channel_id=1, source_target_pairs={{0,8},{8,0},{16,24},{24,16},{32,40},{40,32},{48,56},{56,48},{64,72... | collective-permute-start | bytes 786440 | tf_op jit(solution)/shard_map/ppermute | solution.py:269
  39.2 9.7 %collective-permute-start.2 = (bf16[4,4,16,512]{3,2,1,0:T(8,128)(2,1)S(1)}, bf16[4,4,16,512]{3,2,1,0:T(8,128)(2,1)S(1)}, u32[]{:S(2)}, u32[]{:S(2)}) collective-permute-start(bf16[4,4,16,512]{3,2,1,0:T(8,128)(2,1)S(1)} %get-tuple-element.83), channel_id=1, source_target_pairs={{0,16},{8,24},{16,32},{24,40},{32,48},{40,56},{48,0},{56,8},{64,80... | collective-permute-start | bytes 786440 | tf_op jit(solution)/shard_map/ppermute | solution.py:296
  40.9 13.0 %collective-permute-start.4 = (bf16[4,4,16,512]{3,2,1,0:T(8,128)(2,1)S(1)}, bf16[4,4,16,512]{3,2,1,0:T(8,128)(2,1)S(1)}, u32[]{:S(2)}, u32[]{:S(2)}) collective-permute-start(bf16[4,4,16,512]{3,2,1,0:T(8,128)(2,1)S(1)} %get-tuple-element.84), channel_id=1, source_target_pairs={{0,48},{8,56},{16,0},{24,8},{32,16},{40,24},{48,32},{56,40},{64,11... | collective-permute-start | bytes 786440 | tf_op jit(solution)/shard_map/ppermute | solution.py:296
  42.5 13.2 %collective-permute-start.3 = (bf16[4,4,16,512]{3,2,1,0:T(8,128)(2,1)S(1)}, bf16[4,4,16,512]{3,2,1,0:T(8,128)(2,1)S(1)}, u32[]{:S(2)}, u32[]{:S(2)}) collective-permute-start(bf16[4,4,16,512]{3,2,1,0:T(8,128)(2,1)S(1)} %get-tuple-element.85), channel_id=1, source_target_pairs={{0,32},{8,40},{16,48},{24,56},{32,0},{40,8},{48,16},{56,24},{64,96... | collective-permute-start | bytes 786440 | tf_op jit(solution)/shard_map/ppermute | solution.py:296
  56.5 9.2 %copy-start.1 = (f32[4,16,512]{2,1,0:T(8,128)}, f32[4,16,512]{2,1,0:T(8,128)S(1)}, u32[]{:S(2)}) copy-start(f32[4,16,512]{2,1,0:T(8,128)S(1)} %get-tuple-element.71.refs_0_.refs_3_) | copy-start | bytes 393220
  56.5 9.2 %copy-start.2 = (bf16[4,16,512]{2,1,0:T(8,128)(2,1)}, bf16[4,16,512]{2,1,0:T(8,128)(2,1)S(1)}, u32[]{:S(2)}) copy-start(bf16[4,16,512]{2,1,0:T(8,128)(2,1)S(1)} %get-tuple-element.68.refs_3_.refs_6_) | copy-start | bytes 196612
  56.5 9.2 %copy-start.4 = (bf16[4,16,512]{2,1,0:T(8,128)(2,1)}, bf16[4,16,512]{2,1,0:T(8,128)(2,1)S(1)}, u32[]{:S(2)}) copy-start(bf16[4,16,512]{2,1,0:T(8,128)(2,1)S(1)} %get-tuple-element.70.refs_1_.refs_4_) | copy-start | bytes 196612
  65.7 18.4 %all-to-all-start.1 = ((bf16[8,2,8,16,256]{4,3,2,1,0:T(8,128)(2,1)}), bf16[8,2,8,16,256]{4,3,2,1,0:T(8,128)(2,1)}, u32[]{:S(2)}, u32[]{:S(2)}) async-start(bf16[8,2,8,16,256]{4,3,2,1,0:T(8,128)(2,1)} %get-tuple-element.35), calls=%async_computation.1 | async-start | bytes 2097152 | tf_op jit(solution)/shard_map/all_to_all | solution.py:306
  84.1 7.2 %copy-start.6 = (bf16[4,4,2,6,16,512]{5,4,3,2,1,0:T(8,128)(2,1)S(1)}, bf16[4,4,2,6,16,512]{5,4,3,2,1,0:T(8,128)(2,1)}, u32[]{:S(2)}) copy-start(bf16[4,4,2,6,16,512]{5,4,3,2,1,0:T(8,128)(2,1)} %get-tuple-element.39) | copy-start | bytes 9437188
  84.1 47.1 %all-to-all-start.3 = ((bf16[8,2,8,48,256]{4,3,2,1,0:T(8,128)(2,1)}), bf16[8,2,8,48,256]{4,3,2,1,0:T(8,128)(2,1)}, u32[]{:S(2)}, u32[]{:S(2)}) async-start(bf16[8,2,8,48,256]{4,3,2,1,0:T(8,128)(2,1)} %get-tuple-element.36), calls=%async_computation.3 | async-start | bytes 6291456 | tf_op jit(solution)/shard_map/all_to_all | solution.py:306
  90.8 4.7 %collective-permute-start.10 = (bf16[3,4,12,16,512]{4,3,2,1,0:T(8,128)(2,1)}, bf16[3,4,12,16,512]{4,3,2,1,0:T(8,128)(2,1)S(1)}, u32[]{:S(2)}, u32[]{:S(2)}) collective-permute-start(bf16[3,4,12,16,512]{4,3,2,1,0:T(8,128)(2,1)} %bitcast.114), channel_id=1, source_target_pairs={{0,8},{8,0},{16,24},{24,16},{32,40},{40,32},{48,56},{56,48},{64,72... | collective-permute-start | bytes 7077896 | tf_op jit(solution)/shard_map/ppermute | solution.py:269
  90.8 15.8 %collective-permute-start.7 = (bf16[1,4,12,16,512]{4,3,2,1,0:T(8,128)(2,1)}, bf16[1,4,12,16,512]{4,3,2,1,0:T(8,128)(2,1)S(1)}, u32[]{:S(2)}, u32[]{:S(2)}) collective-permute-start(bf16[1,4,12,16,512]{4,3,2,1,0:T(8,128)(2,1)} %bitcast.115), channel_id=1, source_target_pairs={{0,8},{8,0},{16,24},{24,16},{32,40},{40,32},{48,56},{56,48},{64,72... | collective-permute-start | bytes 2359304 | tf_op jit(solution)/shard_map/ppermute | solution.py:269
  95.6 7.7 %copy-start.5 = (bf16[4,16,512]{2,1,0:T(8,128)(2,1)S(1)}, bf16[4,16,512]{2,1,0:T(8,128)(2,1)}, u32[]{:S(2)}) copy-start(bf16[4,16,512]{2,1,0:T(8,128)(2,1)} %get-tuple-element.37) | copy-start | bytes 196612
  95.6 11.0 %copy-start.3 = (bf16[4,16,512]{2,1,0:T(8,128)(2,1)S(1)}, bf16[4,16,512]{2,1,0:T(8,128)(2,1)}, u32[]{:S(2)}) copy-start(bf16[4,16,512]{2,1,0:T(8,128)(2,1)} %get-tuple-element.38) | copy-start | bytes 196612
  97.8 38.4 %collective-permute-start.11 = (bf16[4,12,16,512]{3,2,1,0:T(8,128)(2,1)}, bf16[4,12,16,512]{3,2,1,0:T(8,128)(2,1)S(1)}, u32[]{:S(2)}, u32[]{:S(2)}) collective-permute-start(bf16[4,12,16,512]{3,2,1,0:T(8,128)(2,1)} %get-tuple-element.65), channel_id=1, source_target_pairs={{0,16},{8,24},{16,32},{24,40},{32,48},{40,56},{48,0},{56,8},{64,80... | collective-permute-start | bytes 2359304 | tf_op jit(solution)/shard_map/ppermute | solution.py:296
  99.7 36.6 %collective-permute-start.13 = (bf16[4,12,16,512]{3,2,1,0:T(8,128)(2,1)}, bf16[4,12,16,512]{3,2,1,0:T(8,128)(2,1)}, u32[]{:S(2)}, u32[]{:S(2)}) collective-permute-start(bf16[4,12,16,512]{3,2,1,0:T(8,128)(2,1)} %get-tuple-element.66), channel_id=1, source_target_pairs={{0,48},{8,56},{16,0},{24,8},{32,16},{40,24},{48,32},{56,40},{64,11... | collective-permute-start | bytes 2359304 | tf_op jit(solution)/shard_map/ppermute | solution.py:296
  101.1 36.2 %collective-permute-start.12 = (bf16[4,12,16,512]{3,2,1,0:T(8,128)(2,1)}, bf16[4,12,16,512]{3,2,1,0:T(8,128)(2,1)}, u32[]{:S(2)}, u32[]{:S(2)}) collective-permute-start(bf16[4,12,16,512]{3,2,1,0:T(8,128)(2,1)} %get-tuple-element.67), channel_id=1, source_target_pairs={{0,32},{8,40},{16,48},{24,56},{32,0},{40,8},{48,16},{56,24},{64,96... | collective-permute-start | bytes 2359304 | tf_op jit(solution)/shard_map/ppermute | solution.py:296
  103.3 27.9 %collective-permute-start.5 = (bf16[4,16,512]{2,1,0:T(8,128)(2,1)S(1)}, bf16[4,16,512]{2,1,0:T(8,128)(2,1)S(1)}, u32[]{:S(2)}, u32[]{:S(2)}) collective-permute-start(bf16[4,16,512]{2,1,0:T(8,128)(2,1)S(1)} %copy-done.5), channel_id=1, source_target_pairs={{0,64},{8,72},{16,80},{24,88},{32,96},{40,104},{48,112},{56,120},{... | collective-permute-start | bytes 196616 | tf_op jit(solution)/shard_map/ppermute | solution.py:302
  106.6 24.6 %collective-permute-start.6 = (bf16[4,16,512]{2,1,0:T(8,128)(2,1)S(1)}, bf16[4,16,512]{2,1,0:T(8,128)(2,1)S(1)}, u32[]{:S(2)}, u32[]{:S(2)}) collective-permute-start(bf16[4,16,512]{2,1,0:T(8,128)(2,1)S(1)} %copy-done.3), channel_id=1, source_target_pairs={{0,192},{8,200},{16,208},{24,216},{32,224},{40,232},{48,240},{56,2... | collective-permute-start | bytes 196616 | tf_op jit(solution)/shard_map/ppermute | solution.py:302
  131.2 0.6 copy-start.9
  131.2 0.6 copy-start.10
  136.1 3.8 %copy-start.11 = (bf16[1,4,2,2,16,512]{5,4,3,2,1,0:T(8,128)(2,1)S(1)}, bf16[1,4,2,2,16,512]{5,4,3,2,1,0:T(8,128)(2,1)}, u32[]{:S(2)}) copy-start(bf16[1,4,2,2,16,512]{5,4,3,2,1,0:T(8,128)(2,1)} %get-tuple-element.42) | copy-start | bytes 786436
  136.1 4.2 %copy-start.7 = (bf16[4,4,2,2,16,512]{5,4,3,2,1,0:T(8,128)(2,1)S(1)}, bf16[4,4,2,2,16,512]{5,4,3,2,1,0:T(8,128)(2,1)}, u32[]{:S(2)}) copy-start(bf16[4,4,2,2,16,512]{5,4,3,2,1,0:T(8,128)(2,1)} %get-tuple-element.41) | copy-start | bytes 3145732
  136.1 4.3 %collective-permute-start.9 = (bf16[3,4,4,16,512]{4,3,2,1,0:T(8,128)(2,1)}, bf16[3,4,4,16,512]{4,3,2,1,0:T(8,128)(2,1)S(1)}, u32[]{:S(2)}, u32[]{:S(2)}) collective-permute-start(bf16[3,4,4,16,512]{4,3,2,1,0:T(8,128)(2,1)} %bitcast.116), channel_id=1, source_target_pairs={{0,8},{8,0},{16,24},{24,16},{32,40},{40,32},{48,56},{56,48},{64,72... | collective-permute-start | bytes 2359304 | tf_op jit(solution)/shard_map/ppermute | solution.py:269
  136.3 0.9 copy-start.8
  139.9 11.6 %collective-permute-start.8 = (bf16[1,4,4,16,512]{4,3,2,1,0:T(8,128)(2,1)S(1)}, bf16[1,4,4,16,512]{4,3,2,1,0:T(8,128)(2,1)S(1)}, u32[]{:S(2)}, u32[]{:S(2)}) collective-permute-start(bf16[1,4,4,16,512]{4,3,2,1,0:T(8,128)(2,1)S(1)} %bitcast.118), channel_id=1, source_target_pairs={{0,8},{8,0},{16,24},{24,16},{32,40},{40,32},{48,56},{56,48},{64,72... | collective-permute-start | bytes 786440 | tf_op jit(solution)/shard_map/ppermute | solution.py:269
  141.4 25.6 %copy-start = (f32[12,16,512]{2,1,0:T(8,128)}, f32[12,16,512]{2,1,0:T(8,128)S(1)}, u32[]{:S(2)}) copy-start(f32[12,16,512]{2,1,0:T(8,128)S(1)} %get-tuple-element.49.refs_5_) | copy-start | bytes 1179652
  141.4 11.6 %collective-permute-start.14 = (bf16[4,4,16,512]{3,2,1,0:T(8,128)(2,1)S(1)}, bf16[4,4,16,512]{3,2,1,0:T(8,128)(2,1)S(1)}, u32[]{:S(2)}, u32[]{:S(2)}) collective-permute-start(bf16[4,4,16,512]{3,2,1,0:T(8,128)(2,1)S(1)} %get-tuple-element.45), channel_id=1, source_target_pairs={{0,16},{8,24},{16,32},{24,40},{32,48},{40,56},{48,0},{56,8},{64,80... | collective-permute-start | bytes 786440 | tf_op jit(solution)/shard_map/ppermute | solution.py:348
  142.9 14.7 %collective-permute-start.15 = (bf16[4,4,16,512]{3,2,1,0:T(8,128)(2,1)S(1)}, bf16[4,4,16,512]{3,2,1,0:T(8,128)(2,1)S(1)}, u32[]{:S(2)}, u32[]{:S(2)}) collective-permute-start(bf16[4,4,16,512]{3,2,1,0:T(8,128)(2,1)S(1)} %get-tuple-element.46), channel_id=1, source_target_pairs={{0,32},{8,40},{16,48},{24,56},{32,0},{40,8},{48,16},{56,24},{64,96... | collective-permute-start | bytes 786440 | tf_op jit(solution)/shard_map/ppermute | solution.py:348
  145.8 16.2 %collective-permute-start.16 = (bf16[4,4,16,512]{3,2,1,0:T(8,128)(2,1)S(1)}, bf16[4,4,16,512]{3,2,1,0:T(8,128)(2,1)S(1)}, u32[]{:S(2)}, u32[]{:S(2)}) collective-permute-start(bf16[4,4,16,512]{3,2,1,0:T(8,128)(2,1)S(1)} %get-tuple-element.47), channel_id=1, source_target_pairs={{0,48},{8,56},{16,0},{24,8},{32,16},{40,24},{48,32},{56,40},{64,11... | collective-permute-start | bytes 786440 | tf_op jit(solution)/shard_map/ppermute | solution.py:348
  147.2 23.3 %collective-permute-start.17 = (bf16[4,16,512]{2,1,0:T(8,128)(2,1)}, bf16[4,16,512]{2,1,0:T(8,128)(2,1)}, u32[]{:S(2)}, u32[]{:S(2)}) collective-permute-start(bf16[4,16,512]{2,1,0:T(8,128)(2,1)} %get-tuple-element.52), channel_id=1, source_target_pairs={{0,128},{8,136},{16,144},{24,152},{32,160},{40,168},{48,176},{56,1... | collective-permute-start | bytes 196616 | tf_op jit(solution)/shard_map/ppermute | solution.py:302
  151.5 20.0 %collective-permute-start.18 = (bf16[12,16,512]{2,1,0:T(8,128)(2,1)S(1)}, bf16[12,16,512]{2,1,0:T(8,128)(2,1)}, u32[]{:S(2)}, u32[]{:S(2)}) collective-permute-start(bf16[12,16,512]{2,1,0:T(8,128)(2,1)S(1)} %get-tuple-element.54), channel_id=1, source_target_pairs={{0,64},{8,72},{16,80},{24,88},{32,96},{40,104},{48,112},{56,120},{... | collective-permute-start | bytes 589832 | tf_op jit(solution)/shard_map/ppermute | solution.py:302
  153.0 18.5 %collective-permute-start.19 = (bf16[12,16,512]{2,1,0:T(8,128)(2,1)S(1)}, bf16[12,16,512]{2,1,0:T(8,128)(2,1)}, u32[]{:S(2)}, u32[]{:S(2)}) collective-permute-start(bf16[12,16,512]{2,1,0:T(8,128)(2,1)S(1)} %get-tuple-element.55), channel_id=1, source_target_pairs={{0,128},{8,136},{16,144},{24,152},{32,160},{40,168},{48,176},{56,1... | collective-permute-start | bytes 589832 | tf_op jit(solution)/shard_map/ppermute | solution.py:302
  157.7 22.4 %collective-permute-start.20 = (bf16[12,16,512]{2,1,0:T(8,128)(2,1)S(1)}, bf16[12,16,512]{2,1,0:T(8,128)(2,1)}, u32[]{:S(2)}, u32[]{:S(2)}) collective-permute-start(bf16[12,16,512]{2,1,0:T(8,128)(2,1)S(1)} %get-tuple-element.56), channel_id=1, source_target_pairs={{0,192},{8,200},{16,208},{24,216},{32,224},{40,232},{48,240},{56,2... | collective-permute-start | bytes 589832 | tf_op jit(solution)/shard_map/ppermute | solution.py:302
  162.9 19.4 %all-to-all-start.4 = ((bf16[4,4,16,512]{3,2,1,0:T(8,128)(2,1)}), bf16[4,4,16,512]{3,2,1,0:T(8,128)(2,1)}, u32[]{:S(2)}, u32[]{:S(2)}) async-start(bf16[4,4,16,512]{3,2,1,0:T(8,128)(2,1)} %fusion.7.refs_3_), calls=%async_computation.4 | async-start | bytes 524288 | tf_op jit(solution)/shard_map/all_to_all | solution.py:320

commit v5 on v4

--- a/solution.py
+++ b/solution.py
@@ -338,9 +338,9 @@
     )
     sums2 = core_step(own, near, far)
     back1, back2 = exchange(back1), exchange(back2)
-    got1 = end_moves(*sums1)
+    got1 = [lax.ppermute(sums1[r], "dp", dp_perm(r, 0, 0)) for r in (1, 3)]
     own, near, far = outer_stage(
-        back1, back2, inputs, grad_out, after=[*got1[::2], sums2[0]]
+        back1, back2, inputs, grad_out, after=[*got1, sums2[0]]
     )
     keep, *sends = core_step(own, near, far)
     gated = gate([*sends, *line_step(*sums2)])
@@ -348,9 +348,10 @@
     outer = add(keep, [lax.ppermute(s, "dp", dp_perm(0, r + 1, 0)) for r, s in enumerate(sends)])
     got2 = end_moves(*sums2)
     outer = outer.astype(half)
-    grad_in, keep1, keep2 = back_stage(
-        back1, back2, up_left, after=(outer,), carry=(sums1[0], sums2[0])
-    )
+    grad_in, keep1, keep2, late = back_stage(
+        back1, back2, up_left, after=(outer,), carry=(sums1[0], sums2[0], sums1[2])
+    )
+    got1.append(lax.ppermute(late, "dp", dp_perm(2, 0, 0)))
     outer = share(outer, False) * factor
     outer = outer.reshape(2, -1, ROWS, BLK_HID)
     grads = [

time: 186 us -> 186 us (level)
  starting transfers between devices: 67.9 us -> 71.7 us
  waiting for transfers between devices: 64.5 us -> 60.8 us
    ppermute x6 -> x3, waiting for transfers between devices: 29.4 us -> 0.01 us  [end_moves(): lax.ppermute(s, 'dp', dp_perm(r + 1, 0, 0))]
    ppermute x0 -> x3, waiting for transfers between devices: none -> 24.3 us  [the longest x2 20.9 us: shards(): got1 = [lax.ppermute(sums1[r], 'dp', dp_perm(r, 0, 0)) for r in (1, 3)]]
    ppermute x0 -> x3, starting transfers between devices: none -> 11.5 us  [the longest x1 6.01 us: shards(): got1.append(lax.ppermute(late, 'dp', dp_perm(2, 0, 0)))]
    ppermute x6 -> x3, starting transfers between devices: 20.3 us -> 9.56 us  [end_moves(): lax.ppermute(s, 'dp', dp_perm(r + 1, 0, 0))]
    all_to_all x1, starting transfers between devices: 4.05 us -> 7.1 us  [share(): lax.all_to_all(array, 'dp', split_axis=0, concat_axis=0, tiled=True, axis...]
  transfers between devices with their start and end apart: 26 -> 26, of which waited for: 11 -> 12; matrix products, arithmetic and copies ran while one was open for 7% -> 7% of each run, Pallas kernels for 16% -> 17%
where the time goes in v5:
time: 186 us; the launch traced here: 183 us
  starting transfers between devices  71.7 us (39%)
  waiting for transfers between devices  60.8 us (33%)
  Pallas kernels  33.9 us (18%)
  other arithmetic  12 us (6%)
  local copies, waits for them, and re-layouts  3.91 us (2%)
    pallas_call x8, Pallas kernels, call(): return lambda *operands: run(*operands, *after, *carry)  33.9 us
    all_to_all x4, starting transfers between devices, exchange(): lax.all_to_all(array, 'block', split_axis=0, concat_axis=0, tiled=True)  25.4 us
    ppermute x2, waiting for transfers between devices, shards(): got1 = [lax.ppermute(sums1[r], 'dp', dp_perm(r, 0, 0)) for r in (1, 3)]  20.9 us
    all_to_all x4, waiting for transfers between devices, exchange(): lax.all_to_all(array, 'block', split_axis=0, concat_axis=0, tiled=True)  19.7 us
    ppermute x6, waiting for transfers between devices, line_step(): lax.ppermute(s, 'dp', dp_perm(0, r + 1, 0))  11.3 us
    ppermute x6, starting transfers between devices, line_step(): lax.ppermute(s, 'dp', dp_perm(0, r + 1, 0))  10.8 us
    ppermute x3, starting transfers between devices, end_moves(): lax.ppermute(s, 'dp', dp_perm(r + 1, 0, 0))  9.56 us
    all_to_all x1, starting transfers between devices, share(): lax.all_to_all(array, 'dp', split_axis=0, concat_axis=0, tiled=True, axis...  7.1 us
  transfers between devices with their start and end apart: 26, of which 12 were waited for; matrix products, arithmetic and copies ran while one was open for 7% of the time, Pallas kernels for 17%

profile of v5, /device:TPU:2, one launch (start us, length us, event | category | flops | bytes accessed | tf_op | source)
XLA Modules:
  0.0 183.2 jit_solution(1781847137608029131)
XLA Ops:
  0.6 3.7 %shard_map.101.refs_4_ = bf16[8,2,2,64,256]{4,3,2,1,0:T(8,128)(2,1)} custom-call(bf16[1024,256]{1,0:T(8,128)(2,1)} %refs_2_.10, bf16[1024,256]{1,0:T(8,128)(2,1)} %refs_3_.5, bf16[8,128,512]{2,1,0:T(8,128)(2,1)} %refs_2_.11, bf16[8,512,128]{2,1,0:T(8,128)(2,1)} %refs_3_.4), custom_call_target="tpu_custom_call" | custom-call | tf_op jit(solution)/shard_map/pallas_call | solution.py:86
  4.3 6.4 %all-to-all-start = ((bf16[8,2,2,64,256]{4,3,2,1,0:T(8,128)(2,1)}), bf16[8,2,2,64,256]{4,3,2,1,0:T(8,128)(2,1)}, u32[]{:S(2)}, u32[]{:S(2)}) async-start(bf16[8,2,2,64,256]{4,3,2,1,0:T(8,128)(2,1)} %shard_map.101.refs_4_), calls=%async_computation | async-start | bytes 2097152 | tf_op jit(solution)/shard_map/all_to_all | solution.py:306
  10.7 4.0 %shard_map.104 = bf16[8,2,6,64,256]{4,3,2,1,0:T(8,128)(2,1)} custom-call(bf16[1024,256]{1,0:T(8,128)(2,1)} %refs_2_.10, bf16[1024,256]{1,0:T(8,128)(2,1)} %refs_3_.5, bf16[8,128,512]{2,1,0:T(8,128)(2,1)} %refs_2_.11, bf16[8,512,128]{2,1,0:T(8,128)(2,1)} %refs_3_.4, bf16[8,2,2,64,256]{4,3,2,1,0:T(8,128)(2,1)} %shard_map.101.refs_4_), custom_call_target="tpu_custom_call" | custom-call | tf_op jit(solution)/shard_map/pallas_call | solution.py:86
  14.7 9.5 %all-to-all-done.refs_0_ = bf16[8,2,2,64,256]{4,3,2,1,0:T(8,128)(2,1)} async-done(((bf16[8,2,2,64,256]{4,3,2,1,0:T(8,128)(2,1)}), bf16[8,2,2,64,256]{4,3,2,1,0:T(8,128)(2,1)}, u32[]{:S(2)}, u32[]{:S(2)}) %all-to-all-start) | async-done | bytes 1048608 | tf_op jit(solution)/shard_map/all_to_all | solution.py:306
  24.2 6.4 %all-to-all-start.2 = ((bf16[8,2,6,64,256]{4,3,2,1,0:T(8,128)(2,1)}), bf16[8,2,6,64,256]{4,3,2,1,0:T(8,128)(2,1)}, u32[]{:S(2)}, u32[]{:S(2)}) async-start(bf16[8,2,6,64,256]{4,3,2,1,0:T(8,128)(2,1)} %shard_map.104), calls=%async_computation.2 | async-start | bytes 6291456 | tf_op jit(solution)/shard_map/all_to_all | solution.py:306
  30.6 5.8 %shard_map.102 = (bf16[8,2,8,16,256]{4,3,2,1,0:T(8,128)(2,1)}, bf16[4,4,2,2,16,512]{5,4,3,2,1,0:T(8,128)(2,1)}, bf16[1,4,2,2,16,512]{5,4,3,2,1,0:T(8,128)(2,1)}, bf16[3,4,2,2,16,512]{5,4,3,2,1,0:T(8,128)(2,1)}) custom-call(bf16[8,2,2,64,256]{4,3,2,1,0:T(8,128)(2,1)} %all-to-all-done.refs_0_, bf16[8,512,512]{2,1,0:T(8,128)(2,1)} %refs_1_.7, ...), custom_call_target="tpu_custom_call" | custom-call | tf_op jit(solution)/shard_map/pallas_call | solution.py:86
  36.9 1.3 fusion.27
  38.2 0.7 collective-permute-done.1
  39.2 1.7 collective-permute-start.2
  40.9 1.7 collective-permute-start.4
  42.5 2.0 %collective-permute-start.3 = (bf16[4,4,16,512]{3,2,1,0:T(8,128)(2,1)S(1)}, bf16[4,4,16,512]{3,2,1,0:T(8,128)(2,1)S(1)}, u32[]{:S(2)}, u32[]{:S(2)}) collective-permute-start(bf16[4,4,16,512]{3,2,1,0:T(8,128)(2,1)S(1)} %get-tuple-element.87), channel_id=1, source_target_pairs={{0,32},{8,40},{16,48},{24,56},{32,0},{40,8},{48,16},{56,24},{64,96... | collective-permute-start | bytes 786440 | tf_op jit(solution)/shard_map/ppermute | solution.py:296
  44.6 4.3 %collective-permute-done.2 = bf16[4,4,16,512]{3,2,1,0:T(8,128)(2,1)S(1)} collective-permute-done((bf16[4,4,16,512]{3,2,1,0:T(8,128)(2,1)S(1)}, bf16[4,4,16,512]{3,2,1,0:T(8,128)(2,1)S(1)}, u32[]{:S(2)}, u32[]{:S(2)}) %collective-permute-start.2) | collective-permute-done | bytes 262176 | tf_op jit(solution)/shard_map/ppermute | solution.py:296
  48.9 5.0 %collective-permute-done.4 = bf16[4,4,16,512]{3,2,1,0:T(8,128)(2,1)S(1)} collective-permute-done((bf16[4,4,16,512]{3,2,1,0:T(8,128)(2,1)S(1)}, bf16[4,4,16,512]{3,2,1,0:T(8,128)(2,1)S(1)}, u32[]{:S(2)}, u32[]{:S(2)}) %collective-permute-start.4) | collective-permute-done | bytes 262176 | tf_op jit(solution)/shard_map/ppermute | solution.py:296
  53.9 1.8 collective-permute-done.3
  55.9 0.7 shard_map.103
  56.6 9.2 %all-to-all-done.2.refs_0_ = bf16[8,2,6,64,256]{4,3,2,1,0:T(8,128)(2,1)} async-done(((bf16[8,2,6,64,256]{4,3,2,1,0:T(8,128)(2,1)}), bf16[8,2,6,64,256]{4,3,2,1,0:T(8,128)(2,1)}, u32[]{:S(2)}, u32[]{:S(2)}) %all-to-all-start.2) | async-done | bytes 3145760 | tf_op jit(solution)/shard_map/all_to_all | solution.py:306
  65.7 5.9 %all-to-all-start.1 = ((bf16[8,2,8,16,256]{4,3,2,1,0:T(8,128)(2,1)}), bf16[8,2,8,16,256]{4,3,2,1,0:T(8,128)(2,1)}, u32[]{:S(2)}, u32[]{:S(2)}) async-start(bf16[8,2,8,16,256]{4,3,2,1,0:T(8,128)(2,1)} %get-tuple-element.36), calls=%async_computation.1 | async-start | bytes 2097152 | tf_op jit(solution)/shard_map/all_to_all | solution.py:306
  71.7 11.5 %shard_map.105 = (bf16[8,2,8,48,256]{4,3,2,1,0:T(8,128)(2,1)}, bf16[4,4,2,6,16,512]{5,4,3,2,1,0:T(8,128)(2,1)}, bf16[1,4,2,6,16,512]{5,4,3,2,1,0:T(8,128)(2,1)},...) custom-call(bf16[8,2,6,64,256]{4,3,2,1,0:T(8,128)(2,1)} %all-to-all-, ...), custom_call_target="tpu_custom_call", output_to_operand_aliasing={{4}: (3, {}), {5}: (4, {}), {6}: (5, {}), {7}: (6, {})} | custom-call | tf_op jit(solution)/shard_map/pallas_call | solution.py:86
  83.1 1.0 all-to-all-done.1.refs_0_
  84.2 6.7 %all-to-all-start.3 = ((bf16[8,2,8,48,256]{4,3,2,1,0:T(8,128)(2,1)}), bf16[8,2,8,48,256]{4,3,2,1,0:T(8,128)(2,1)}, u32[]{:S(2)}, u32[]{:S(2)}) async-start(bf16[8,2,8,48,256]{4,3,2,1,0:T(8,128)(2,1)} %get-tuple-element.37), calls=%async_computation.3 | async-start | bytes 6291456 | tf_op jit(solution)/shard_map/all_to_all | solution.py:306
  91.7 3.9 %collective-permute-done.10 = bf16[3,4,12,16,512]{4,3,2,1,0:T(8,128)(2,1)S(1)} collective-permute-done((bf16[3,4,12,16,512]{4,3,2,1,0:T(8,128)(2,1)}, bf16[3,4,12,16,512]{4,3,2,1,0:T(8,128)(2,1)S(1)}, u32[]{:S(2)}, u32[]{:S(2)}) %collective-permute-start.10) | collective-permute-done | bytes 2359328 | tf_op jit(solution)/shard_map/ppermute | solution.py:269
  95.6 2.2 %fusion.2 = (bf16[4,12,16,512]{3,2,1,0:T(8,128)(2,1)}, bf16[4,12,16,512]{3,2,1,0:T(8,128)(2,1)}, bf16[4,12,16,512]{3,2,1,0:T(8,128)(2,1)}) fusion(bf16[4,12,16,512]{3,2,1,0:T(8,128)(2,1)S(1)} %bitcast.101, bf16[3,4,12,16,512]{4,3,2,1,0:T(8,128)(2,1)S(1)} %collective-permute-done.10, bf16[4,12,16,512]{3,2,1,0:T(8,128)(2,1)S(1)} %bitcast.102, ...), kind=kLoop, calls=%fused_computation.5 | loop fusion | flops 4718592 | bytes 7077888 | tf_op jit(solution)/shard_map/convert_element_type | solution.py:272
  97.8 1.8 %collective-permute-start.11 = (bf16[4,12,16,512]{3,2,1,0:T(8,128)(2,1)}, bf16[4,12,16,512]{3,2,1,0:T(8,128)(2,1)S(1)}, u32[]{:S(2)}, u32[]{:S(2)}) collective-permute-start(bf16[4,12,16,512]{3,2,1,0:T(8,128)(2,1)} %get-tuple-element.67), channel_id=1, source_target_pairs={{0,16},{8,24},{16,32},{24,40},{32,48},{40,56},{48,0},{56,8},{64,80... | collective-permute-start | bytes 2359304 | tf_op jit(solution)/shard_map/ppermute | solution.py:296
  99.7 1.4 collective-permute-start.13
  101.1 2.2 %collective-permute-start.12 = (bf16[4,12,16,512]{3,2,1,0:T(8,128)(2,1)}, bf16[4,12,16,512]{3,2,1,0:T(8,128)(2,1)}, u32[]{:S(2)}, u32[]{:S(2)}) collective-permute-start(bf16[4,12,16,512]{3,2,1,0:T(8,128)(2,1)} %get-tuple-element.69), channel_id=1, source_target_pairs={{0,32},{8,40},{16,48},{24,56},{32,0},{40,8},{48,16},{56,24},{64,96... | collective-permute-start | bytes 2359304 | tf_op jit(solution)/shard_map/ppermute | solution.py:296
  103.3 3.3 %collective-permute-start.5 = (bf16[4,16,512]{2,1,0:T(8,128)(2,1)S(1)}, bf16[4,16,512]{2,1,0:T(8,128)(2,1)S(1)}, u32[]{:S(2)}, u32[]{:S(2)}) collective-permute-start(bf16[4,16,512]{2,1,0:T(8,128)(2,1)S(1)} %copy-done.7), channel_id=1, source_target_pairs={{0,64},{8,72},{16,80},{24,88},{32,96},{40,104},{48,112},{56,120},{... | collective-permute-start | bytes 196616 | tf_op jit(solution)/shard_map/ppermute | solution.py:341
  106.6 2.2 %collective-permute-start.6 = (bf16[4,16,512]{2,1,0:T(8,128)(2,1)S(1)}, bf16[4,16,512]{2,1,0:T(8,128)(2,1)S(1)}, u32[]{:S(2)}, u32[]{:S(2)}) collective-permute-start(bf16[4,16,512]{2,1,0:T(8,128)(2,1)S(1)} %copy-done.5), channel_id=1, source_target_pairs={{0,192},{8,200},{16,208},{24,216},{32,224},{40,232},{48,240},{56,2... | collective-permute-start | bytes 196616 | tf_op jit(solution)/shard_map/ppermute | solution.py:341
  108.8 1.5 convert_add_fusion.3.refs_6_
  110.3 20.9 %collective-permute-done.5.refs_4_ = bf16[4,16,512]{2,1,0:T(8,128)(2,1)S(1)} collective-permute-done((bf16[4,16,512]{2,1,0:T(8,128)(2,1)S(1)}, bf16[4,16,512]{2,1,0:T(8,128)(2,1)S(1)}, u32[]{:S(2)}, u32[]{:S(2)}) %collective-permute-start.5) | collective-permute-done | bytes 65568 | tf_op jit(solution)/shard_map/ppermute | solution.py:341
  131.9 4.2 %shard_map.106 = (bf16[4,4,2,2,16,512]{5,4,3,2,1,0:T(8,128)(2,1)}, bf16[1,4,2,2,16,512]{5,4,3,2,1,0:T(8,128)(2,1)}, bf16[3,4,2,2,16,512]{5,4,3,2,1,0:T(8,128)(2,1)}) custom-call(bf16[8,2,8,16,256]{4,3,2,1,0:T(8,128)(2,1)} %all-to-all-done.1.refs_0_, bf16[8,2,8,48,256]{4,3,2,1,0:T(8,128)(2,1)} %all-to-all-done.3.refs_1_, bf16[1024,256]{1,0:T(8,128)(2,1)} %refs_2_.10, ...), custom_call_target="tpu_custom_call" | custom-call | tf_op jit(solution)/shard_map/pallas_call | solution.py:86
  136.3 0.9 copy-done.10
  137.3 2.6 %fusion.17 = (bf16[12,16,512]{2,1,0:T(8,128)(2,1)S(1)}, bf16[12,16,512]{2,1,0:T(8,128)(2,1)S(1)}, bf16[12,16,512]{2,1,0:T(8,128)(2,1)S(1)}, f32[12,16,512]{2,1,0:T(8,128)S(1)}) fusion(f32[4,12,16,512]{3,2,1,0:T(8,128)} %convert_add_fusion.3.refs_6_, bf16[4,12,16,512]{3,2,1,0:T(8,128)(2,1)} %collective-permute-done.13, ...), kind=kLoop, calls=%fused_computation.46 | loop fusion | flops 2654208 | bytes 4915200 | tf_op jit(solution)/shard_map/add | solution.py:292
  141.3 1.6 collective-permute-start.14
  142.9 2.9 %collective-permute-start.15 = (bf16[4,4,16,512]{3,2,1,0:T(8,128)(2,1)S(1)}, bf16[4,4,16,512]{3,2,1,0:T(8,128)(2,1)S(1)}, u32[]{:S(2)}, u32[]{:S(2)}) collective-permute-start(bf16[4,4,16,512]{3,2,1,0:T(8,128)(2,1)S(1)} %get-tuple-element.47), channel_id=1, source_target_pairs={{0,32},{8,40},{16,48},{24,56},{32,0},{40,8},{48,16},{56,24},{64,96... | collective-permute-start | bytes 786440 | tf_op jit(solution)/shard_map/ppermute | solution.py:348
  145.8 1.3 collective-permute-start.16
  147.2 1.3 collective-permute-start.18
  148.4 4.5 %collective-permute-start.19 = (bf16[12,16,512]{2,1,0:T(8,128)(2,1)S(1)}, bf16[12,16,512]{2,1,0:T(8,128)(2,1)}, u32[]{:S(2)}, u32[]{:S(2)}) collective-permute-start(bf16[12,16,512]{2,1,0:T(8,128)(2,1)S(1)} %get-tuple-element.57), channel_id=1, source_target_pairs={{0,128},{8,136},{16,144},{24,152},{32,160},{40,168},{48,176},{56,1... | collective-permute-start | bytes 589832 | tf_op jit(solution)/shard_map/ppermute | solution.py:302
  152.9 3.8 %collective-permute-start.20 = (bf16[12,16,512]{2,1,0:T(8,128)(2,1)S(1)}, bf16[12,16,512]{2,1,0:T(8,128)(2,1)}, u32[]{:S(2)}, u32[]{:S(2)}) collective-permute-start(bf16[12,16,512]{2,1,0:T(8,128)(2,1)S(1)} %get-tuple-element.58), channel_id=1, source_target_pairs={{0,192},{8,200},{16,208},{24,216},{32,224},{40,232},{48,240},{56,2... | collective-permute-start | bytes 589832 | tf_op jit(solution)/shard_map/ppermute | solution.py:302
  156.7 0.9 collective-permute-done.15
  157.6 1.0 fusion.7.refs_3_
  158.6 7.1 %all-to-all-start.4 = ((bf16[4,4,16,512]{3,2,1,0:T(8,128)(2,1)}), bf16[4,4,16,512]{3,2,1,0:T(8,128)(2,1)}, u32[]{:S(2)}, u32[]{:S(2)}) async-start(bf16[4,4,16,512]{3,2,1,0:T(8,128)(2,1)} %fusion.7.refs_3_), calls=%async_computation.4 | async-start | bytes 524288 | tf_op jit(solution)/shard_map/all_to_all | solution.py:320
  165.7 3.5 %shard_map.108 = (bf16[1024,256]{1,0:T(8,128)(2,1)}, f32[4,16,512]{2,1,0:T(8,128)}, f32[12,16,512]{2,1,0:T(8,128)}, bf16[4,16,512]{2,1,0:T(8,128)(2,1)}) custom-call(bf16[8,2,8,16,256]{4,3,2,1,0:T(8,128)(2,1)} %all-to-all-done.1.refs_0_, ...), custom_call_target="tpu_custom_call", output_to_operand_aliasing={{1}: (4, {}), {2}: (5, {}), {3}: (6, {})} | custom-call | tf_op jit(solution)/shard_map/pallas_call | solution.py:86
  169.2 6.0 %collective-permute-start.17 = (bf16[4,16,512]{2,1,0:T(8,128)(2,1)}, bf16[4,16,512]{2,1,0:T(8,128)(2,1)S(1)}, u32[]{:S(2)}, u32[]{:S(2)}) collective-permute-start(bf16[4,16,512]{2,1,0:T(8,128)(2,1)} %get-tuple-element.54), channel_id=1, source_target_pairs={{0,128},{8,136},{16,144},{24,152},{32,160},{40,168},{48,176},{56,1... | collective-permute-start | bytes 196616 | tf_op jit(solution)/shard_map/ppermute | solution.py:354
  175.2 1.3 add_multiply_fusion
  176.6 3.4 %collective-permute-done.17 = bf16[4,16,512]{2,1,0:T(8,128)(2,1)S(1)} collective-permute-done((bf16[4,16,512]{2,1,0:T(8,128)(2,1)}, bf16[4,16,512]{2,1,0:T(8,128)(2,1)S(1)}, u32[]{:S(2)}, u32[]{:S(2)}) %collective-permute-start.17) | collective-permute-done | bytes 65568 | tf_op jit(solution)/shard_map/ppermute | solution.py:354
  180.0 0.8 pad_maximum_fusion
  180.9 1.0 convert_reduce_fusion
  181.9 0.7 reshape_squeeze.4
  (66 shorter events, 5.0 us)
Async XLA Ops:
  4.3 19.9 %all-to-all-start = ((bf16[8,2,2,64,256]{4,3,2,1,0:T(8,128)(2,1)}), bf16[8,2,2,64,256]{4,3,2,1,0:T(8,128)(2,1)}, u32[]{:S(2)}, u32[]{:S(2)}) async-start(bf16[8,2,2,64,256]{4,3,2,1,0:T(8,128)(2,1)} %shard_map.101.refs_4_), calls=%async_computation | async-start | bytes 2097152 | tf_op jit(solution)/shard_map/all_to_all | solution.py:306
  24.2 41.5 %all-to-all-start.2 = ((bf16[8,2,6,64,256]{4,3,2,1,0:T(8,128)(2,1)}), bf16[8,2,6,64,256]{4,3,2,1,0:T(8,128)(2,1)}, u32[]{:S(2)}, u32[]{:S(2)}) async-start(bf16[8,2,6,64,256]{4,3,2,1,0:T(8,128)(2,1)} %shard_map.104), calls=%async_computation.2 | async-start | bytes 6291456 | tf_op jit(solution)/shard_map/all_to_all | solution.py:306
  36.4 2.5 %collective-permute-start.1 = (bf16[3,4,4,16,512]{4,3,2,1,0:T(8,128)(2,1)}, bf16[3,4,4,16,512]{4,3,2,1,0:T(8,128)(2,1)S(1)}, u32[]{:S(2)}, u32[]{:S(2)}) collective-permute-start(bf16[3,4,4,16,512]{4,3,2,1,0:T(8,128)(2,1)} %bitcast.117), channel_id=1, source_target_pairs={{0,8},{8,0},{16,24},{24,16},{32,40},{40,32},{48,56},{56,48},{64,72... | collective-permute-start | bytes 2359304 | tf_op jit(solution)/shard_map/ppermute | solution.py:269
  36.4 8.1 %collective-permute-start = (bf16[1,4,4,16,512]{4,3,2,1,0:T(8,128)(2,1)}, bf16[1,4,4,16,512]{4,3,2,1,0:T(8,128)(2,1)S(1)}, u32[]{:S(2)}, u32[]{:S(2)}) collective-permute-start(bf16[1,4,4,16,512]{4,3,2,1,0:T(8,128)(2,1)} %bitcast.119), channel_id=1, source_target_pairs={{0,8},{8,0},{16,24},{24,16},{32,40},{40,32},{48,56},{56,48},{64,72... | collective-permute-start | bytes 786440 | tf_op jit(solution)/shard_map/ppermute | solution.py:269
  39.2 9.7 %collective-permute-start.2 = (bf16[4,4,16,512]{3,2,1,0:T(8,128)(2,1)S(1)}, bf16[4,4,16,512]{3,2,1,0:T(8,128)(2,1)S(1)}, u32[]{:S(2)}, u32[]{:S(2)}) collective-permute-start(bf16[4,4,16,512]{3,2,1,0:T(8,128)(2,1)S(1)} %get-tuple-element.85), channel_id=1, source_target_pairs={{0,16},{8,24},{16,32},{24,40},{32,48},{40,56},{48,0},{56,8},{64,80... | collective-permute-start | bytes 786440 | tf_op jit(solution)/shard_map/ppermute | solution.py:296
  40.9 13.0 %collective-permute-start.4 = (bf16[4,4,16,512]{3,2,1,0:T(8,128)(2,1)S(1)}, bf16[4,4,16,512]{3,2,1,0:T(8,128)(2,1)S(1)}, u32[]{:S(2)}, u32[]{:S(2)}) collective-permute-start(bf16[4,4,16,512]{3,2,1,0:T(8,128)(2,1)S(1)} %get-tuple-element.86), channel_id=1, source_target_pairs={{0,48},{8,56},{16,0},{24,8},{32,16},{40,24},{48,32},{56,40},{64,11... | collective-permute-start | bytes 786440 | tf_op jit(solution)/shard_map/ppermute | solution.py:296
  42.5 13.2 %collective-permute-start.3 = (bf16[4,4,16,512]{3,2,1,0:T(8,128)(2,1)S(1)}, bf16[4,4,16,512]{3,2,1,0:T(8,128)(2,1)S(1)}, u32[]{:S(2)}, u32[]{:S(2)}) collective-permute-start(bf16[4,4,16,512]{3,2,1,0:T(8,128)(2,1)S(1)} %get-tuple-element.87), channel_id=1, source_target_pairs={{0,32},{8,40},{16,48},{24,56},{32,0},{40,8},{48,16},{56,24},{64,96... | collective-permute-start | bytes 786440 | tf_op jit(solution)/shard_map/ppermute | solution.py:296
  55.9 9.9 %copy-start.1 = (f32[4,16,512]{2,1,0:T(8,128)}, f32[4,16,512]{2,1,0:T(8,128)S(1)}, u32[]{:S(2)}) copy-start(f32[4,16,512]{2,1,0:T(8,128)S(1)} %get-tuple-element.73.refs_0_.refs_3_) | copy-start | bytes 393220
  55.9 9.9 %copy-start.3 = (bf16[4,16,512]{2,1,0:T(8,128)(2,1)}, bf16[4,16,512]{2,1,0:T(8,128)(2,1)S(1)}, u32[]{:S(2)}) copy-start(bf16[4,16,512]{2,1,0:T(8,128)(2,1)S(1)} %get-tuple-element.71.refs_2_.refs_5_) | copy-start | bytes 196612
  55.9 9.8 %copy-start.4 = (bf16[4,16,512]{2,1,0:T(8,128)(2,1)}, bf16[4,16,512]{2,1,0:T(8,128)(2,1)S(1)}, u32[]{:S(2)}) copy-start(bf16[4,16,512]{2,1,0:T(8,128)(2,1)S(1)} %get-tuple-element.70.refs_3_.refs_6_) | copy-start | bytes 196612
  55.9 9.8 %copy-start.6 = (bf16[4,16,512]{2,1,0:T(8,128)(2,1)}, bf16[4,16,512]{2,1,0:T(8,128)(2,1)S(1)}, u32[]{:S(2)}) copy-start(bf16[4,16,512]{2,1,0:T(8,128)(2,1)S(1)} %get-tuple-element.72.refs_1_.refs_4_) | copy-start | bytes 196612
  65.7 18.4 %all-to-all-start.1 = ((bf16[8,2,8,16,256]{4,3,2,1,0:T(8,128)(2,1)}), bf16[8,2,8,16,256]{4,3,2,1,0:T(8,128)(2,1)}, u32[]{:S(2)}, u32[]{:S(2)}) async-start(bf16[8,2,8,16,256]{4,3,2,1,0:T(8,128)(2,1)} %get-tuple-element.36), calls=%async_computation.1 | async-start | bytes 2097152 | tf_op jit(solution)/shard_map/all_to_all | solution.py:306
  84.1 7.2 %copy-start.8 = (bf16[4,4,2,6,16,512]{5,4,3,2,1,0:T(8,128)(2,1)S(1)}, bf16[4,4,2,6,16,512]{5,4,3,2,1,0:T(8,128)(2,1)}, u32[]{:S(2)}) copy-start(bf16[4,4,2,6,16,512]{5,4,3,2,1,0:T(8,128)(2,1)} %get-tuple-element.40) | copy-start | bytes 9437188
  84.2 47.1 %all-to-all-start.3 = ((bf16[8,2,8,48,256]{4,3,2,1,0:T(8,128)(2,1)}), bf16[8,2,8,48,256]{4,3,2,1,0:T(8,128)(2,1)}, u32[]{:S(2)}, u32[]{:S(2)}) async-start(bf16[8,2,8,48,256]{4,3,2,1,0:T(8,128)(2,1)} %get-tuple-element.37), calls=%async_computation.3 | async-start | bytes 6291456 | tf_op jit(solution)/shard_map/all_to_all | solution.py:306
  90.8 4.7 %collective-permute-start.10 = (bf16[3,4,12,16,512]{4,3,2,1,0:T(8,128)(2,1)}, bf16[3,4,12,16,512]{4,3,2,1,0:T(8,128)(2,1)S(1)}, u32[]{:S(2)}, u32[]{:S(2)}) collective-permute-start(bf16[3,4,12,16,512]{4,3,2,1,0:T(8,128)(2,1)} %bitcast.114), channel_id=1, source_target_pairs={{0,8},{8,0},{16,24},{24,16},{32,40},{40,32},{48,56},{56,48},{64,72... | collective-permute-start | bytes 7077896 | tf_op jit(solution)/shard_map/ppermute | solution.py:269
  90.8 15.7 %collective-permute-start.7 = (bf16[1,4,12,16,512]{4,3,2,1,0:T(8,128)(2,1)}, bf16[1,4,12,16,512]{4,3,2,1,0:T(8,128)(2,1)S(1)}, u32[]{:S(2)}, u32[]{:S(2)}) collective-permute-start(bf16[1,4,12,16,512]{4,3,2,1,0:T(8,128)(2,1)} %bitcast.115), channel_id=1, source_target_pairs={{0,8},{8,0},{16,24},{24,16},{32,40},{40,32},{48,56},{56,48},{64,72... | collective-permute-start | bytes 2359304 | tf_op jit(solution)/shard_map/ppermute | solution.py:269
  95.6 7.7 %copy-start.7 = (bf16[4,16,512]{2,1,0:T(8,128)(2,1)S(1)}, bf16[4,16,512]{2,1,0:T(8,128)(2,1)}, u32[]{:S(2)}) copy-start(bf16[4,16,512]{2,1,0:T(8,128)(2,1)} %get-tuple-element.38) | copy-start | bytes 196612
  95.6 11.0 %copy-start.5 = (bf16[4,16,512]{2,1,0:T(8,128)(2,1)S(1)}, bf16[4,16,512]{2,1,0:T(8,128)(2,1)}, u32[]{:S(2)}) copy-start(bf16[4,16,512]{2,1,0:T(8,128)(2,1)} %get-tuple-element.39) | copy-start | bytes 196612
  97.8 38.4 %collective-permute-start.11 = (bf16[4,12,16,512]{3,2,1,0:T(8,128)(2,1)}, bf16[4,12,16,512]{3,2,1,0:T(8,128)(2,1)S(1)}, u32[]{:S(2)}, u32[]{:S(2)}) collective-permute-start(bf16[4,12,16,512]{3,2,1,0:T(8,128)(2,1)} %get-tuple-element.67), channel_id=1, source_target_pairs={{0,16},{8,24},{16,32},{24,40},{32,48},{40,56},{48,0},{56,8},{64,80... | collective-permute-start | bytes 2359304 | tf_op jit(solution)/shard_map/ppermute | solution.py:296
  99.7 36.6 %collective-permute-start.13 = (bf16[4,12,16,512]{3,2,1,0:T(8,128)(2,1)}, bf16[4,12,16,512]{3,2,1,0:T(8,128)(2,1)}, u32[]{:S(2)}, u32[]{:S(2)}) collective-permute-start(bf16[4,12,16,512]{3,2,1,0:T(8,128)(2,1)} %get-tuple-element.68), channel_id=1, source_target_pairs={{0,48},{8,56},{16,0},{24,8},{32,16},{40,24},{48,32},{56,40},{64,11... | collective-permute-start | bytes 2359304 | tf_op jit(solution)/shard_map/ppermute | solution.py:296
  101.1 36.2 %collective-permute-start.12 = (bf16[4,12,16,512]{3,2,1,0:T(8,128)(2,1)}, bf16[4,12,16,512]{3,2,1,0:T(8,128)(2,1)}, u32[]{:S(2)}, u32[]{:S(2)}) collective-permute-start(bf16[4,12,16,512]{3,2,1,0:T(8,128)(2,1)} %get-tuple-element.69), channel_id=1, source_target_pairs={{0,32},{8,40},{16,48},{24,56},{32,0},{40,8},{48,16},{56,24},{64,96... | collective-permute-start | bytes 2359304 | tf_op jit(solution)/shard_map/ppermute | solution.py:296
  103.3 27.9 %collective-permute-start.5 = (bf16[4,16,512]{2,1,0:T(8,128)(2,1)S(1)}, bf16[4,16,512]{2,1,0:T(8,128)(2,1)S(1)}, u32[]{:S(2)}, u32[]{:S(2)}) collective-permute-start(bf16[4,16,512]{2,1,0:T(8,128)(2,1)S(1)} %copy-done.7), channel_id=1, source_target_pairs={{0,64},{8,72},{16,80},{24,88},{32,96},{40,104},{48,112},{56,120},{... | collective-permute-start | bytes 196616 | tf_op jit(solution)/shard_map/ppermute | solution.py:341
  106.6 24.7 %collective-permute-start.6 = (bf16[4,16,512]{2,1,0:T(8,128)(2,1)S(1)}, bf16[4,16,512]{2,1,0:T(8,128)(2,1)S(1)}, u32[]{:S(2)}, u32[]{:S(2)}) collective-permute-start(bf16[4,16,512]{2,1,0:T(8,128)(2,1)S(1)} %copy-done.5), channel_id=1, source_target_pairs={{0,192},{8,200},{16,208},{24,216},{32,224},{40,232},{48,240},{56,2... | collective-permute-start | bytes 196616 | tf_op jit(solution)/shard_map/ppermute | solution.py:341
  131.2 0.6 copy-start.11
  131.2 0.6 copy-start.13
  136.1 3.7 %copy-start.15 = (bf16[1,4,2,2,16,512]{5,4,3,2,1,0:T(8,128)(2,1)S(1)}, bf16[1,4,2,2,16,512]{5,4,3,2,1,0:T(8,128)(2,1)}, u32[]{:S(2)}) copy-start(bf16[1,4,2,2,16,512]{5,4,3,2,1,0:T(8,128)(2,1)} %get-tuple-element.43) | copy-start | bytes 786436
  136.1 4.2 %copy-start.9 = (bf16[4,4,2,2,16,512]{5,4,3,2,1,0:T(8,128)(2,1)S(1)}, bf16[4,4,2,2,16,512]{5,4,3,2,1,0:T(8,128)(2,1)}, u32[]{:S(2)}) copy-start(bf16[4,4,2,2,16,512]{5,4,3,2,1,0:T(8,128)(2,1)} %get-tuple-element.42) | copy-start | bytes 3145732
  136.1 4.3 %collective-permute-start.9 = (bf16[3,4,4,16,512]{4,3,2,1,0:T(8,128)(2,1)}, bf16[3,4,4,16,512]{4,3,2,1,0:T(8,128)(2,1)S(1)}, u32[]{:S(2)}, u32[]{:S(2)}) collective-permute-start(bf16[3,4,4,16,512]{4,3,2,1,0:T(8,128)(2,1)} %bitcast.116), channel_id=1, source_target_pairs={{0,8},{8,0},{16,24},{24,16},{32,40},{40,32},{48,56},{56,48},{64,72... | collective-permute-start | bytes 2359304 | tf_op jit(solution)/shard_map/ppermute | solution.py:269
  136.2 0.9 copy-start.10
  139.9 8.6 %collective-permute-start.8 = (bf16[1,4,4,16,512]{4,3,2,1,0:T(8,128)(2,1)S(1)}, bf16[1,4,4,16,512]{4,3,2,1,0:T(8,128)(2,1)S(1)}, u32[]{:S(2)}, u32[]{:S(2)}) collective-permute-start(bf16[1,4,4,16,512]{4,3,2,1,0:T(8,128)(2,1)S(1)} %bitcast.118), channel_id=1, source_target_pairs={{0,8},{8,0},{16,24},{24,16},{32,40},{40,32},{48,56},{56,48},{64,72... | collective-permute-start | bytes 786440 | tf_op jit(solution)/shard_map/ppermute | solution.py:269
  141.3 24.4 %copy-start = (f32[12,16,512]{2,1,0:T(8,128)}, f32[12,16,512]{2,1,0:T(8,128)S(1)}, u32[]{:S(2)}) copy-start(f32[12,16,512]{2,1,0:T(8,128)S(1)} %get-tuple-element.50.refs_5_) | copy-start | bytes 1179652
  141.3 11.6 %collective-permute-start.14 = (bf16[4,4,16,512]{3,2,1,0:T(8,128)(2,1)S(1)}, bf16[4,4,16,512]{3,2,1,0:T(8,128)(2,1)S(1)}, u32[]{:S(2)}, u32[]{:S(2)}) collective-permute-start(bf16[4,4,16,512]{3,2,1,0:T(8,128)(2,1)S(1)} %get-tuple-element.46), channel_id=1, source_target_pairs={{0,16},{8,24},{16,32},{24,40},{32,48},{40,56},{48,0},{56,8},{64,80... | collective-permute-start | bytes 786440 | tf_op jit(solution)/shard_map/ppermute | solution.py:348
  142.9 14.7 %collective-permute-start.15 = (bf16[4,4,16,512]{3,2,1,0:T(8,128)(2,1)S(1)}, bf16[4,4,16,512]{3,2,1,0:T(8,128)(2,1)S(1)}, u32[]{:S(2)}, u32[]{:S(2)}) collective-permute-start(bf16[4,4,16,512]{3,2,1,0:T(8,128)(2,1)S(1)} %get-tuple-element.47), channel_id=1, source_target_pairs={{0,32},{8,40},{16,48},{24,56},{32,0},{40,8},{48,16},{56,24},{64,96... | collective-permute-start | bytes 786440 | tf_op jit(solution)/shard_map/ppermute | solution.py:348
  145.8 11.8 %collective-permute-start.16 = (bf16[4,4,16,512]{3,2,1,0:T(8,128)(2,1)S(1)}, bf16[4,4,16,512]{3,2,1,0:T(8,128)(2,1)S(1)}, u32[]{:S(2)}, u32[]{:S(2)}) collective-permute-start(bf16[4,4,16,512]{3,2,1,0:T(8,128)(2,1)S(1)} %get-tuple-element.48), channel_id=1, source_target_pairs={{0,48},{8,56},{16,0},{24,8},{32,16},{40,24},{48,32},{56,40},{64,11... | collective-permute-start | bytes 786440 | tf_op jit(solution)/shard_map/ppermute | solution.py:348
  147.2 28.1 %collective-permute-start.18 = (bf16[12,16,512]{2,1,0:T(8,128)(2,1)S(1)}, bf16[12,16,512]{2,1,0:T(8,128)(2,1)}, u32[]{:S(2)}, u32[]{:S(2)}) collective-permute-start(bf16[12,16,512]{2,1,0:T(8,128)(2,1)S(1)} %get-tuple-element.56), channel_id=1, source_target_pairs={{0,64},{8,72},{16,80},{24,88},{32,96},{40,104},{48,112},{56,120},{... | collective-permute-start | bytes 589832 | tf_op jit(solution)/shard_map/ppermute | solution.py:302
  148.4 26.8 %collective-permute-start.19 = (bf16[12,16,512]{2,1,0:T(8,128)(2,1)S(1)}, bf16[12,16,512]{2,1,0:T(8,128)(2,1)}, u32[]{:S(2)}, u32[]{:S(2)}) collective-permute-start(bf16[12,16,512]{2,1,0:T(8,128)(2,1)S(1)} %get-tuple-element.57), channel_id=1, source_target_pairs={{0,128},{8,136},{16,144},{24,152},{32,160},{40,168},{48,176},{56,1... | collective-permute-start | bytes 589832 | tf_op jit(solution)/shard_map/ppermute | solution.py:302
  152.9 22.3 %collective-permute-start.20 = (bf16[12,16,512]{2,1,0:T(8,128)(2,1)S(1)}, bf16[12,16,512]{2,1,0:T(8,128)(2,1)}, u32[]{:S(2)}, u32[]{:S(2)}) collective-permute-start(bf16[12,16,512]{2,1,0:T(8,128)(2,1)S(1)} %get-tuple-element.58), channel_id=1, source_target_pairs={{0,192},{8,200},{16,208},{24,216},{32,224},{40,232},{48,240},{56,2... | collective-permute-start | bytes 589832 | tf_op jit(solution)/shard_map/ppermute | solution.py:302
  158.6 22.3 %all-to-all-start.4 = ((bf16[4,4,16,512]{3,2,1,0:T(8,128)(2,1)}), bf16[4,4,16,512]{3,2,1,0:T(8,128)(2,1)}, u32[]{:S(2)}, u32[]{:S(2)}) async-start(bf16[4,4,16,512]{3,2,1,0:T(8,128)(2,1)} %fusion.7.refs_3_), calls=%async_computation.4 | async-start | bytes 524288 | tf_op jit(solution)/shard_map/all_to_all | solution.py:320
  169.2 10.8 %copy-start.2 = (f32[4,16,512]{2,1,0:T(8,128)S(1)}, f32[4,16,512]{2,1,0:T(8,128)}, u32[]{:S(2)}) copy-start(f32[4,16,512]{2,1,0:T(8,128)} %get-tuple-element.53) | copy-start | bytes 393220
  169.2 10.8 %copy-start.12 = (bf16[4,16,512]{2,1,0:T(8,128)(2,1)S(1)}, bf16[4,16,512]{2,1,0:T(8,128)(2,1)}, u32[]{:S(2)}) copy-start(bf16[4,16,512]{2,1,0:T(8,128)(2,1)} %copy-done.11) | copy-start | bytes 196612
  169.2 10.8 %copy-start.14 = (bf16[4,16,512]{2,1,0:T(8,128)(2,1)S(1)}, bf16[4,16,512]{2,1,0:T(8,128)(2,1)}, u32[]{:S(2)}) copy-start(bf16[4,16,512]{2,1,0:T(8,128)(2,1)} %copy-done.13) | copy-start | bytes 196612
  169.2 10.7 %collective-permute-start.17 = (bf16[4,16,512]{2,1,0:T(8,128)(2,1)}, bf16[4,16,512]{2,1,0:T(8,128)(2,1)S(1)}, u32[]{:S(2)}, u32[]{:S(2)}) collective-permute-start(bf16[4,16,512]{2,1,0:T(8,128)(2,1)} %get-tuple-element.54), channel_id=1, source_target_pairs={{0,128},{8,136},{16,144},{24,152},{32,160},{40,168},{48,176},{56,1... | collective-permute-start | bytes 196616 | tf_op jit(solution)/shard_map/ppermute | solution.py:354
